TPU v7x, 256 devices: a whole 4x4x8 slice. The times are simulated.
256 devices in a mesh: dp: 16 (over y_lo, x, core), cls: 16 (over y_hi, z).
Axes of the slice: x: 4, y: 4 (y_hi: 2, y_lo: 2; y = y_hi * 2 + y_lo), z: 8, core: 2. Of those that a mesh axis runs over, the one named last changes fastest.
Arguments:
- embeddings: bfloat16 [1024, 256], P('dp'), may hold values from -0.75 to 0.75
- labels: int32 [1024], P('dp'), may hold values from 0 to 524287
- centres: bfloat16 [3, 524288, 256], P(None, ('dp', 'cls')), may hold values from -6 to 6
Outputs:
- loss: float32 [], replicated
- grad_embeddings: bfloat16 [1024, 256], P('dp')
- grad_centres: bfloat16 [3, 524288, 256], P(None, ('dp', 'cls'))
All inputs are finite; a program needn't handle non-finite values.
Results may differ from a plain program's by a relative error of at most 0.0067.
Values may be sent and summed in bfloat16 or wider, within the bound.
No kernel may reach another device: no remote copies, remote signals or barrier semaphores. Data moves between devices by JAX's collectives and lax.ppermute only.
A program may use at most 64 MiB of HBM per device.

v0:
```python
import jax
import jax.numpy as jnp
from jax import lax
from jax.sharding import PartitionSpec as P

norm_eps = 1e-06
logit_scale = 30.0
margin_value = 0.2
pool_temp = 0.1


def normalize(values):
    floats = values.astype(jnp.float32)
    width = floats.shape[-1]
    norm_rows = jnp.sqrt(width * (jnp.mean(floats * floats, axis=-1, keepdims=True) + norm_eps))
    return (floats / norm_rows, norm_rows)


def block_terms(unit_rows, unit_cent, local_labels, first, block):
    cent_block = lax.dynamic_slice_in_dim(unit_cent, first, block, 1)
    cosines = jnp.einsum("be,kce->kbc", unit_rows, cent_block, preferred_element_type=jnp.float32)
    weights = jnp.exp(cosines / pool_temp)
    weights = weights / jnp.sum(weights, axis=0, keepdims=True)
    pooled = jnp.sum(weights * cosines, axis=0)
    columns = first + jnp.arange(block, dtype=jnp.int32)
    onehot = (local_labels[:, None] == columns[None, :]).astype(jnp.float32)
    logits = logit_scale * (pooled - margin_value * onehot)
    return (cent_block, cosines, weights, pooled, onehot, logits)


def per_device(embeddings, labels, centres):
    unit_own, norm_own = normalize(embeddings)
    raw_rows, all_labels = (
        lax.all_gather(embeddings, "dp", axis=0, tiled=True),
        lax.all_gather(labels, "dp", axis=0, tiled=True),
    )
    unit_rows = normalize(raw_rows)[0].astype(jnp.bfloat16)
    unit_c_f, norm_c = normalize(centres)
    unit_cent = unit_c_f.astype(jnp.bfloat16)
    local_classes = centres.shape[1]
    offset = lax.axis_index(("dp", "cls")) * local_classes
    local_labels = all_labels - offset
    block = min(512, local_classes)
    count = local_classes // block
    rows = unit_rows.shape[0]

    def forward(step, carry):
        sums, target = carry
        first = (step * block).astype(jnp.int32)
        terms = block_terms(unit_rows, unit_cent, local_labels, first, block)
        logits, onehot = (terms[5], terms[4])
        return (sums + jnp.sum(jnp.exp(logits), axis=1), target + jnp.sum(logits * onehot, axis=1))

    zeros = jnp.zeros((rows,), jnp.float32)
    sum_part, target_part = lax.fori_loop(0, count, forward, (zeros, zeros))
    total_exp, target = lax.psum((sum_part, target_part), ("dp", "cls"))
    loss = jnp.mean(jnp.log(total_exp) - target)

    def backward(step, carry):
        grad_unit, grads = carry
        first = (step * block).astype(jnp.int32)
        cent_block, cosines, weights, pooled, onehot, logits = block_terms(
            unit_rows, unit_cent, local_labels, first, block
        )
        dpool = logit_scale * (jnp.exp(logits) / total_exp[:, None] - onehot)
        gcos = (dpool[None] * weights * (1.0 + (cosines - pooled[None]) / pool_temp)).astype(
            jnp.bfloat16
        )
        grad_unit = grad_unit + jnp.einsum(
            "kbc,kce->be", gcos, cent_block, preferred_element_type=jnp.float32
        )
        grad_cent = jnp.einsum("kbc,be->kce", gcos, unit_rows, preferred_element_type=jnp.float32)
        unit_part = lax.dynamic_slice_in_dim(unit_c_f, first, block, 1)
        norm_part = lax.dynamic_slice_in_dim(norm_c, first, block, 1)
        result = (
            grad_cent - unit_part * jnp.sum(unit_part * grad_cent, axis=-1, keepdims=True)
        ) / norm_part
        grads = lax.dynamic_update_slice_in_dim(grads, result.astype(jnp.bfloat16), first, 1)
        return (grad_unit, grads)

    start = (
        jnp.zeros((rows, unit_rows.shape[1]), jnp.float32),
        jnp.zeros(centres.shape, jnp.bfloat16),
    )
    grad_unit, grad_centres = lax.fori_loop(0, count, backward, start)
    share = lax.psum_scatter(grad_unit, "dp", scatter_dimension=0, tiled=True)
    own_grad = lax.psum(share, "cls")
    grad_embeddings = (
        own_grad - unit_own * jnp.sum(unit_own * own_grad, axis=-1, keepdims=True)
    ) / norm_own
    return (loss, grad_embeddings.astype(jnp.bfloat16), grad_centres)


def solution(mesh):
    return jax.shard_map(
        per_device,
        mesh=mesh,
        in_specs=(P("dp", None), P("dp"), P(None, ("dp", "cls"), None)),
        out_specs=(P(), P("dp", None), P(None, ("dp", "cls"), None)),
        check_vma=False,
    )
```

profile of v0, /device:TPU:2, one launch (start us, length us, event | category | flops | bytes accessed | tf_op | source)
XLA Modules:
  0.0 431.4 jit_solution(14681344248581908352)
XLA Ops:
  7.2 3.2 copy.18
  11.2 4.9 %convert_divide_fusion = (f32[3,2048,256]{1,2,0:T(8,128)}, bf16[3,2048,256]{1,2,0:T(8,128)(2,1)}) fusion(bf16[3,2048,256]{1,2,0:T(8,128)(2,1)S(1)} %copy.18, f32[3,2048]{1,0:T(4,128)S(1)} %get-tuple-element.402), kind=kLoop, calls=%fused_computation.56 | loop fusion | flops 4718592 | bytes 12607488 | tf_op jit(solution)/shard_map/div | solution.py:16
  16.1 4.7 %copy.19 = bf16[3,2048,256]{2,1,0:T(8,128)(2,1)} copy(bf16[3,2048,256]{1,2,0:T(8,128)(2,1)} %get-tuple-element.400) | data formatting | bytes 6291456
  20.8 19.6 %all_gather.6 = bf16[1024,256]{1,0:T(8,128)(2,1)S(1)} all-gather(bf16[64,256]{1,0:T(8,128)(2,1)S(1)} %copy-done), channel_id=1, replica_groups=mesh['dp'=16,'cls'=16] {'dp'}, dimensions={0}, use_global_device_ids=true | all-gather | bytes 557056 | tf_op jit(solution)/shard_map/all_gather | solution.py:34
  42.4 8.9 %all-reduce = s32[1024]{0:T(1024)S(1)} all-reduce(s32[1024]{0:T(1024)S(1)} %dynamic-update-slice), channel_id=1, replica_groups=mesh['dp'=16,'cls'=16] {'dp'}, use_global_device_ids=true, to_apply=%add | all-reduce | flops 1024 | bytes 8192
  51.3 1.0 copy.21
  52.3 18.6 %while.32 = (s32[]{:T(128)}, f32[1024]{0:T(1024)S(1)}, f32[1024]{0:T(1024)S(1)}, bf16[3,2048,256]{2,1,0:T(8,128)(2,1)}, bf16[1024,256]{1,0:T(8,128)(2,1)S(1)}, /...) while((s32[]{:T(128)}, f32[1024]{0:T(1024)S(1)}, f32[1024]{0:T(1024)S(1)}, ...), condition=%wide.region_7.8_spmd.clone, body=%wide.region_2.7_spmd.clone.sunk | while | flops 817367552 | bytes 22323372 | solution.py:55
  52.3 2.5 fusion.61
  54.8 1.4 fusion.62
  57.0 2.5 fusion.61
  59.5 1.4 fusion.62
  61.6 2.5 fusion.61
  64.2 1.4 fusion.62
  66.3 2.5 fusion.61
  68.8 1.4 fusion.62
  70.9 80.3 %all-reduce.1 = (f32[1024]{0:T(1024)S(1)}, f32[1024]{0:T(1024)S(1)}) all-reduce(f32[1024]{0:T(1024)S(1)} %get-tuple-element.269, f32[1024]{0:T(1024)S(1)} %get-tuple-element.268), channel_id=1, replica_groups=mesh['dp'=16,'cls'=16] {'dp','cls'}, use_global_device_ids=true, to_apply=%region_9.0 | all-reduce | flops 2048 | bytes 16384 | tf_op jit(solution)/shard_map/psum | solution.py:56
  151.3 1.9 broadcast_in_dim.45.clone
  153.1 64.1 %while.33 = (s32[]{:T(128)}, f32[1024,256]{1,0:T(8,128)}, bf16[3,2048,256]{2,1,0:T(8,128)(2,1)}, bf16[3,2048,256]{2,1,0:T(8,128)(2,1)}, bf16[1024,256]{0,1:T(8,1...) while((s32[]{:T(128)}, f32[1024,256]{1,0:T(8,128)}, ...), condition=%wide.region_15.16_spmd.clone, body=%wide.region_11.15_spmd.clone.sunk | while | flops 2443577600 | bytes 61637836 | solution.py:85
  153.1 2.6 fusion.69
  155.8 1.4 fusion.70
  157.9 2.0 fusion.72
  160.0 3.1 fusion.73
  163.1 2.0 fusion.74
  165.2 2.6 divide_convert_fusion.3
  168.1 0.9 constant_dynamic-update-slice_fusion.2
  169.0 2.6 fusion.69
  171.6 1.4 fusion.70
  173.8 2.0 fusion.72
  175.8 3.5 fusion.73
  179.3 2.1 fusion.74
  181.4 2.5 divide_convert_fusion.3
  184.2 0.9 constant_dynamic-update-slice_fusion.2
  185.1 2.6 fusion.69
  187.8 1.4 fusion.70
  189.9 2.0 fusion.72
  192.0 3.5 fusion.73
  195.5 2.1 fusion.74
  197.5 2.4 divide_convert_fusion.3
  201.2 2.6 fusion.69
  203.9 1.4 fusion.70
  206.0 2.0 fusion.72
  208.1 3.5 fusion.73
  211.5 2.1 fusion.74
  213.6 2.4 divide_convert_fusion.3
  217.5 56.1 %reduce-scatter.2.cloned.1.call-done = f32[64,256]{1,0:T(8,128)} async-done(((f32[1024,256]{1,0:T(8,128)}), f32[64,256]{1,0:T(8,128)}) %reduce-scatter.2.cloned.1.call-update) | async-done | bytes 65552 | tf_op jit(solution)/shard_map/reduce_scatter | solution.py:86
  274.9 146.0 %all-reduce.4.cloned.1.call-done = f32[64,256]{1,0:T(8,128)} async-done(((f32[64,256]{1,0:T(8,128)}), f32[64,256]{1,0:T(8,128)}) %all-reduce.4.cloned.1.call-update) | async-done | bytes 65552 | tf_op jit(solution)/shard_map/psum | solution.py:87
  420.8 1.0 multiply_reduce_fusion.1
  421.9 1.6 divide_convert_fusion.1
  (55 shorter events, 11.6 us)
Async XLA Ops:
  7.2 266.4 %reduce-scatter.2.cloned.1.call-start = ((), (), s32[]{:S(2)}) async-start(), calls=%async_computation.1 | async-start | bytes 1114112 | tf_op jit(solution)/shard_map/reduce_scatter | solution.py:86
  16.1 4.7 %copy-start = (bf16[64,256]{1,0:T(8,128)(2,1)S(1)}, bf16[64,256]{1,0:T(8,128)(2,1)}, u32[]{:S(2)}) copy-start(bf16[64,256]{1,0:T(8,128)(2,1)} %param.7) | copy-start | bytes 98308
  16.1 24.8 %copy-start.2 = (u32[256]{0:T(256)S(1)}, u32[256]{0:T(256)}, u32[]{:S(2)}) copy-start(u32[256]{0:T(256)} %constant.160) | copy-start | bytes 3076
  16.1 26.0 %copy-start.1 = (s32[64]{0:T(128)S(1)}, s32[64]{0:T(128)}, u32[]{:S(2)}) copy-start(s32[64]{0:T(128)} %param.8) | copy-start | bytes 772
  217.3 203.5 %all-reduce.4.cloned.1.call-start = ((), (), s32[]{:S(2)}) async-start(), calls=%async_computation.2 | async-start | bytes 131072 | tf_op jit(solution)/shard_map/psum | solution.py:87
Sparse Core Ops, SparseCore 0:
  217.4 56.1 reduce-scatter.1
  276.4 144.3 all-reduce.3
where the time goes:
time: 432 us; the launch traced here: 431 us
  waiting for transfers between devices  202 us (47%)
  blocking collectives  109 us (25%)
  other arithmetic  44.3 us (10%)
  matrix products  42.4 us (10%)
  local copies, waits for them, and re-layouts  16.6 us (4%)
  between operations  16.6 us (4%)
    psum x1, waiting for transfers between devices, per_device(): own_grad = lax.psum(share, 'cls')  146 us
    psum x1, blocking collectives, per_device(): total_exp, target = lax.psum((sum_part, target_part), ('dp', 'cls'))  80.3 us
    reduce_scatter x1, waiting for transfers between devices, per_device(): share = lax.psum_scatter(grad_unit, 'dp', scatter_dimension=0, tiled=True)  56.1 us
    dot_general x8, matrix products, block_terms(): jnp.einsum('be,kce->kbc', unit_rows, cent_block, preferred_element_type=j...  20.7 us
    all_gather x1, blocking collectives, per_device(): lax.all_gather(embeddings, 'dp', axis=0, tiled=True)  19.6 us
    dot_general x4, matrix products, backward(): jnp.einsum('kbc,kce->be', gcos, cent_block, preferred_element_type=jnp.fl...  13.5 us
    reduce_sum x8, other arithmetic, block_terms(): pooled = jnp.sum(weights * cosines, axis=0)  10.9 us
    mul x4, other arithmetic, backward(): unit_part * jnp.sum(unit_part * grad_cent, axis=-1, keepdims=True)  10 us
  transfers between devices with their start and end apart: 2, of which 2 were waited for; matrix products, arithmetic and copies ran while one was open for 0% of the time, Pallas kernels for 0%

commit v1 on v0

v1 whole, which is shorter than its diff:
```python
import functools
import math

import jax
import jax.numpy as jnp
import numpy as np
from jax import lax
from jax.experimental import pallas as pl
from jax.experimental.pallas import tpu as pltpu
from jax.sharding import Mesh
from jax.sharding import PartitionSpec as P

norm_eps = 1e-06
logit_scale = 30.0
margin_value = 0.2
pool_temp = 0.1

LN2 = math.log(2.0)
A = 1.0 / (pool_temp * LN2)
L = logit_scale * pool_temp
MARGIN2 = logit_scale * margin_value / LN2
INV_LN2 = 1.0 / LN2
OUT_SCALE = logit_scale * LN2

SUB = 3
E = 256
TC = 256
BB = 256
RC = 16
EXTRA = 32

f32 = jnp.float32
bf16 = jnp.bfloat16


def split3(x):
    hi = x.astype(bf16)
    rest = x - hi.astype(f32)
    mid = rest.astype(bf16)
    lo = (rest - mid.astype(f32)).astype(bf16)
    return hi, mid, lo


def inv_norm(floats):
    mean = jnp.sum(floats * floats, axis=-1, keepdims=True) * (1.0 / E)
    return lax.rsqrt(E * (mean + norm_eps))


def send_kernel(slot_ref, emb_ref, lab_ref, out_ref):
    rows = emb_ref[...].astype(f32)
    unit = rows * inv_norm(rows)
    n = rows.shape[0]
    out_ref[pl.ds(0, n), :] = unit.astype(bf16)
    labels = lab_ref[...]
    lane = lax.broadcasted_iota(jnp.int32, (1, E), 1)
    wide = jnp.concatenate([labels] * (E // n), axis=1)
    mine = (lane >= slot_ref[0]) & (lane < slot_ref[0] + n)
    wide = jnp.where(mine, wide, 0)
    row = lax.broadcasted_iota(jnp.int32, (16, E), 0)
    digit = jnp.where(row == 0, wide & 127, jnp.where(row == 1, (wide >> 7) & 127, wide >> 14))
    out_ref[pl.ds(n, 16), :] = jnp.where(row < 3, digit, 0).astype(f32).astype(bf16)


def gather_kernel(rows_own, got_ref, ut_ref, lab_ref):
    parts = got_ref.shape[0]
    per = E // rows_own
    for q in range(parts // per):
        digits = jnp.zeros((16, E), f32)
        for j in range(per):
            digits += got_ref[q * per + j, pl.ds(rows_own, 16), :].astype(f32)
        lab = digits[0:1] + 128.0 * digits[1:2] + 16384.0 * digits[2:3]
        lab_ref[:, pl.ds(q * E, E)] = lab.astype(jnp.int32)
        block = jnp.concatenate(
            [got_ref[q * per + j, pl.ds(0, rows_own), :].astype(f32) for j in range(per)], axis=0
        )
        ut_ref[:, pl.ds(q * E, E)] = block.T.astype(bf16)


def elementwise(c0, c1, c2):
    d1 = (c1 - c0) * A
    d2 = (c2 - c0) * A
    e1 = jnp.exp2(d1)
    e2 = jnp.exp2(d2)
    r = 1.0 / (1.0 + e1 + e2)
    z = (e1 * d1 + e2 * d2) * r
    power = c0 * (L * A) + z * L
    shift = INV_LN2 - z
    return e1, e2, d1, d2, r, power, shift


def forward_kernel(
    first_ref, cent_ref, ut_ref, lab_ref, pt_ref, out_ref, cb, xs, sums, target, g1, g2
):
    step = pl.program_id(0)
    steps = pl.num_programs(0)
    batch = ut_ref.shape[1]

    @pl.when(step == 0)
    def _():
        sums[...] = jnp.zeros_like(sums)
        target[...] = jnp.zeros_like(target)
        g1[...] = jnp.zeros_like(g1)
        g2[...] = jnp.zeros_like(g2)

    for k in range(SUB):
        rows = cent_ref[k].astype(f32)
        cb[pl.ds(k * TC, TC), :] = (rows * inv_norm(rows)).astype(bf16)

    first = first_ref[0] + step * TC
    labels = lab_ref[...] - first
    some = jnp.max(jnp.where((labels >= 0) & (labels < TC), 1, 0)) > 0

    def block(b):
        cols = pl.ds(b * BB, BB)
        xs[b % 2] = jnp.dot(cb[...], ut_ref[:, cols], preferred_element_type=f32)

    def terms(b, labelled):
        cols = pl.ds(b * BB, BB)
        total = jnp.zeros((8, BB), f32)
        tgt = jnp.zeros((8, BB), f32)
        for c in range(TC // RC):
            x = [xs[b % 2, pl.ds(k * TC + c * RC, RC), :] for k in range(SUB)]
            e1, e2, d1, d2, r, power, shift = elementwise(*x)
            if labelled:
                row = lax.broadcasted_iota(jnp.int32, (RC, BB), 0) + c * RC
                hit = row == labels[:, b * BB : (b + 1) * BB]
                power = jnp.where(hit, power - MARGIN2, power)
                t = jnp.where(hit, power, 0.0)
                tgt += t[0:8] + t[8:16]
            ex = jnp.exp2(power)
            total += ex[0:8] + ex[8:16]
            g = ex * r
            p = (g * shift, (g * e1) * (d1 + shift), (g * e2) * (d2 + shift))
            for k in range(SUB):
                pt_ref[k, pl.ds(c * RC, RC), cols] = p[k].astype(bf16)
        sums[:, cols] += total
        if labelled:
            target[:, cols] += tgt

    @pl.when(jnp.logical_not(some))
    def _():
        for b in range(batch // BB):
            block(b)
            terms(b, False)
        for b in range(batch // BB):
            cols = pl.ds(b * BB, BB)
            p = jnp.concatenate([pt_ref[k, :, cols] for k in range(SUB)], axis=0)
            g1[:, cols] += lax.dot_general(
                cb[...], p, (((0,), (0,)), ((), ())), preferred_element_type=f32
            )

    @pl.when(some)
    def _():
        for b in range(batch // BB):
            block(b)
            terms(b, True)
        for b in range(batch // BB):
            cols = pl.ds(b * BB, BB)
            row = lax.broadcasted_iota(jnp.int32, (TC, BB), 0)
            hit = row == labels[:, b * BB : (b + 1) * BB]
            p = [pt_ref[k, :, cols].astype(f32) for k in range(SUB)]
            own = jnp.concatenate([jnp.where(hit, v, 0.0) for v in p], axis=0).astype(bf16)
            rest = jnp.concatenate([jnp.where(hit, 0.0, v) for v in p], axis=0).astype(bf16)
            dims = (((0,), (0,)), ((), ()))
            g1[:, cols] += lax.dot_general(cb[...], rest, dims, preferred_element_type=f32)
            g2[:, cols] += lax.dot_general(cb[...], own, dims, preferred_element_type=f32)

    @pl.when(step == steps - 1)
    def _():
        parts, height = out_ref.shape[0], out_ref.shape[1]
        n = batch // parts
        per = E // n
        tot = jnp.sum(sums[...], axis=0, keepdims=True)
        tgt = jnp.sum(target[...], axis=0, keepdims=True)
        scale = jnp.exp2(-tgt)
        blocks = batch // E
        for q in range(blocks):
            cols = slice(q * E, (q + 1) * E)
            a = g1[:, cols].T.astype(bf16)
            o = (g2[:, cols] * scale[:, cols]).T.astype(bf16)
            for j in range(per):
                out_ref[q * per + j, pl.ds(0, n), :] = a[j * n : (j + 1) * n]
                out_ref[q * per + j, pl.ds(n, n), :] = o[j * n : (j + 1) * n]
        rows = [tot[:, q * E : (q + 1) * E] for q in range(blocks)]
        rows += [tgt[:, q * E : (q + 1) * E] for q in range(blocks)]
        values = jnp.concatenate(rows, axis=0)
        out_extra(out_ref, 2 * n, values)


def out_extra(out_ref, at, values):
    hi, mid, lo = split3(values)
    pad = jnp.zeros((EXTRA - 3 * values.shape[0], E), f32)
    extra = jnp.concatenate(
        [hi.astype(f32), mid.astype(f32), lo.astype(f32), pad], axis=0
    ).astype(bf16)
    if len(out_ref.shape) == 3:
        for j in range(out_ref.shape[0]):
            out_ref[j, pl.ds(at, EXTRA), :] = extra
    else:
        out_ref[pl.ds(at, EXTRA), :] = extra


def summed(got_ref):
    acc = got_ref[0].astype(f32)
    for j in range(1, got_ref.shape[0]):
        acc += got_ref[j].astype(f32)
    return acc


def middle_kernel(n, blocks, got_ref, out_ref):
    acc = summed(got_ref)
    out_ref[pl.ds(0, 2 * n), :] = acc[0 : 2 * n].astype(bf16)
    extra = acc[2 * n :]
    m = 2 * blocks
    values = extra[0:m] + extra[m : 2 * m] + extra[2 * m : 3 * m]
    out_extra(out_ref, 2 * n, values)


def backward_kernel(
    first_ref, got_ref, emb_ref, ut_ref, lab_ref, cent_ref, pt_ref,
    loss_ref, ge_ref, gc_ref, ust, fac,
):
    step = pl.program_id(0)
    batch = ut_ref.shape[1]
    n = emb_ref.shape[0]
    blocks = batch // E

    @pl.when(step == 0)
    def _():
        acc = summed(got_ref)
        extra = acc[2 * n :]
        m = 2 * blocks
        values = extra[0:m] + extra[m : 2 * m] + extra[2 * m : 3 * m]
        tot = jnp.concatenate([values[q : q + 1] for q in range(blocks)], axis=1)
        tgt = jnp.concatenate([values[blocks + q : blocks + q + 1] for q in range(blocks)], axis=1)
        terms = jnp.log(tot) - tgt * LN2
        loss_ref[...] = jnp.sum(terms, axis=1, keepdims=True) * (1.0 / batch)
        inv = OUT_SCALE / tot
        ust[...] = (ut_ref[...].astype(f32) * inv).astype(bf16)
        fac[...] = 1.0 - tot * jnp.exp2(-tgt)
        rows = emb_ref[...].astype(f32)
        r = inv_norm(rows)
        unit = rows * r
        lane = lax.broadcasted_iota(jnp.int32, (n, batch), 1)
        row = lax.broadcasted_iota(jnp.int32, (n, batch), 0)
        mine = lane == row + first_ref[1]
        inv_col = jnp.sum(jnp.where(mine, inv, 0.0), axis=1, keepdims=True)
        own_col = jnp.sum(
            jnp.where(mine, jnp.exp2(tgt) * inv - OUT_SCALE, 0.0), axis=1, keepdims=True
        )
        g = acc[0:n] * inv_col + acc[n : 2 * n] * own_col
        g = (g - unit * jnp.sum(unit * g, axis=1, keepdims=True)) * r
        ge_ref[...] = g.astype(bf16)

    first = first_ref[0] + step * TC
    labels = lab_ref[...] - first
    some = jnp.max(jnp.where((labels >= 0) & (labels < TC), 1, 0)) > 0

    def finish(k, p):
        dims = (((1,), (1,)), ((), ()))
        g = lax.dot_general(p, ust[...], dims, preferred_element_type=f32)
        rows = cent_ref[k].astype(f32)
        r = inv_norm(rows)
        unit = rows * r
        g = (g - unit * jnp.sum(unit * g, axis=1, keepdims=True)) * r
        gc_ref[k] = g.astype(bf16)

    @pl.when(jnp.logical_not(some))
    def _():
        for k in range(SUB):
            finish(k, pt_ref[k])

    @pl.when(some)
    def _():
        hit = lax.broadcasted_iota(jnp.int32, (TC, batch), 0) == labels
        factor = jnp.where(hit, fac[...], 1.0)
        for k in range(SUB):
            finish(k, (pt_ref[k].astype(f32) * factor).astype(bf16))


def per_device(embeddings, labels, centres):
    n = embeddings.shape[0]
    parts = lax.axis_size("dp")
    others = lax.axis_size("cls")
    batch = n * parts
    blocks = batch // E
    local = centres.shape[1]
    steps = local // TC
    dp = lax.axis_index("dp")
    first = (dp * others + lax.axis_index("cls")) * local
    smem = pl.BlockSpec(memory_space=pltpu.SMEM)
    vmem = pl.BlockSpec(memory_space=pltpu.VMEM)
    whole = lambda shape: pl.BlockSpec(shape, lambda i: (0,) * len(shape))
    params = pltpu.CompilerParams(vmem_limit_bytes=48 * 1024 * 1024)

    slot = ((dp % (E // n)) * n).astype(jnp.int32).reshape(1)
    sent = pl.pallas_call(
        send_kernel,
        out_shape=jax.ShapeDtypeStruct((n + 16, E), bf16),
        in_specs=[smem, vmem, vmem],
        out_specs=vmem,
    )(slot, embeddings, labels.reshape(1, n))
    got = lax.all_to_all(jnp.broadcast_to(sent[None], (parts, n + 16, E)), "dp", 0, 0)
    ut, all_labels = pl.pallas_call(
        functools.partial(gather_kernel, n),
        out_shape=(
            jax.ShapeDtypeStruct((E, batch), bf16),
            jax.ShapeDtypeStruct((1, batch), jnp.int32),
        ),
        in_specs=[vmem],
        out_specs=(vmem, vmem),
        compiler_params=params,
    )(got)

    height = 2 * n + EXTRA
    where = jnp.stack([first, dp * n]).astype(jnp.int32)
    pt, payload = pl.pallas_call(
        forward_kernel,
        grid=(steps,),
        out_shape=(
            jax.ShapeDtypeStruct((SUB, local, batch), bf16),
            jax.ShapeDtypeStruct((parts, height, E), bf16),
        ),
        in_specs=[
            smem,
            pl.BlockSpec((SUB, TC, E), lambda i: (0, i, 0)),
            whole((E, batch)),
            whole((1, batch)),
        ],
        out_specs=(
            pl.BlockSpec((SUB, TC, batch), lambda i: (0, i, 0)),
            whole((parts, height, E)),
        ),
        scratch_shapes=[
            pltpu.VMEM((SUB * TC, E), bf16),
            pltpu.VMEM((2, SUB * TC, BB), f32),
            pltpu.VMEM((8, batch), f32),
            pltpu.VMEM((8, batch), f32),
            pltpu.VMEM((E, batch), f32),
            pltpu.VMEM((E, batch), f32),
        ],
        compiler_params=params,
    )(where, centres, ut, all_labels)

    got1 = lax.all_to_all(payload, "dp", 0, 0)
    second = pl.pallas_call(
        functools.partial(middle_kernel, n, blocks),
        out_shape=jax.ShapeDtypeStruct((height, E), bf16),
        in_specs=[vmem],
        out_specs=vmem,
        compiler_params=params,
    )(got1)
    got2 = lax.all_to_all(jnp.broadcast_to(second[None], (others, height, E)), "cls", 0, 0)

    loss, grad_embeddings, grad_centres = pl.pallas_call(
        backward_kernel,
        grid=(steps,),
        out_shape=(
            jax.ShapeDtypeStruct((1, 1), f32),
            jax.ShapeDtypeStruct((n, E), bf16),
            jax.ShapeDtypeStruct((SUB, local, E), bf16),
        ),
        in_specs=[
            smem,
            whole((others, height, E)),
            whole((n, E)),
            whole((E, batch)),
            whole((1, batch)),
            pl.BlockSpec((SUB, TC, E), lambda i: (0, i, 0)),
            pl.BlockSpec((SUB, TC, batch), lambda i: (0, i, 0)),
        ],
        out_specs=(
            whole((1, 1)),
            whole((n, E)),
            pl.BlockSpec((SUB, TC, E), lambda i: (0, i, 0)),
        ),
        scratch_shapes=[pltpu.VMEM((E, batch), bf16), pltpu.VMEM((1, batch), f32)],
        compiler_params=params,
    )(where, got2, embeddings, ut, all_labels, centres, pt)
    return (loss.reshape(()), grad_embeddings, grad_centres)


def solution(mesh):
    return jax.shard_map(
        per_device,
        mesh=mesh,
        in_specs=(P("dp", None), P("dp"), P(None, ("dp", "cls"), None)),
        out_specs=(P(), P("dp", None), P(None, ("dp", "cls"), None)),
        check_vma=False,
    )
```

time: 432 us -> 126 us (0.29)
  waiting for transfers between devices: 202 us -> 9.04 us
  other arithmetic: 44.3 us -> 0.07 us
  matrix products: 42.4 us -> 0 us
  blocking collectives: 109 us -> 69.6 us
  Pallas kernels: 0 us -> 35 us
  between operations: 16.6 us -> 0.69 us
  local copies, waits for them, and re-layouts: 16.6 us -> 3.67 us
  starting transfers between devices: 0.08 us -> 5.86 us
    psum x1 -> x0, waiting for transfers between devices: 146 us -> none  [per_device(): own_grad = lax.psum(share, 'cls')]
    psum x1 -> x0, blocking collectives: 80.3 us -> none  [per_device(): total_exp, target = lax.psum((sum_part, target_part), ('dp', 'cls'))]
    all_to_all x0 -> x2, blocking collectives: none -> 69.6 us  [the longest x1 44.8 us: per_device(): lax.all_to_all(jnp.broadcast_to(second[None], (others, height, E)), 'cls'...]
    reduce_scatter x1 -> x0, waiting for transfers between devices: 56.1 us -> none  [per_device(): share = lax.psum_scatter(grad_unit, 'dp', scatter_dimension=0, tiled=True)]
    dot_general x16 -> x0, matrix products: 42.4 us -> none  [the longest x8 20.7 us: block_terms(): jnp.einsum('be,kce->kbc', unit_rows, cent_block, preferred_element_type=j...]
    pallas_call x0 -> x5, Pallas kernels: none -> 35 us  [the longest x1 20.6 us: per_device(): pl.pallas_call(forward_kernel, grid=(steps,), out_shape=(jax.ShapeDtypeSt...]
    all_gather x1 -> x0, blocking collectives: 19.6 us -> none  [per_device(): lax.all_gather(embeddings, 'dp', axis=0, tiled=True)]
    reduce_sum x17 -> x0, other arithmetic: 16.3 us -> none  [the longest x8 10.9 us: block_terms(): pooled = jnp.sum(weights * cosines, axis=0)]
  transfers between devices with their start and end apart: 2 -> 1, of which waited for: 2 -> 1; matrix products, arithmetic and copies ran while one was open for 0% -> 0% of each run, Pallas kernels for 0% -> 0%
where the time goes in v1:
time: 126 us; the launch traced here: 124 us
  blocking collectives  69.6 us (55%)
  Pallas kernels  35 us (28%)
  waiting for transfers between devices  9.04 us (7%)
  starting transfers between devices  5.86 us (5%)
  local copies, waits for them, and re-layouts  3.67 us (3%)
    all_to_all x1, blocking collectives, per_device(): lax.all_to_all(jnp.broadcast_to(second[None], (others, height, E)), 'cls'...  44.8 us
    all_to_all x1, blocking collectives, per_device(): got1 = lax.all_to_all(payload, 'dp', 0, 0)  24.8 us
    pallas_call x1, Pallas kernels, per_device(): pl.pallas_call(forward_kernel, grid=(steps,), out_shape=(jax.ShapeDtypeSt...  20.6 us
    pallas_call x1, Pallas kernels, per_device(): pl.pallas_call(backward_kernel, grid=(steps,), out_shape=(jax.ShapeDtypeS...  12.5 us
    all_to_all x1, waiting for transfers between devices, per_device(): lax.all_to_all(jnp.broadcast_to(sent[None], (parts, n + 16, E)), 'dp', 0, 0)  9.04 us
    all_to_all x1, starting transfers between devices, per_device(): lax.all_to_all(jnp.broadcast_to(sent[None], (parts, n + 16, E)), 'dp', 0, 0)  5.86 us
  transfers between devices with their start and end apart: 1, of which 1 were waited for; matrix products, arithmetic and copies ran while one was open for 0% of the time, Pallas kernels for 0%

profile of v1, /device:TPU:2, one launch (start us, length us, event | category | flops | bytes accessed | tf_op | source)
XLA Modules:
  0.0 123.9 jit_solution(10922289358905338309)
XLA Ops:
  0.6 1.5 %shard_map.58 = bf16[80,256]{1,0:T(8,128)(2,1)} custom-call(s32[1]{0:T(128)} %bitcast.2.slot_ref, bf16[64,256]{1,0:T(8,128)(2,1)} %emb_ref.3, s32[1,64]{1,0:T(1,128)} %bitcast.5), custom_call_target="tpu_custom_call" | custom-call | tf_op jit(solution)/shard_map/pallas_call | solution.py:297
  2.1 1.7 %broadcast_in_dim.4 = bf16[16,80,256]{2,1,0:T(8,128)(2,1)} broadcast(bf16[80,256]{1,0:T(8,128)(2,1)} %shard_map.58), dimensions={1,2} | broadcast | bytes 696320 | tf_op jit(solution)/shard_map/broadcast_in_dim | solution.py:303
  3.8 5.9 %all-to-all-start = ((bf16[16,80,256]{2,1,0:T(8,128)(2,1)}), bf16[16,80,256]{2,1,0:T(8,128)(2,1)S(1)}, u32[]{:S(2)}, u32[]{:S(2)}) async-start(bf16[16,80,256]{2,1,0:T(8,128)(2,1)} %broadcast_in_dim.4), calls=%async_computation | async-start | bytes 1310720 | tf_op jit(solution)/shard_map/all_to_all | solution.py:303
  9.6 0.1 pad_add_fusion.first_ref
  9.7 9.0 %all-to-all-done.got_ref = bf16[16,80,256]{2,1,0:T(8,128)(2,1)S(1)} async-done(((bf16[16,80,256]{2,1,0:T(8,128)(2,1)}), bf16[16,80,256]{2,1,0:T(8,128)(2,1)S(1)}, u32[]{:S(2)}, u32[]{:S(2)}) %all-to-all-start) | async-done | bytes 655392 | tf_op jit(solution)/shard_map/all_to_all | solution.py:303
  18.7 0.2 shard_map.59
  19.0 0.0 copy-start
  19.0 1.9 %copy-done = bf16[3,2048,256]{2,1,0:T(8,128)(2,1)S(1)} copy-done((bf16[3,2048,256]{2,1,0:T(8,128)(2,1)S(1)}, bf16[3,2048,256]{2,1,0:T(8,128)(2,1)}, u32[]{:S(2)}) %copy-start) | copy-done | bytes 3145752
  20.8 20.6 %shard_map.60 = (bf16[3,2048,1024]{2,1,0:T(8,128)(2,1)}, bf16[16,160,256]{2,1,0:T(8,128)(2,1)S(1)}) custom-call(s32[2]{0:T(128)S(1)} %pad_add_fusion.first_ref, bf16[3,2048,256]{2,1,0:T(8,128)(2,1)S(1)} %copy-done, bf16[256,1024]{1,0:T(8,128)(2,1)S(1)} %get-tuple-element.10.ut_ref, s32[1,1024]{1,0:T(1,128)S(1)} %get-tuple-element.11.lab_ref), custom_call_target="tpu_custom_call" | custom-call | tf_op jit(solution)/shard_map/pallas_call | solution.py:317
  41.5 24.8 %all_to_all.15.got_ref = bf16[16,160,256]{2,1,0:T(8,128)(2,1)S(1)} all-to-all(bf16[16,160,256]{2,1,0:T(8,128)(2,1)S(1)} %get-tuple-element.12), channel_id=1, replica_groups=mesh['dp'=16,'cls'=16] {'dp'}, dimensions={0} | all-to-all | bytes 2621440 | tf_op jit(solution)/shard_map/all_to_all | solution.py:345
  66.3 0.2 shard_map.61
  66.5 0.0 copy-start.1
  66.5 0.1 broadcast_in_dim.5
  66.6 0.0 copy-start.2
  66.6 44.8 %all_to_all.16.got_ref = bf16[16,160,256]{2,1,0:T(8,128)(2,1)S(1)} all-to-all(bf16[16,160,256]{2,1,0:T(8,128)(2,1)S(1)} %broadcast_in_dim.5), channel_id=1, replica_groups=mesh['dp'=16,'cls'=16] {'cls'}, dimensions={0} | all-to-all | bytes 2621440 | tf_op jit(solution)/shard_map/all_to_all | solution.py:353
  111.4 0.0 copy-done.1
  111.4 0.0 copy-done.2
  111.4 12.5 %shard_map.62 = (f32[1,1]{1,0:T(1,128)}, bf16[64,256]{1,0:T(8,128)(2,1)}, bf16[3,2048,256]{2,1,0:T(8,128)(2,1)}) custom-call(s32[2]{0:T(128)S(1)} %pad_add_fusion.first_ref, bf16[16,160,256]{2,1,0:T(8,128)(2,1)S(1)} %all_to_all.16.got_ref, bf16[64,256]{1,0:T(8,128)(2,1)S(1)} %copy-done.2, bf16[256,1024]{1,0:T(8,128)(2,1)S(1)} %get-tuple-element.10.ut_ref, ...), custom_call_target="tpu_custom_call" | custom-call | tf_op jit(solution)/shard_map/pallas_call | solution.py:355
Async XLA Ops:
  3.8 15.0 %all-to-all-start = ((bf16[16,80,256]{2,1,0:T(8,128)(2,1)}), bf16[16,80,256]{2,1,0:T(8,128)(2,1)S(1)}, u32[]{:S(2)}, u32[]{:S(2)}) async-start(bf16[16,80,256]{2,1,0:T(8,128)(2,1)} %broadcast_in_dim.4), calls=%async_computation | async-start | bytes 1310720 | tf_op jit(solution)/shard_map/all_to_all | solution.py:303
  19.0 1.9 %copy-start = (bf16[3,2048,256]{2,1,0:T(8,128)(2,1)S(1)}, bf16[3,2048,256]{2,1,0:T(8,128)(2,1)}, u32[]{:S(2)}) copy-start(bf16[3,2048,256]{2,1,0:T(8,128)(2,1)} %cent_ref.3) | copy-start | bytes 9437188
  66.5 44.9 %copy-start.1 = (bf16[3,2048,256]{2,1,0:T(8,128)(2,1)S(1)}, bf16[3,2048,256]{2,1,0:T(8,128)(2,1)}, u32[]{:S(2)}) copy-start(bf16[3,2048,256]{2,1,0:T(8,128)(2,1)} %cent_ref.3) | copy-start | bytes 9437188
  66.6 44.8 %copy-start.2 = (bf16[64,256]{1,0:T(8,128)(2,1)S(1)}, bf16[64,256]{1,0:T(8,128)(2,1)}, u32[]{:S(2)}) copy-start(bf16[64,256]{1,0:T(8,128)(2,1)} %emb_ref.3) | copy-start | bytes 98308

commit v2 on v1

v2 whole, which is shorter than its diff:
```python
import functools
import math

import jax
import jax.numpy as jnp
from jax import lax
from jax.experimental import pallas as pl
from jax.experimental.pallas import tpu as pltpu
from jax.sharding import PartitionSpec as P

norm_eps = 1e-06
logit_scale = 30.0
margin_value = 0.2
pool_temp = 0.1

LN2 = math.log(2.0)
A = 1.0 / (pool_temp * LN2)
L = logit_scale * pool_temp
MARGIN2 = logit_scale * margin_value / LN2
INV_LN2 = 1.0 / LN2
OUT_SCALE = logit_scale * LN2

SUB = 3
E = 256
TC = 256
BB = 256
RC = 16
EXTRA = 16

f32 = jnp.float32
bf16 = jnp.bfloat16


def split3(x):
    hi = x.astype(bf16)
    rest = x - hi.astype(f32)
    mid = rest.astype(bf16)
    lo = (rest - mid.astype(f32)).astype(bf16)
    return hi, mid, lo


def inv_norm(floats):
    mean = jnp.sum(floats * floats, axis=-1, keepdims=True) * (1.0 / E)
    return lax.rsqrt(E * (mean + norm_eps))


def send_kernel(slot_ref, emb_ref, lab_ref, out_ref):
    rows = emb_ref[...].astype(f32)
    unit = (rows * inv_norm(rows)).astype(bf16)
    n = rows.shape[0]
    labels = lab_ref[...]
    lane = lax.broadcasted_iota(jnp.int32, (1, E), 1)
    wide = jnp.concatenate([labels] * (E // n), axis=1)
    mine = (lane >= slot_ref[0]) & (lane < slot_ref[0] + n)
    wide = jnp.where(mine, wide, 0)
    row = lax.broadcasted_iota(jnp.int32, (16, E), 0)
    digit = jnp.where(row == 0, wide & 127, jnp.where(row == 1, (wide >> 7) & 127, wide >> 14))
    digit = jnp.where(row < 3, digit, 0).astype(f32).astype(bf16)
    for j in range(out_ref.shape[0]):
        out_ref[j, pl.ds(0, n), :] = unit
        out_ref[j, pl.ds(n, 16), :] = digit


def centre_kernel(cent_ref, cb_ref, cbt_ref):
    for k in range(SUB):
        rows = cent_ref[k].astype(f32)
        unit = rows * inv_norm(rows)
        cb_ref[0, pl.ds(k * TC, TC), :] = unit.astype(bf16)
        cbt_ref[0, :, pl.ds(k * TC, TC)] = unit.T.astype(bf16)


def gather_kernel(rows_own, got_ref, ut_ref, lab_ref):
    parts = got_ref.shape[0]
    per = E // rows_own
    for q in range(parts // per):
        digits = jnp.zeros((16, E), f32)
        for j in range(per):
            digits += got_ref[q * per + j, pl.ds(rows_own, 16), :].astype(f32)
        lab = digits[0:1] + 128.0 * digits[1:2] + 16384.0 * digits[2:3]
        lab_ref[:, pl.ds(q * E, E)] = lab.astype(jnp.int32)
        block = jnp.concatenate(
            [got_ref[q * per + j, pl.ds(0, rows_own), :].astype(f32) for j in range(per)], axis=0
        )
        ut_ref[:, pl.ds(q * E, E)] = block.T.astype(bf16)


def elementwise(c0, c1, c2):
    d1 = (c1 - c0) * A
    d2 = (c2 - c0) * A
    e1 = jnp.exp2(d1)
    e2 = jnp.exp2(d2)
    r = 1.0 / (1.0 + e1 + e2)
    z = (e1 * d1 + e2 * d2) * r
    power = c0 * (L * A) + z * L
    shift = INV_LN2 - z
    return e1, e2, d1, d2, r, power, shift


def forward_kernel(
    first_ref, cb_ref, cbt_ref, ut_ref, lab_ref, pt_ref, out_ref, target, xs, sums, g1, g2
):
    step = pl.program_id(0)
    steps = pl.num_programs(0)
    batch = ut_ref.shape[1]

    @pl.when(step == 0)
    def _():
        sums[...] = jnp.zeros_like(sums)
        target[...] = jnp.zeros_like(target)
        g1[...] = jnp.zeros_like(g1)
        g2[...] = jnp.zeros_like(g2)

    first = first_ref[0] + step * TC
    labels = lab_ref[...] - first
    some = jnp.max(jnp.where((labels >= 0) & (labels < TC), 1, 0)) > 0

    def block(b):
        cols = pl.ds(b * BB, BB)
        xs[b % 2] = jnp.dot(cb_ref[0], ut_ref[:, cols], preferred_element_type=f32)

    def terms(b, labelled):
        cols = pl.ds(b * BB, BB)
        total = jnp.zeros((8, BB), f32)
        tgt = jnp.zeros((8, BB), f32)
        for c in range(TC // RC):
            x = [xs[b % 2, pl.ds(k * TC + c * RC, RC), :] for k in range(SUB)]
            e1, e2, d1, d2, r, power, shift = elementwise(*x)
            if labelled:
                row = lax.broadcasted_iota(jnp.int32, (RC, BB), 0) + c * RC
                hit = row == labels[:, b * BB : (b + 1) * BB]
                power = jnp.where(hit, power - MARGIN2, power)
                t = jnp.where(hit, power, 0.0)
                tgt += t[0:8] + t[8:16]
            ex = jnp.exp2(power)
            total += ex[0:8] + ex[8:16]
            g = ex * r
            p = (g * shift, (g * e1) * (d1 + shift), (g * e2) * (d2 + shift))
            for k in range(SUB):
                pt_ref[k, pl.ds(c * RC, RC), cols] = p[k].astype(bf16)
        sums[:, cols] += total
        if labelled:
            target[:, cols] += tgt

    @pl.when(jnp.logical_not(some))
    def _():
        block(0)
        for b in range(batch // BB):
            cols = pl.ds(b * BB, BB)
            if (b + 1) * BB < batch:
                block(b + 1)
            terms(b, False)
            p = jnp.concatenate([pt_ref[k, :, cols] for k in range(SUB)], axis=0)
            g1[:, cols] += jnp.dot(cbt_ref[0], p, preferred_element_type=f32)

    @pl.when(some)
    def _():
        block(0)
        for b in range(batch // BB):
            cols = pl.ds(b * BB, BB)
            if (b + 1) * BB < batch:
                block(b + 1)
            terms(b, True)
            row = lax.broadcasted_iota(jnp.int32, (TC, BB), 0)
            hit = row == labels[:, b * BB : (b + 1) * BB]
            p = [pt_ref[k, :, cols].astype(f32) for k in range(SUB)]
            own = jnp.concatenate([jnp.where(hit, v, 0.0) for v in p], axis=0).astype(bf16)
            rest = jnp.concatenate([jnp.where(hit, 0.0, v) for v in p], axis=0).astype(bf16)
            g1[:, cols] += jnp.dot(cbt_ref[0], rest, preferred_element_type=f32)
            g2[:, cols] += jnp.dot(cbt_ref[0], own, preferred_element_type=f32)

    @pl.when(step == steps - 1)
    def _():
        parts = out_ref.shape[0]
        n = batch // parts
        per = E // n
        blocks = batch // E
        tot = jnp.sum(sums[...], axis=0, keepdims=True)
        tgt = jnp.sum(target[...], axis=0, keepdims=True)
        scale = jnp.exp2(-tgt)
        all_targets = jnp.sum(tgt, axis=1, keepdims=True)
        totals = jnp.concatenate([tot[:, q * E : (q + 1) * E] for q in range(blocks)], axis=0)
        for q in range(blocks):
            cols = slice(q * E, (q + 1) * E)
            a = g1[:, cols].T.astype(bf16)
            o = (g2[:, cols] * scale[:, cols]).T.astype(bf16)
            extra = pack_extra(totals, tgt[:, cols], all_targets).astype(bf16)
            for j in range(per):
                out_ref[q * per + j, pl.ds(0, n), :] = a[j * n : (j + 1) * n]
                out_ref[q * per + j, pl.ds(n, n), :] = o[j * n : (j + 1) * n]
                out_ref[q * per + j, pl.ds(2 * n, EXTRA), :] = extra


def pack_extra(totals, target, all_targets):
    lane = lax.broadcasted_iota(jnp.int32, (1, E), 1)
    hi, mid, lo = split3(all_targets)
    tail = jnp.where(lane == 0, hi.astype(f32), jnp.where(lane == 1, mid.astype(f32), 0.0))
    tail = jnp.where(lane == 2, lo.astype(f32), tail)
    values = [v.astype(f32) for v in split3(totals)] + [v.astype(f32) for v in split3(target)]
    pad = EXTRA - 3 * totals.shape[0] - 4
    return jnp.concatenate(values + [tail] + [jnp.zeros((pad, E), f32)] * (pad > 0), axis=0)


def unpack_extra(extra, blocks):
    totals = extra[0:blocks] + extra[blocks : 2 * blocks] + extra[2 * blocks : 3 * blocks]
    m = 3 * blocks
    target = extra[m : m + 1] + extra[m + 1 : m + 2] + extra[m + 2 : m + 3]
    all_targets = jnp.sum(extra[m + 3 : m + 4], axis=1, keepdims=True)
    return totals, target, all_targets


def summed(got_ref):
    acc = got_ref[0].astype(f32)
    for j in range(1, got_ref.shape[0]):
        acc += got_ref[j].astype(f32)
    return acc


def middle_kernel(n, blocks, got_ref, out_ref):
    acc = summed(got_ref)
    extra = pack_extra(*unpack_extra(acc[2 * n :], blocks))
    others, height = out_ref.shape[0], out_ref.shape[1]
    m = n // others
    pad = jnp.zeros((height - 2 * m - EXTRA, E), f32)
    for j in range(others):
        one = acc[j * m : (j + 1) * m]
        two = acc[n + j * m : n + (j + 1) * m]
        out_ref[j] = jnp.concatenate([one, two, extra, pad], axis=0).astype(bf16)


def rows_kernel(
    m, where_ref, got_ref, emb_ref, ut_ref, own_ref, loss_ref, ust_ref, fac_ref, rows_ref
):
    batch = ut_ref.shape[1]
    blocks = batch // E
    n = emb_ref.shape[0]
    acc = summed(got_ref)
    totals, target, all_targets = unpack_extra(acc[2 * m : 2 * m + EXTRA], blocks)
    tot = jnp.concatenate([totals[q : q + 1] for q in range(blocks)], axis=1)
    logs = jnp.sum(jnp.log(tot), axis=1, keepdims=True) - all_targets * LN2
    loss_ref[...] = logs * (1.0 / batch)
    inv = OUT_SCALE / tot
    ust_ref[...] = (ut_ref[...].astype(f32) * inv).astype(bf16)
    own = jnp.sum(own_ref[...], axis=0, keepdims=True)
    fac_ref[...] = 1.0 - tot * jnp.exp2(-own)
    lane = lax.broadcasted_iota(jnp.int32, (m, batch), 1)
    row = lax.broadcasted_iota(jnp.int32, (m, batch), 0)
    inv_col = jnp.sum(jnp.where(lane == row + where_ref[1], inv, 0.0), axis=1, keepdims=True)
    lane = lax.broadcasted_iota(jnp.int32, (m, E), 1)
    row = lax.broadcasted_iota(jnp.int32, (m, E), 0)
    mine = lane == row + where_ref[2]
    t = jnp.sum(jnp.where(mine, target, 0.0), axis=1, keepdims=True)
    g = acc[0:m] * inv_col + acc[m : 2 * m] * (jnp.exp2(t) * inv_col - OUT_SCALE)
    lane = lax.broadcasted_iota(jnp.int32, (m, n), 1)
    row = lax.broadcasted_iota(jnp.int32, (m, n), 0)
    pick = jnp.where(lane == row + where_ref[3], 1.0, 0.0).astype(bf16)
    rows = jnp.dot(pick, emb_ref[...], preferred_element_type=f32)
    r = inv_norm(rows)
    unit = rows * r
    g = (g - unit * jnp.sum(unit * g, axis=1, keepdims=True)) * r
    g = jnp.concatenate([g, jnp.zeros((16 - m, E), f32)], axis=0).astype(bf16)
    for j in range(rows_ref.shape[0]):
        rows_ref[j] = g


def collect_kernel(m, got_ref, out_ref):
    parts = [got_ref[j].astype(f32)[0:m] for j in range(got_ref.shape[0])]
    out_ref[...] = jnp.concatenate(parts, axis=0).astype(bf16)


def backward_kernel(first_ref, fac_ref, ust_ref, lab_ref, cent_ref, pt_ref, gc_ref):
    step = pl.program_id(0)
    batch = ust_ref.shape[1]
    first = first_ref[0] + step * TC
    labels = lab_ref[...] - first
    some = jnp.max(jnp.where((labels >= 0) & (labels < TC), 1, 0)) > 0

    def finish(k, p):
        dims = (((1,), (1,)), ((), ()))
        g = lax.dot_general(p, ust_ref[...], dims, preferred_element_type=f32)
        rows = cent_ref[k].astype(f32)
        r = inv_norm(rows)
        unit = rows * r
        g = (g - unit * jnp.sum(unit * g, axis=1, keepdims=True)) * r
        gc_ref[k] = g.astype(bf16)

    @pl.when(jnp.logical_not(some))
    def _():
        for k in range(SUB):
            finish(k, pt_ref[k])

    @pl.when(some)
    def _():
        hit = lax.broadcasted_iota(jnp.int32, (TC, batch), 0) == labels
        factor = jnp.where(hit, fac_ref[...], 1.0)
        for k in range(SUB):
            finish(k, (pt_ref[k].astype(f32) * factor).astype(bf16))


def per_device(embeddings, labels, centres):
    n = embeddings.shape[0]
    parts = lax.axis_size("dp")
    others = lax.axis_size("cls")
    batch = n * parts
    blocks = batch // E
    local = centres.shape[1]
    steps = local // TC
    m = n // others
    dp = lax.axis_index("dp")
    cls = lax.axis_index("cls")
    first = (dp * others + cls) * local
    slot = (dp & (E // n - 1)) * n
    where = jnp.stack([first, dp * n + cls * m, slot + cls * m, cls * m]).astype(jnp.int32)
    smem = pl.BlockSpec(memory_space=pltpu.SMEM)
    vmem = pl.BlockSpec(memory_space=pltpu.VMEM)
    whole = lambda shape: pl.BlockSpec(shape, lambda i: (0,) * len(shape))
    params = pltpu.CompilerParams(vmem_limit_bytes=24 * 1024 * 1024)
    shape = jax.ShapeDtypeStruct

    sent = pl.pallas_call(
        send_kernel,
        out_shape=shape((parts, n + 16, E), bf16),
        in_specs=[smem, vmem, vmem],
        out_specs=vmem,
    )(slot.astype(jnp.int32).reshape(1), embeddings, labels.reshape(1, n))
    got = lax.all_to_all(sent, "dp", 0, 0)
    tile = pl.BlockSpec((SUB, TC, E), lambda i: (0, i, 0))
    rows_tile = pl.BlockSpec((1, SUB * TC, E), lambda i: (i, 0, 0))
    cols_tile = pl.BlockSpec((1, E, SUB * TC), lambda i: (i, 0, 0))
    cb, cbt = pl.pallas_call(
        centre_kernel,
        grid=(steps,),
        out_shape=(shape((steps, SUB * TC, E), bf16), shape((steps, E, SUB * TC), bf16)),
        in_specs=[tile],
        out_specs=(rows_tile, cols_tile),
        compiler_params=params,
        cost_estimate=pl.CostEstimate(flops=10**9, bytes_accessed=10**7, transcendentals=0),
    )(centres)
    ut, all_labels = pl.pallas_call(
        functools.partial(gather_kernel, n),
        out_shape=(shape((E, batch), bf16), shape((1, batch), jnp.int32)),
        in_specs=[vmem],
        out_specs=(vmem, vmem),
        compiler_params=params,
    )(got)

    height = 2 * n + EXTRA
    pt, payload, own_target = pl.pallas_call(
        forward_kernel,
        grid=(steps,),
        out_shape=(
            shape((SUB, local, batch), bf16),
            shape((parts, height, E), bf16),
            shape((8, batch), f32),
        ),
        in_specs=[smem, rows_tile, cols_tile, whole((E, batch)), whole((1, batch))],
        out_specs=(
            pl.BlockSpec((SUB, TC, batch), lambda i: (0, i, 0)),
            whole((parts, height, E)),
            whole((8, batch)),
        ),
        scratch_shapes=[
            pltpu.VMEM((2, SUB * TC, BB), f32),
            pltpu.VMEM((8, batch), f32),
            pltpu.VMEM((E, batch), f32),
            pltpu.VMEM((E, batch), f32),
        ],
        compiler_params=params,
    )(where, cb, cbt, ut, all_labels)

    got1 = lax.all_to_all(payload, "dp", 0, 0)
    second = pl.pallas_call(
        functools.partial(middle_kernel, n, blocks),
        out_shape=shape((others, 32, E), bf16),
        in_specs=[vmem],
        out_specs=vmem,
        compiler_params=params,
    )(got1)
    got2 = lax.all_to_all(second, "cls", 0, 0)
    loss, ust, fac, rows = pl.pallas_call(
        functools.partial(rows_kernel, m),
        out_shape=(
            shape((1, 1), f32),
            shape((E, batch), bf16),
            shape((1, batch), f32),
            shape((others, 16, E), bf16),
        ),
        in_specs=[smem, vmem, vmem, vmem, vmem],
        out_specs=(vmem, vmem, vmem, vmem),
        compiler_params=params,
    )(where, got2, embeddings, ut, own_target)
    got3 = lax.all_to_all(rows, "cls", 0, 0)
    grad_centres = pl.pallas_call(
        backward_kernel,
        grid=(steps,),
        out_shape=shape((SUB, local, E), bf16),
        in_specs=[
            smem,
            whole((1, batch)),
            whole((E, batch)),
            whole((1, batch)),
            tile,
            pl.BlockSpec((SUB, TC, batch), lambda i: (0, i, 0)),
        ],
        out_specs=tile,
        compiler_params=params,
        cost_estimate=pl.CostEstimate(flops=4 * 10**9, bytes_accessed=2 * 10**7, transcendentals=0),
    )(where, fac, ust, all_labels, centres, pt)
    grad_embeddings = pl.pallas_call(
        functools.partial(collect_kernel, m),
        out_shape=shape((n, E), bf16),
        in_specs=[vmem],
        out_specs=vmem,
    )(got3)
    return (loss.reshape(()), grad_embeddings, grad_centres)


def solution(mesh):
    return jax.shard_map(
        per_device,
        mesh=mesh,
        in_specs=(P("dp", None), P("dp"), P(None, ("dp", "cls"), None)),
        out_specs=(P(), P("dp", None), P(None, ("dp", "cls"), None)),
        check_vma=False,
    )
```

time: 126 us -> 119 us (0.944)
  the two profiles are of different devices: /device:TPU:2 before, /device:TPU:16 now
where the time goes in v2:
time: 119 us; the launch traced here: 118 us
  blocking collectives  41.9 us (35%)
  Pallas kernels  40.7 us (34%)
  local copies, waits for them, and re-layouts  17 us (14%)
  starting transfers between devices  11.9 us (10%)
  waiting for transfers between devices  5.94 us (5%)
    pallas_call x1, Pallas kernels, per_device(): pl.pallas_call(forward_kernel, grid=(steps,), out_shape=(shape((SUB, loca...  21.5 us
    all_to_all x1, blocking collectives, per_device(): got2 = lax.all_to_all(second, 'cls', 0, 0)  21.1 us
    all_to_all x1, blocking collectives, per_device(): got1 = lax.all_to_all(payload, 'dp', 0, 0)  20.8 us
    unnamed x20, local copies, waits for them, and re-layouts  17 us
    pallas_call x1, Pallas kernels, per_device(): pl.pallas_call(backward_kernel, grid=(steps,), out_shape=shape((SUB, loca...  10.1 us
    all_to_all x1, starting transfers between devices, per_device(): got3 = lax.all_to_all(rows, 'cls', 0, 0)  6.76 us
    all_to_all x1, waiting for transfers between devices, per_device(): got = lax.all_to_all(sent, 'dp', 0, 0)  5.94 us
    all_to_all x1, starting transfers between devices, per_device(): got = lax.all_to_all(sent, 'dp', 0, 0)  5.17 us
  transfers between devices with their start and end apart: 2, of which 1 were waited for; matrix products, arithmetic and copies ran while one was open for 0% of the time, Pallas kernels for 11%

profile of v2, /device:TPU:16, one launch (start us, length us, event | category | flops | bytes accessed | tf_op | source)
XLA Modules:
  0.0 118.3 jit_solution(2876086528342644143)
XLA Ops:
  0.6 1.7 %shard_map.59 = bf16[16,80,256]{2,1,0:T(8,128)(2,1)} custom-call(s32[1]{0:T(128)} %bitcast.4.slot_ref, bf16[64,256]{1,0:T(8,128)(2,1)} %emb_ref.3, s32[1,64]{1,0:T(1,128)} %bitcast.7), custom_call_target="tpu_custom_call" | custom-call | tf_op jit(solution)/shard_map/pallas_call | solution.py:319
  2.4 5.2 %all-to-all-start = ((bf16[16,80,256]{2,1,0:T(8,128)(2,1)}), bf16[16,80,256]{2,1,0:T(8,128)(2,1)}, u32[]{:S(2)}, u32[]{:S(2)}) async-start(bf16[16,80,256]{2,1,0:T(8,128)(2,1)} %shard_map.59), calls=%async_computation | async-start | bytes 1310720 | tf_op jit(solution)/shard_map/all_to_all | solution.py:325
  7.6 0.0 copy-start.4
  7.6 1.9 %copy-done.4 = bf16[3,2048,256]{2,1,0:T(8,128)(2,1)S(1)} copy-done((bf16[3,2048,256]{2,1,0:T(8,128)(2,1)S(1)}, bf16[3,2048,256]{2,1,0:T(8,128)(2,1)}, u32[]{:S(2)}) %copy-start.4) | copy-done | bytes 3145752
  9.5 2.7 %shard_map.58 = (bf16[8,768,256]{2,1,0:T(8,128)(2,1)S(1)}, bf16[8,256,768]{2,1,0:T(8,128)(2,1)S(1)}) custom-call(bf16[3,2048,256]{2,1,0:T(8,128)(2,1)S(1)} %copy-done.4), custom_call_target="tpu_custom_call" | custom-call | flops 1000000000 | bytes 10000000 | tf_op jit(solution)/shard_map/pallas_call | solution.py:329
  12.2 0.0 copy-start.2
  12.2 1.7 %copy-done.2 = bf16[8,256,768]{2,1,0:T(8,128)(2,1)} copy-done((bf16[8,256,768]{2,1,0:T(8,128)(2,1)}, bf16[8,256,768]{2,1,0:T(8,128)(2,1)S(1)}, u32[]{:S(2)}) %copy-start.2) | copy-done | bytes 3145752
  13.9 0.1 pad_add_fusion.first_ref.where_ref
  13.9 5.9 %all-to-all-done.got_ref = bf16[16,80,256]{2,1,0:T(8,128)(2,1)} async-done(((bf16[16,80,256]{2,1,0:T(8,128)(2,1)}), bf16[16,80,256]{2,1,0:T(8,128)(2,1)}, u32[]{:S(2)}, u32[]{:S(2)}) %all-to-all-start) | async-done | bytes 655392 | tf_op jit(solution)/shard_map/all_to_all | solution.py:325
  19.9 1.3 %shard_map.60 = (bf16[256,1024]{1,0:T(8,128)(2,1)S(1)}, s32[1,1024]{1,0:T(1,128)S(1)}) custom-call(bf16[16,80,256]{2,1,0:T(8,128)(2,1)} %all-to-all-done.got_ref), custom_call_target="tpu_custom_call" | custom-call | tf_op jit(solution)/shard_map/pallas_call | solution.py:338
  21.2 0.0 copy-start.3
  21.2 1.9 %copy-done.3 = bf16[8,256,768]{2,1,0:T(8,128)(2,1)S(1)} copy-done((bf16[8,256,768]{2,1,0:T(8,128)(2,1)S(1)}, bf16[8,256,768]{2,1,0:T(8,128)(2,1)}, u32[]{:S(2)}) %copy-start.3) | copy-done | bytes 3145752
  23.1 21.5 %shard_map.61 = (bf16[3,2048,1024]{2,1,0:T(8,128)(2,1)S(1)}, bf16[16,144,256]{2,1,0:T(8,128)(2,1)S(1)}, f32[8,1024]{1,0:T(8,128)S(1)}) custom-call(s32[4]{0:T(128)S(1)} %pad_add_fusion.first_ref.where_ref, bf16[8,768,256]{2,1,0:T(8,128)(2,1)S(1)} %get-tuple-element.14.cb_ref, bf16[8,256,768]{2,1,0:T(8,128)(2,1)S(1)} %copy-done.3, ...), custom_call_target="tpu_custom_call" | custom-call | tf_op jit(solution)/shard_map/pallas_call | solution.py:347
  44.6 0.0 copy-start
  44.6 4.5 %copy-done = bf16[3,2048,1024]{2,1,0:T(8,128)(2,1)} copy-done((bf16[3,2048,1024]{2,1,0:T(8,128)(2,1)}, bf16[3,2048,1024]{2,1,0:T(8,128)(2,1)S(1)}, u32[]{:S(2)}) %copy-start) | copy-done | bytes 12582936
  49.2 0.0 copy-start.8
  49.2 0.0 copy-start.5
  49.2 20.8 %all_to_all.20.got_ref = bf16[16,144,256]{2,1,0:T(8,128)(2,1)S(1)} all-to-all(bf16[16,144,256]{2,1,0:T(8,128)(2,1)S(1)} %get-tuple-element.18), channel_id=1, replica_groups=mesh['dp'=16,'cls'=16] {'dp'}, dimensions={0} | all-to-all | bytes 2359296 | tf_op jit(solution)/shard_map/all_to_all | solution.py:370
  70.0 0.2 shard_map.62
  70.2 21.1 %all_to_all.21.got_ref = bf16[16,32,256]{2,1,0:T(8,128)(2,1)S(1)} all-to-all(bf16[16,32,256]{2,1,0:T(8,128)(2,1)S(1)} %shard_map.62), channel_id=1, replica_groups=mesh['dp'=16,'cls'=16] {'cls'}, dimensions={0} | all-to-all | bytes 524288 | tf_op jit(solution)/shard_map/all_to_all | solution.py:378
  91.3 0.0 copy-done.8
  91.3 1.6 %shard_map.63 = (f32[1,1]{1,0:T(1,128)}, bf16[256,1024]{1,0:T(8,128)(2,1)S(1)}, f32[1,1024]{1,0:T(1,128)S(1)}, bf16[16,16,256]{2,1,0:T(8,128)(2,1)}) custom-call(s32[4]{0:T(128)S(1)} %pad_add_fusion.first_ref.where_ref, bf16[16,32,256]{2,1,0:T(8,128)(2,1)S(1)} %all_to_all.21.got_ref, bf16[64,256]{1,0:T(8,128)(2,1)S(1)} %copy-done.8, ...), custom_call_target="tpu_custom_call" | custom-call | tf_op jit(solution)/shard_map/pallas_call | solution.py:379
  92.9 0.0 copy-start.6
  92.9 0.8 copy-done.6
  93.7 6.8 %all-to-all-start.3 = ((bf16[16,16,256]{2,1,0:T(8,128)(2,1)}), bf16[16,16,256]{2,1,0:T(8,128)(2,1)S(1)}, u32[]{:S(2)}, u32[]{:S(2)}) async-start(bf16[16,16,256]{2,1,0:T(8,128)(2,1)} %get-tuple-element.21), calls=%async_computation.3 | async-start | bytes 262144 | tf_op jit(solution)/shard_map/all_to_all | solution.py:391
  100.4 0.0 copy-done.5
  100.4 0.0 copy-start.1
  100.5 4.6 %copy-done.1 = bf16[3,2048,1024]{2,1,0:T(8,128)(2,1)S(1)} copy-done((bf16[3,2048,1024]{2,1,0:T(8,128)(2,1)S(1)}, bf16[3,2048,1024]{2,1,0:T(8,128)(2,1)}, u32[]{:S(2)}) %copy-start.1) | copy-done | bytes 12582936
  105.0 0.0 copy-start.7
  105.0 1.0 copy-done.7
  106.1 10.1 %shard_map.65 = bf16[3,2048,256]{2,1,0:T(8,128)(2,1)} custom-call(s32[4]{0:T(128)S(1)} %pad_add_fusion.first_ref.where_ref, f32[1,1024]{1,0:T(1,128)S(1)} %get-tuple-element.22.fac_ref, bf16[256,1024]{1,0:T(8,128)(2,1)S(1)} %copy-done.7, s32[1,1024]{1,0:T(1,128)S(1)} %get-tuple-element.17.lab_ref, bf16[3,2048,256]{2,1,0:T(8,128)(2,1)S(1)} %copy-done.5, ...), custom_call_target="tpu_custom_call" | custom-call | flops 4000000000 | bytes 20000000 | tf_op jit(solution)/shard_map/pallas_call | solution.py:392
  116.1 0.0 all-to-all-done.3.got_ref
  116.1 0.0 copy-start.9
  116.1 0.7 copy-done.9
  116.8 1.5 %shard_map.64 = bf16[64,256]{1,0:T(8,128)(2,1)} custom-call(bf16[16,16,256]{2,1,0:T(8,128)(2,1)} %copy-done.9), custom_call_target="tpu_custom_call" | custom-call | tf_op jit(solution)/shard_map/pallas_call | solution.py:408
Async XLA Ops:
  2.4 17.5 %all-to-all-start = ((bf16[16,80,256]{2,1,0:T(8,128)(2,1)}), bf16[16,80,256]{2,1,0:T(8,128)(2,1)}, u32[]{:S(2)}, u32[]{:S(2)}) async-start(bf16[16,80,256]{2,1,0:T(8,128)(2,1)} %shard_map.59), calls=%async_computation | async-start | bytes 1310720 | tf_op jit(solution)/shard_map/all_to_all | solution.py:325
  7.6 1.9 %copy-start.4 = (bf16[3,2048,256]{2,1,0:T(8,128)(2,1)S(1)}, bf16[3,2048,256]{2,1,0:T(8,128)(2,1)}, u32[]{:S(2)}) copy-start(bf16[3,2048,256]{2,1,0:T(8,128)(2,1)} %cent_ref.3) | copy-start | bytes 9437188
  12.2 1.7 %copy-start.2 = (bf16[8,256,768]{2,1,0:T(8,128)(2,1)}, bf16[8,256,768]{2,1,0:T(8,128)(2,1)S(1)}, u32[]{:S(2)}) copy-start(bf16[8,256,768]{2,1,0:T(8,128)(2,1)S(1)} %get-tuple-element.15.cbt_ref) | copy-start | bytes 9437188
  21.2 1.9 %copy-start.3 = (bf16[8,256,768]{2,1,0:T(8,128)(2,1)S(1)}, bf16[8,256,768]{2,1,0:T(8,128)(2,1)}, u32[]{:S(2)}) copy-start(bf16[8,256,768]{2,1,0:T(8,128)(2,1)} %copy-done.2) | copy-start | bytes 9437188
  44.6 4.5 %copy-start = (bf16[3,2048,1024]{2,1,0:T(8,128)(2,1)}, bf16[3,2048,1024]{2,1,0:T(8,128)(2,1)S(1)}, u32[]{:S(2)}) copy-start(bf16[3,2048,1024]{2,1,0:T(8,128)(2,1)S(1)} %get-tuple-element.24.pt_ref) | copy-start | bytes 37748740
  49.2 42.2 %copy-start.8 = (bf16[64,256]{1,0:T(8,128)(2,1)S(1)}, bf16[64,256]{1,0:T(8,128)(2,1)}, u32[]{:S(2)}) copy-start(bf16[64,256]{1,0:T(8,128)(2,1)} %emb_ref.3) | copy-start | bytes 98308
  49.2 51.3 %copy-start.5 = (bf16[3,2048,256]{2,1,0:T(8,128)(2,1)S(1)}, bf16[3,2048,256]{2,1,0:T(8,128)(2,1)}, u32[]{:S(2)}) copy-start(bf16[3,2048,256]{2,1,0:T(8,128)(2,1)} %cent_ref.3) | copy-start | bytes 9437188
  92.9 0.8 copy-start.6
  93.7 22.5 %all-to-all-start.3 = ((bf16[16,16,256]{2,1,0:T(8,128)(2,1)}), bf16[16,16,256]{2,1,0:T(8,128)(2,1)S(1)}, u32[]{:S(2)}, u32[]{:S(2)}) async-start(bf16[16,16,256]{2,1,0:T(8,128)(2,1)} %get-tuple-element.21), calls=%async_computation.3 | async-start | bytes 262144 | tf_op jit(solution)/shard_map/all_to_all | solution.py:391
  100.4 4.6 %copy-start.1 = (bf16[3,2048,1024]{2,1,0:T(8,128)(2,1)S(1)}, bf16[3,2048,1024]{2,1,0:T(8,128)(2,1)}, u32[]{:S(2)}) copy-start(bf16[3,2048,1024]{2,1,0:T(8,128)(2,1)} %copy-done) | copy-start | bytes 37748740
  105.0 1.0 copy-start.7
  116.1 0.7 copy-start.9

commit v3 on v2

--- a/solution.py
+++ b/solution.py
@@ -22,10 +22,11 @@
 
 SUB = 3
 E = 256
-TC = 256
+TC = 512
 BB = 256
 RC = 16
 EXTRA = 16
+GROUP = 8
 
 f32 = jnp.float32
 bf16 = jnp.bfloat16
@@ -111,8 +112,10 @@
         g2[...] = jnp.zeros_like(g2)
 
     first = first_ref[0] + step * TC
+    base = pl.multiple_of(step * TC, TC)
     labels = lab_ref[...] - first
-    some = jnp.max(jnp.where((labels >= 0) & (labels < TC), 1, 0)) > 0
+    inside = jnp.where((labels >= 0) & (labels < TC), 1, 0)
+    some = jnp.max(inside) > 0
 
     def block(b):
         cols = pl.ds(b * BB, BB)
@@ -136,37 +139,52 @@
             g = ex * r
             p = (g * shift, (g * e1) * (d1 + shift), (g * e2) * (d2 + shift))
             for k in range(SUB):
-                pt_ref[k, pl.ds(c * RC, RC), cols] = p[k].astype(bf16)
+                pt_ref[k, pl.ds(base + c * RC, RC), cols] = p[k].astype(bf16)
         sums[:, cols] += total
         if labelled:
             target[:, cols] += tgt
 
+    def rows_sum(b):
+        cols = pl.ds(b * BB, BB)
+        p = jnp.concatenate([pt_ref[k, pl.ds(base, TC), cols] for k in range(SUB)], axis=0)
+        g1[:, cols] += jnp.dot(cbt_ref[0], p, preferred_element_type=f32)
+
+    def rows_sum_labelled(b):
+        cols = pl.ds(b * BB, BB)
+        row = lax.broadcasted_iota(jnp.int32, (TC, BB), 0)
+        hit = row == labels[:, b * BB : (b + 1) * BB]
+        for k in range(SUB):
+            p = pt_ref[k, pl.ds(base, TC), cols].astype(f32)
+            own = jnp.where(hit, p, 0.0).astype(bf16)
+            rest = jnp.where(hit, 0.0, p).astype(bf16)
+            cbt = cbt_ref[0, :, pl.ds(k * TC, TC)]
+            g1[:, cols] += jnp.dot(cbt, rest, preferred_element_type=f32)
+            g2[:, cols] += jnp.dot(cbt, own, preferred_element_type=f32)
+
     @pl.when(jnp.logical_not(some))
     def _():
         block(0)
         for b in range(batch // BB):
-            cols = pl.ds(b * BB, BB)
             if (b + 1) * BB < batch:
                 block(b + 1)
             terms(b, False)
-            p = jnp.concatenate([pt_ref[k, :, cols] for k in range(SUB)], axis=0)
-            g1[:, cols] += jnp.dot(cbt_ref[0], p, preferred_element_type=f32)
+            rows_sum(b)
 
     @pl.when(some)
     def _():
-        block(0)
         for b in range(batch // BB):
-            cols = pl.ds(b * BB, BB)
-            if (b + 1) * BB < batch:
-                block(b + 1)
-            terms(b, True)
-            row = lax.broadcasted_iota(jnp.int32, (TC, BB), 0)
-            hit = row == labels[:, b * BB : (b + 1) * BB]
-            p = [pt_ref[k, :, cols].astype(f32) for k in range(SUB)]
-            own = jnp.concatenate([jnp.where(hit, v, 0.0) for v in p], axis=0).astype(bf16)
-            rest = jnp.concatenate([jnp.where(hit, 0.0, v) for v in p], axis=0).astype(bf16)
-            g1[:, cols] += jnp.dot(cbt_ref[0], rest, preferred_element_type=f32)
-            g2[:, cols] += jnp.dot(cbt_ref[0], own, preferred_element_type=f32)
+            block(b)
+            here = jnp.max(inside[:, b * BB : (b + 1) * BB]) > 0
+
+            @pl.when(here)
+            def _():
+                terms(b, True)
+                rows_sum_labelled(b)
+
+            @pl.when(jnp.logical_not(here))
+            def _():
+                terms(b, False)
+                rows_sum(b)
 
     @pl.when(step == steps - 1)
     def _():
@@ -219,12 +237,13 @@
     acc = summed(got_ref)
     extra = pack_extra(*unpack_extra(acc[2 * n :], blocks))
     others, height = out_ref.shape[0], out_ref.shape[1]
-    m = n // others
+    m = n // GROUP
     pad = jnp.zeros((height - 2 * m - EXTRA, E), f32)
     for j in range(others):
-        one = acc[j * m : (j + 1) * m]
-        two = acc[n + j * m : n + (j + 1) * m]
-        out_ref[j] = jnp.concatenate([one, two, extra, pad], axis=0).astype(bf16)
+        at = (j % GROUP) * m
+        one = acc[at : at + m]
+        two = acc[n + at : n + at + m]
+        out_ref[j] = jnp.concatenate([one, two, extra] + [pad] * (pad.shape[0] > 0), axis=0).astype(bf16)
 
 
 def rows_kernel(
@@ -257,22 +276,24 @@
     r = inv_norm(rows)
     unit = rows * r
     g = (g - unit * jnp.sum(unit * g, axis=1, keepdims=True)) * r
-    g = jnp.concatenate([g, jnp.zeros((16 - m, E), f32)], axis=0).astype(bf16)
     for j in range(rows_ref.shape[0]):
-        rows_ref[j] = g
-
-
-def collect_kernel(m, got_ref, out_ref):
-    parts = [got_ref[j].astype(f32)[0:m] for j in range(got_ref.shape[0])]
-    out_ref[...] = jnp.concatenate(parts, axis=0).astype(bf16)
-
-
-def backward_kernel(first_ref, fac_ref, ust_ref, lab_ref, cent_ref, pt_ref, gc_ref):
+        rows_ref[j] = g.astype(bf16)
+
+
+def backward_kernel(
+    first_ref, fac_ref, ust_ref, lab_ref, got_ref, cent_ref, pt_ref, ge_ref, gc_ref
+):
     step = pl.program_id(0)
     batch = ust_ref.shape[1]
     first = first_ref[0] + step * TC
+    base = pl.multiple_of(step * TC, TC)
     labels = lab_ref[...] - first
     some = jnp.max(jnp.where((labels >= 0) & (labels < TC), 1, 0)) > 0
+
+    @pl.when(step == 0)
+    def _():
+        parts = [got_ref[j].astype(f32) for j in range(got_ref.shape[0])]
+        ge_ref[...] = jnp.concatenate(parts, axis=0).astype(bf16)
 
     def finish(k, p):
         dims = (((1,), (1,)), ((), ()))
@@ -286,14 +307,14 @@
     @pl.when(jnp.logical_not(some))
     def _():
         for k in range(SUB):
-            finish(k, pt_ref[k])
+            finish(k, pt_ref[k, pl.ds(base, TC), :])
 
     @pl.when(some)
     def _():
         hit = lax.broadcasted_iota(jnp.int32, (TC, batch), 0) == labels
         factor = jnp.where(hit, fac_ref[...], 1.0)
         for k in range(SUB):
-            finish(k, (pt_ref[k].astype(f32) * factor).astype(bf16))
+            finish(k, (pt_ref[k, pl.ds(base, TC), :].astype(f32) * factor).astype(bf16))
 
 
 def per_device(embeddings, labels, centres):
@@ -304,12 +325,13 @@
     blocks = batch // E
     local = centres.shape[1]
     steps = local // TC
-    m = n // others
+    m = n // GROUP
     dp = lax.axis_index("dp")
     cls = lax.axis_index("cls")
     first = (dp * others + cls) * local
     slot = (dp & (E // n - 1)) * n
-    where = jnp.stack([first, dp * n + cls * m, slot + cls * m, cls * m]).astype(jnp.int32)
+    at = (cls & (GROUP - 1)) * m
+    where = jnp.stack([first, dp * n + at, slot + at, at]).astype(jnp.int32)
     smem = pl.BlockSpec(memory_space=pltpu.SMEM)
     vmem = pl.BlockSpec(memory_space=pltpu.VMEM)
     whole = lambda shape: pl.BlockSpec(shape, lambda i: (0,) * len(shape))
@@ -354,7 +376,7 @@
         ),
         in_specs=[smem, rows_tile, cols_tile, whole((E, batch)), whole((1, batch))],
         out_specs=(
-            pl.BlockSpec((SUB, TC, batch), lambda i: (0, i, 0)),
+            vmem,
             whole((parts, height, E)),
             whole((8, batch)),
         ),
@@ -382,35 +404,30 @@
             shape((1, 1), f32),
             shape((E, batch), bf16),
             shape((1, batch), f32),
-            shape((others, 16, E), bf16),
+            shape((GROUP, m, E), bf16),
         ),
         in_specs=[smem, vmem, vmem, vmem, vmem],
         out_specs=(vmem, vmem, vmem, vmem),
         compiler_params=params,
     )(where, got2, embeddings, ut, own_target)
-    got3 = lax.all_to_all(rows, "cls", 0, 0)
-    grad_centres = pl.pallas_call(
+    groups = [list(range(g, g + GROUP)) for g in range(0, others, GROUP)]
+    got3 = lax.all_to_all(rows, "cls", 0, 0, axis_index_groups=groups)
+    grad_embeddings, grad_centres = pl.pallas_call(
         backward_kernel,
         grid=(steps,),
-        out_shape=shape((SUB, local, E), bf16),
+        out_shape=(shape((n, E), bf16), shape((SUB, local, E), bf16)),
         in_specs=[
             smem,
             whole((1, batch)),
             whole((E, batch)),
             whole((1, batch)),
+            whole((GROUP, m, E)),
             tile,
-            pl.BlockSpec((SUB, TC, batch), lambda i: (0, i, 0)),
+            vmem,
         ],
-        out_specs=tile,
-        compiler_params=params,
-        cost_estimate=pl.CostEstimate(flops=4 * 10**9, bytes_accessed=2 * 10**7, transcendentals=0),
-    )(where, fac, ust, all_labels, centres, pt)
-    grad_embeddings = pl.pallas_call(
-        functools.partial(collect_kernel, m),
-        out_shape=shape((n, E), bf16),
-        in_specs=[vmem],
-        out_specs=vmem,
-    )(got3)
+        out_specs=(whole((n, E)), tile),
+        compiler_params=params,
+    )(where, fac, ust, all_labels, got3, centres, pt)
     return (loss.reshape(()), grad_embeddings, grad_centres)
 
 

time: 119 us -> 113 us (0.950)
  the two profiles are of different devices: /device:TPU:16 before, /device:TPU:2 now
where the time goes in v3:
time: 113 us
  blocking collectives  58.1 us (51%)
  Pallas kernels  38.9 us (34%)
  starting transfers between devices  6.27 us (6%)
  local copies, waits for them, and re-layouts  5.44 us (5%)
  waiting for transfers between devices  3.27 us (3%)
    pallas_call x1, Pallas kernels, per_device(): pl.pallas_call(forward_kernel, grid=(steps,), out_shape=(shape((SUB, loca...  23.5 us
    all_to_all x1, blocking collectives, per_device(): got2 = lax.all_to_all(second, 'cls', 0, 0)  23.2 us
    all_to_all x1, blocking collectives, per_device(): got1 = lax.all_to_all(payload, 'dp', 0, 0)  22.8 us
    all_to_all x1, blocking collectives, per_device(): got3 = lax.all_to_all(rows, 'cls', 0, 0, axis_index_groups=groups)  12 us
    pallas_call x1, Pallas kernels, per_device(): pl.pallas_call(backward_kernel, grid=(steps,), out_shape=(shape((n, E), b...  8.33 us
    all_to_all x1, starting transfers between devices, per_device(): got = lax.all_to_all(sent, 'dp', 0, 0)  6.27 us
    unnamed x10, local copies, waits for them, and re-layouts  5.44 us
    all_to_all x1, waiting for transfers between devices, per_device(): got = lax.all_to_all(sent, 'dp', 0, 0)  3.27 us
  transfers between devices with their start and end apart: 1, of which 1 were waited for; matrix products, arithmetic and copies ran while one was open for 0% of the time, Pallas kernels for 2%

profile of v3, /device:TPU:2, one launch (start us, length us, event | category | flops | bytes accessed | tf_op | source)
XLA Modules:
  0.0 112.8 jit_solution(7407261175363056720)
XLA Ops:
  0.6 1.7 %shard_map.59 = bf16[16,80,256]{2,1,0:T(8,128)(2,1)} custom-call(s32[1]{0:T(128)} %bitcast.4.slot_ref, bf16[64,256]{1,0:T(8,128)(2,1)} %emb_ref.3, s32[1,64]{1,0:T(1,128)} %bitcast.7), custom_call_target="tpu_custom_call" | custom-call | tf_op jit(solution)/shard_map/pallas_call | solution.py:341
  2.4 6.3 %all-to-all-start = ((bf16[16,80,256]{2,1,0:T(8,128)(2,1)}), bf16[16,80,256]{2,1,0:T(8,128)(2,1)}, u32[]{:S(2)}, u32[]{:S(2)}) async-start(bf16[16,80,256]{2,1,0:T(8,128)(2,1)} %shard_map.59), calls=%async_computation | async-start | bytes 1310720 | tf_op jit(solution)/shard_map/all_to_all | solution.py:347
  8.6 0.0 copy-start
  8.7 1.9 %copy-done = bf16[3,2048,256]{2,1,0:T(8,128)(2,1)S(1)} copy-done((bf16[3,2048,256]{2,1,0:T(8,128)(2,1)S(1)}, bf16[3,2048,256]{2,1,0:T(8,128)(2,1)}, u32[]{:S(2)}) %copy-start) | copy-done | bytes 3145752
  10.5 2.4 %shard_map.58 = (bf16[4,1536,256]{2,1,0:T(8,128)(2,1)S(1)}, bf16[4,256,1536]{2,1,0:T(8,128)(2,1)S(1)}) custom-call(bf16[3,2048,256]{2,1,0:T(8,128)(2,1)S(1)} %copy-done), custom_call_target="tpu_custom_call" | custom-call | flops 1000000000 | bytes 10000000 | tf_op jit(solution)/shard_map/pallas_call | solution.py:351
  12.9 0.0 copy-start.2
  12.9 1.7 %copy-done.2 = bf16[4,256,1536]{2,1,0:T(8,128)(2,1)} copy-done((bf16[4,256,1536]{2,1,0:T(8,128)(2,1)}, bf16[4,256,1536]{2,1,0:T(8,128)(2,1)S(1)}, u32[]{:S(2)}) %copy-start.2) | copy-done | bytes 3145752
  14.6 0.1 pad_add_fusion.first_ref.where_ref
  14.6 3.3 %all-to-all-done.got_ref = bf16[16,80,256]{2,1,0:T(8,128)(2,1)} async-done(((bf16[16,80,256]{2,1,0:T(8,128)(2,1)}), bf16[16,80,256]{2,1,0:T(8,128)(2,1)}, u32[]{:S(2)}, u32[]{:S(2)}) %all-to-all-start) | async-done | bytes 655392 | tf_op jit(solution)/shard_map/all_to_all | solution.py:347
  17.9 1.3 %shard_map.60 = (bf16[256,1024]{1,0:T(8,128)(2,1)S(1)}, s32[1,1024]{1,0:T(1,128)S(1)}) custom-call(bf16[16,80,256]{2,1,0:T(8,128)(2,1)} %all-to-all-done.got_ref), custom_call_target="tpu_custom_call" | custom-call | tf_op jit(solution)/shard_map/pallas_call | solution.py:360
  19.2 0.0 copy-start.3
  19.2 1.9 %copy-done.3 = bf16[4,256,1536]{2,1,0:T(8,128)(2,1)S(1)} copy-done((bf16[4,256,1536]{2,1,0:T(8,128)(2,1)S(1)}, bf16[4,256,1536]{2,1,0:T(8,128)(2,1)}, u32[]{:S(2)}) %copy-start.3) | copy-done | bytes 3145752
  21.1 23.5 %shard_map.61 = (bf16[3,2048,1024]{2,1,0:T(8,128)(2,1)S(1)}, bf16[16,144,256]{2,1,0:T(8,128)(2,1)S(1)}, f32[8,1024]{1,0:T(8,128)S(1)}) custom-call(s32[4]{0:T(128)S(1)} %pad_add_fusion.first_ref.where_ref, bf16[4,1536,256]{2,1,0:T(8,128)(2,1)S(1)} %get-tuple-element.16.cb_ref, bf16[4,256,1536]{2,1,0:T(8,128)(2,1)S(1)} %copy-done.3, ...), custom_call_target="tpu_custom_call" | custom-call | tf_op jit(solution)/shard_map/pallas_call | solution.py:369
  44.7 0.0 copy-start.4
  44.7 0.0 copy-start.1
  44.7 22.8 %all_to_all.20.got_ref = bf16[16,144,256]{2,1,0:T(8,128)(2,1)S(1)} all-to-all(bf16[16,144,256]{2,1,0:T(8,128)(2,1)S(1)} %get-tuple-element.20), channel_id=1, replica_groups=mesh['dp'=16,'cls'=16] {'dp'}, dimensions={0} | all-to-all | bytes 2359296 | tf_op jit(solution)/shard_map/all_to_all | solution.py:392
  67.5 0.2 shard_map.62
  67.8 23.2 %all_to_all.21.got_ref = bf16[16,32,256]{2,1,0:T(8,128)(2,1)S(1)} all-to-all(bf16[16,32,256]{2,1,0:T(8,128)(2,1)S(1)} %shard_map.62), channel_id=1, replica_groups=mesh['dp'=16,'cls'=16] {'cls'}, dimensions={0} | all-to-all | bytes 524288 | tf_op jit(solution)/shard_map/all_to_all | solution.py:400
  91.0 0.0 copy-done.4
  91.0 1.4 %shard_map.63 = (f32[1,1]{1,0:T(1,128)}, bf16[256,1024]{1,0:T(8,128)(2,1)S(1)}, f32[1,1024]{1,0:T(1,128)S(1)}, bf16[8,8,256]{2,1,0:T(8,128)(2,1)S(1)}) custom-call(s32[4]{0:T(128)S(1)} %pad_add_fusion.first_ref.where_ref, bf16[16,32,256]{2,1,0:T(8,128)(2,1)S(1)} %all_to_all.21.got_ref, bf16[64,256]{1,0:T(8,128)(2,1)S(1)} %copy-done.4, ...), custom_call_target="tpu_custom_call" | custom-call | tf_op jit(solution)/shard_map/pallas_call | solution.py:401
  92.4 12.0 %all_to_all.22.got_ref = bf16[8,8,256]{2,1,0:T(8,128)(2,1)S(1)} all-to-all(bf16[8,8,256]{2,1,0:T(8,128)(2,1)S(1)} %get-tuple-element.25), channel_id=1, replica_groups={{0,1,2,3,4,5,6,7},{8,9,10,11,12,13,14,15},{16,17,18,19,20,21,22,23},{24..., dimensions={0} | all-to-all | bytes 65536 | tf_op jit(solution)/shard_map/all_to_all | solution.py:414
  104.4 0.0 copy-done.1
  104.4 8.3 %shard_map.64 = (bf16[64,256]{1,0:T(8,128)(2,1)}, bf16[3,2048,256]{2,1,0:T(8,128)(2,1)}) custom-call(s32[4]{0:T(128)S(1)} %pad_add_fusion.first_ref.where_ref, f32[1,1024]{1,0:T(1,128)S(1)} %get-tuple-element.23.fac_ref, bf16[256,1024]{1,0:T(8,128)(2,1)S(1)} %get-tuple-element.24.ust_ref, s32[1,1024]{1,0:T(1,128)S(1)} %get-tuple-element.19.lab_ref, ...), custom_call_target="tpu_custom_call" | custom-call | tf_op jit(solution)/shard_map/pallas_call | solution.py:415
Async XLA Ops:
  2.4 15.5 %all-to-all-start = ((bf16[16,80,256]{2,1,0:T(8,128)(2,1)}), bf16[16,80,256]{2,1,0:T(8,128)(2,1)}, u32[]{:S(2)}, u32[]{:S(2)}) async-start(bf16[16,80,256]{2,1,0:T(8,128)(2,1)} %shard_map.59), calls=%async_computation | async-start | bytes 1310720 | tf_op jit(solution)/shard_map/all_to_all | solution.py:347
  8.6 1.9 %copy-start = (bf16[3,2048,256]{2,1,0:T(8,128)(2,1)S(1)}, bf16[3,2048,256]{2,1,0:T(8,128)(2,1)}, u32[]{:S(2)}) copy-start(bf16[3,2048,256]{2,1,0:T(8,128)(2,1)} %cent_ref.3) | copy-start | bytes 9437188
  12.9 1.7 %copy-start.2 = (bf16[4,256,1536]{2,1,0:T(8,128)(2,1)}, bf16[4,256,1536]{2,1,0:T(8,128)(2,1)S(1)}, u32[]{:S(2)}) copy-start(bf16[4,256,1536]{2,1,0:T(8,128)(2,1)S(1)} %get-tuple-element.17.cbt_ref) | copy-start | bytes 9437188
  19.2 1.9 %copy-start.3 = (bf16[4,256,1536]{2,1,0:T(8,128)(2,1)S(1)}, bf16[4,256,1536]{2,1,0:T(8,128)(2,1)}, u32[]{:S(2)}) copy-start(bf16[4,256,1536]{2,1,0:T(8,128)(2,1)} %copy-done.2) | copy-start | bytes 9437188
  44.7 46.4 %copy-start.4 = (bf16[64,256]{1,0:T(8,128)(2,1)S(1)}, bf16[64,256]{1,0:T(8,128)(2,1)}, u32[]{:S(2)}) copy-start(bf16[64,256]{1,0:T(8,128)(2,1)} %emb_ref.3) | copy-start | bytes 98308
  44.7 59.7 %copy-start.1 = (bf16[3,2048,256]{2,1,0:T(8,128)(2,1)S(1)}, bf16[3,2048,256]{2,1,0:T(8,128)(2,1)}, u32[]{:S(2)}) copy-start(bf16[3,2048,256]{2,1,0:T(8,128)(2,1)} %cent_ref.3) | copy-start | bytes 9437188

commit v4 on v3

--- a/solution.py
+++ b/solution.py
@@ -24,7 +24,9 @@
 E = 256
 TC = 512
 BB = 256
+FT = 256
 RC = 16
+AWAY = -1e4
 EXTRA = 16
 GROUP = 8
 
@@ -70,7 +72,7 @@
         cbt_ref[0, :, pl.ds(k * TC, TC)] = unit.T.astype(bf16)
 
 
-def gather_kernel(rows_own, got_ref, ut_ref, lab_ref):
+def gather_kernel(rows_own, where_ref, got_ref, ut_ref, lab_ref, flag_ref):
     parts = got_ref.shape[0]
     per = E // rows_own
     for q in range(parts // per):
@@ -83,6 +85,16 @@
             [got_ref[q * per + j, pl.ds(0, rows_own), :].astype(f32) for j in range(per)], axis=0
         )
         ut_ref[:, pl.ds(q * E, E)] = block.T.astype(bf16)
+    tiles, width = flag_ref.shape
+    batch = lab_ref.shape[1]
+    tile = (lab_ref[...] - where_ref[0]) >> (FT.bit_length() - 1)
+    hits = (lax.broadcasted_iota(jnp.int32, (tiles, batch), 0) == tile).astype(f32)
+    lane = lax.broadcasted_iota(jnp.int32, (tiles, width), 1)
+    flags = jnp.zeros((tiles, width), f32)
+    for b in range(batch // BB):
+        count = jnp.sum(hits[:, b * BB : (b + 1) * BB], axis=1, keepdims=True)
+        flags = jnp.where(lane == b, count, flags)
+    flag_ref[...] = flags.astype(jnp.int32)
 
 
 def elementwise(c0, c1, c2):
@@ -98,7 +110,8 @@
 
 
 def forward_kernel(
-    first_ref, cb_ref, cbt_ref, ut_ref, lab_ref, pt_ref, out_ref, target, xs, sums, g1, g2
+    first_ref, flag_ref, cb_ref, cbt_ref, ut_ref, lab_ref,
+    pt_ref, out_ref, target, own_ref, xs, sums, g1, g2,
 ):
     step = pl.program_id(0)
     steps = pl.num_programs(0)
@@ -108,32 +121,45 @@
     def _():
         sums[...] = jnp.zeros_like(sums)
         target[...] = jnp.zeros_like(target)
+        own_ref[...] = jnp.zeros_like(own_ref)
         g1[...] = jnp.zeros_like(g1)
         g2[...] = jnp.zeros_like(g2)
 
     first = first_ref[0] + step * TC
     base = pl.multiple_of(step * TC, TC)
-    labels = lab_ref[...] - first
-    inside = jnp.where((labels >= 0) & (labels < TC), 1, 0)
-    some = jnp.max(inside) > 0
 
     def block(b):
         cols = pl.ds(b * BB, BB)
         xs[b % 2] = jnp.dot(cb_ref[0], ut_ref[:, cols], preferred_element_type=f32)
 
-    def terms(b, labelled):
+    def set_labels_apart(b, h):
+        cols = pl.ds(b * BB, BB)
+        row = lax.broadcasted_iota(jnp.int32, (FT, BB), 0) + h * FT
+        hit = row == lab_ref[:, cols] - first
+        known = jnp.sum(jnp.where(hit, 1.0, 0.0), axis=0, keepdims=True) > 0
+        x = []
+        for k in range(SUB):
+            rows = pl.ds(k * TC + h * FT, FT)
+            v = xs[b % 2, rows, :]
+            x.append(jnp.sum(jnp.where(hit, v, 0.0), axis=0, keepdims=True))
+            xs[b % 2, rows, :] = jnp.where(hit, AWAY, v)
+        e1, e2, d1, d2, r, power, shift = elementwise(*x)
+        power = power - MARGIN2
+        target[0:1, cols] += jnp.where(known, power, 0.0)
+        sums[0:1, cols] += jnp.where(known, jnp.exp2(power), 0.0)
+        p = (r * shift, (r * e1) * (d1 + shift), (r * e2) * (d2 + shift))
+        for k in range(SUB):
+            own_ref[k : k + 1, cols] += jnp.where(known, p[k], 0.0)
+            own = jnp.where(hit, p[k], 0.0).astype(bf16)
+            cbt = cbt_ref[0, :, pl.ds(k * TC + h * FT, FT)]
+            g2[:, cols] += jnp.dot(cbt, own, preferred_element_type=f32)
+
+    def terms(b):
         cols = pl.ds(b * BB, BB)
         total = jnp.zeros((8, BB), f32)
-        tgt = jnp.zeros((8, BB), f32)
         for c in range(TC // RC):
             x = [xs[b % 2, pl.ds(k * TC + c * RC, RC), :] for k in range(SUB)]
             e1, e2, d1, d2, r, power, shift = elementwise(*x)
-            if labelled:
-                row = lax.broadcasted_iota(jnp.int32, (RC, BB), 0) + c * RC
-                hit = row == labels[:, b * BB : (b + 1) * BB]
-                power = jnp.where(hit, power - MARGIN2, power)
-                t = jnp.where(hit, power, 0.0)
-                tgt += t[0:8] + t[8:16]
             ex = jnp.exp2(power)
             total += ex[0:8] + ex[8:16]
             g = ex * r
@@ -141,50 +167,22 @@
             for k in range(SUB):
                 pt_ref[k, pl.ds(base + c * RC, RC), cols] = p[k].astype(bf16)
         sums[:, cols] += total
-        if labelled:
-            target[:, cols] += tgt
 
     def rows_sum(b):
         cols = pl.ds(b * BB, BB)
         p = jnp.concatenate([pt_ref[k, pl.ds(base, TC), cols] for k in range(SUB)], axis=0)
         g1[:, cols] += jnp.dot(cbt_ref[0], p, preferred_element_type=f32)
 
-    def rows_sum_labelled(b):
-        cols = pl.ds(b * BB, BB)
-        row = lax.broadcasted_iota(jnp.int32, (TC, BB), 0)
-        hit = row == labels[:, b * BB : (b + 1) * BB]
-        for k in range(SUB):
-            p = pt_ref[k, pl.ds(base, TC), cols].astype(f32)
-            own = jnp.where(hit, p, 0.0).astype(bf16)
-            rest = jnp.where(hit, 0.0, p).astype(bf16)
-            cbt = cbt_ref[0, :, pl.ds(k * TC, TC)]
-            g1[:, cols] += jnp.dot(cbt, rest, preferred_element_type=f32)
-            g2[:, cols] += jnp.dot(cbt, own, preferred_element_type=f32)
-
-    @pl.when(jnp.logical_not(some))
-    def _():
-        block(0)
-        for b in range(batch // BB):
-            if (b + 1) * BB < batch:
-                block(b + 1)
-            terms(b, False)
-            rows_sum(b)
-
-    @pl.when(some)
-    def _():
-        for b in range(batch // BB):
-            block(b)
-            here = jnp.max(inside[:, b * BB : (b + 1) * BB]) > 0
-
-            @pl.when(here)
-            def _():
-                terms(b, True)
-                rows_sum_labelled(b)
-
-            @pl.when(jnp.logical_not(here))
-            def _():
-                terms(b, False)
-                rows_sum(b)
+    block(0)
+    for b in range(batch // BB):
+        for h in range(TC // FT):
+            pl.when(flag_ref[step * (TC // FT) + h, b] > 0)(
+                functools.partial(set_labels_apart, b, h)
+            )
+        if (b + 1) * BB < batch:
+            block(b + 1)
+        terms(b)
+        rows_sum(b)
 
     @pl.when(step == steps - 1)
     def _():
@@ -194,13 +192,12 @@
         blocks = batch // E
         tot = jnp.sum(sums[...], axis=0, keepdims=True)
         tgt = jnp.sum(target[...], axis=0, keepdims=True)
-        scale = jnp.exp2(-tgt)
         all_targets = jnp.sum(tgt, axis=1, keepdims=True)
         totals = jnp.concatenate([tot[:, q * E : (q + 1) * E] for q in range(blocks)], axis=0)
         for q in range(blocks):
             cols = slice(q * E, (q + 1) * E)
             a = g1[:, cols].T.astype(bf16)
-            o = (g2[:, cols] * scale[:, cols]).T.astype(bf16)
+            o = g2[:, cols].T.astype(bf16)
             extra = pack_extra(totals, tgt[:, cols], all_targets).astype(bf16)
             for j in range(per):
                 out_ref[q * per + j, pl.ds(0, n), :] = a[j * n : (j + 1) * n]
@@ -247,7 +244,8 @@
 
 
 def rows_kernel(
-    m, where_ref, got_ref, emb_ref, ut_ref, own_ref, loss_ref, ust_ref, fac_ref, rows_ref
+    m, where_ref, got_ref, emb_ref, ut_ref, target_ref, own_ref,
+    loss_ref, ust_ref, fac_ref, rows_ref,
 ):
     batch = ut_ref.shape[1]
     blocks = batch // E
@@ -259,8 +257,8 @@
     loss_ref[...] = logs * (1.0 / batch)
     inv = OUT_SCALE / tot
     ust_ref[...] = (ut_ref[...].astype(f32) * inv).astype(bf16)
-    own = jnp.sum(own_ref[...], axis=0, keepdims=True)
-    fac_ref[...] = 1.0 - tot * jnp.exp2(-own)
+    own_target = jnp.sum(target_ref[...], axis=0, keepdims=True)
+    fac_ref[...] = own_ref[...] * (jnp.exp2(own_target) - tot)
     lane = lax.broadcasted_iota(jnp.int32, (m, batch), 1)
     row = lax.broadcasted_iota(jnp.int32, (m, batch), 0)
     inv_col = jnp.sum(jnp.where(lane == row + where_ref[1], inv, 0.0), axis=1, keepdims=True)
@@ -281,40 +279,61 @@
 
 
 def backward_kernel(
-    first_ref, fac_ref, ust_ref, lab_ref, got_ref, cent_ref, pt_ref, ge_ref, gc_ref
+    first_ref, flag_ref, fac_ref, ust_ref, lab_ref, got_ref, cent_ref, pt_ref, ge_ref, gc_ref, gs
 ):
     step = pl.program_id(0)
     batch = ust_ref.shape[1]
     first = first_ref[0] + step * TC
     base = pl.multiple_of(step * TC, TC)
-    labels = lab_ref[...] - first
-    some = jnp.max(jnp.where((labels >= 0) & (labels < TC), 1, 0)) > 0
+    dims = (((1,), (1,)), ((), ()))
 
     @pl.when(step == 0)
     def _():
         parts = [got_ref[j].astype(f32) for j in range(got_ref.shape[0])]
         ge_ref[...] = jnp.concatenate(parts, axis=0).astype(bf16)
 
-    def finish(k, p):
-        dims = (((1,), (1,)), ((), ()))
-        g = lax.dot_general(p, ust_ref[...], dims, preferred_element_type=f32)
+    def product(k):
+        return lax.dot_general(
+            pt_ref[k, pl.ds(base, TC), :], ust_ref[...], dims, preferred_element_type=f32
+        )
+
+    def finish(k, g):
         rows = cent_ref[k].astype(f32)
         r = inv_norm(rows)
         unit = rows * r
         g = (g - unit * jnp.sum(unit * g, axis=1, keepdims=True)) * r
         gc_ref[k] = g.astype(bf16)
 
+    def add_labels(b, h):
+        cols = pl.ds(b * BB, BB)
+        row = lax.broadcasted_iota(jnp.int32, (FT, BB), 0) + h * FT
+        hit = row == lab_ref[:, cols] - first
+        for k in range(SUB):
+            own = jnp.where(hit, fac_ref[k : k + 1, cols], 0.0).astype(bf16)
+            gs[k, pl.ds(h * FT, FT), :] += lax.dot_general(
+                own, ust_ref[:, cols], dims, preferred_element_type=f32
+            )
+
+    flags = [
+        (b, h, flag_ref[step * (TC // FT) + h, b])
+        for b in range(batch // BB)
+        for h in range(TC // FT)
+    ]
+    some = sum(f for _, _, f in flags) > 0
+
     @pl.when(jnp.logical_not(some))
     def _():
         for k in range(SUB):
-            finish(k, pt_ref[k, pl.ds(base, TC), :])
+            finish(k, product(k))
 
     @pl.when(some)
     def _():
-        hit = lax.broadcasted_iota(jnp.int32, (TC, batch), 0) == labels
-        factor = jnp.where(hit, fac_ref[...], 1.0)
-        for k in range(SUB):
-            finish(k, (pt_ref[k, pl.ds(base, TC), :].astype(f32) * factor).astype(bf16))
+        for k in range(SUB):
+            gs[k] = product(k)
+        for b, h, flag in flags:
+            pl.when(flag > 0)(functools.partial(add_labels, b, h))
+        for k in range(SUB):
+            finish(k, gs[k])
 
 
 def per_device(embeddings, labels, centres):
@@ -357,27 +376,33 @@
         compiler_params=params,
         cost_estimate=pl.CostEstimate(flops=10**9, bytes_accessed=10**7, transcendentals=0),
     )(centres)
-    ut, all_labels = pl.pallas_call(
+    ut, all_labels, flags = pl.pallas_call(
         functools.partial(gather_kernel, n),
-        out_shape=(shape((E, batch), bf16), shape((1, batch), jnp.int32)),
-        in_specs=[vmem],
-        out_specs=(vmem, vmem),
-        compiler_params=params,
-    )(got)
+        out_shape=(
+            shape((E, batch), bf16),
+            shape((1, batch), jnp.int32),
+            shape((local // FT, 128), jnp.int32),
+        ),
+        in_specs=[smem, vmem],
+        out_specs=(vmem, vmem, vmem),
+        compiler_params=params,
+    )(where, got)
 
     height = 2 * n + EXTRA
-    pt, payload, own_target = pl.pallas_call(
+    pt, payload, own_target, own = pl.pallas_call(
         forward_kernel,
         grid=(steps,),
         out_shape=(
             shape((SUB, local, batch), bf16),
             shape((parts, height, E), bf16),
             shape((8, batch), f32),
+            shape((8, batch), f32),
         ),
-        in_specs=[smem, rows_tile, cols_tile, whole((E, batch)), whole((1, batch))],
+        in_specs=[smem, smem, rows_tile, cols_tile, whole((E, batch)), whole((1, batch))],
         out_specs=(
             vmem,
             whole((parts, height, E)),
+            whole((8, batch)),
             whole((8, batch)),
         ),
         scratch_shapes=[
@@ -387,7 +412,7 @@
             pltpu.VMEM((E, batch), f32),
         ],
         compiler_params=params,
-    )(where, cb, cbt, ut, all_labels)
+    )(where, flags, cb, cbt, ut, all_labels)
 
     got1 = lax.all_to_all(payload, "dp", 0, 0)
     second = pl.pallas_call(
@@ -403,13 +428,13 @@
         out_shape=(
             shape((1, 1), f32),
             shape((E, batch), bf16),
-            shape((1, batch), f32),
+            shape((8, batch), f32),
             shape((GROUP, m, E), bf16),
         ),
-        in_specs=[smem, vmem, vmem, vmem, vmem],
+        in_specs=[smem, vmem, vmem, vmem, vmem, vmem],
         out_specs=(vmem, vmem, vmem, vmem),
         compiler_params=params,
-    )(where, got2, embeddings, ut, own_target)
+    )(where, got2, embeddings, ut, own_target, own)
     groups = [list(range(g, g + GROUP)) for g in range(0, others, GROUP)]
     got3 = lax.all_to_all(rows, "cls", 0, 0, axis_index_groups=groups)
     grad_embeddings, grad_centres = pl.pallas_call(
@@ -418,7 +443,8 @@
         out_shape=(shape((n, E), bf16), shape((SUB, local, E), bf16)),
         in_specs=[
             smem,
-            whole((1, batch)),
+            smem,
+            whole((8, batch)),
             whole((E, batch)),
             whole((1, batch)),
             whole((GROUP, m, E)),
@@ -426,8 +452,9 @@
             vmem,
         ],
         out_specs=(whole((n, E)), tile),
-        compiler_params=params,
-    )(where, fac, ust, all_labels, got3, centres, pt)
+        scratch_shapes=[pltpu.VMEM((SUB, TC, E), f32)],
+        compiler_params=params,
+    )(where, flags, fac, ust, all_labels, got3, centres, pt)
     return (loss.reshape(()), grad_embeddings, grad_centres)
 
 

time: 113 us -> 112 us (level)
  blocking collectives: 58.1 us -> 56.9 us
    pallas_call x1, Pallas kernels: 23.5 us -> 22.3 us  [per_device(): pl.pallas_call(forward_kernel, grid=(steps,), out_shape=(shape((SUB, loca...]
where the time goes in v4:
time: 112 us; the launch traced here: 111 us
  blocking collectives  56.9 us (51%)
  Pallas kernels  38.4 us (34%)
  starting transfers between devices  6.27 us (6%)
  local copies, waits for them, and re-layouts  5.45 us (5%)
  waiting for transfers between devices  3.27 us (3%)
    all_to_all x1, blocking collectives, per_device(): got2 = lax.all_to_all(second, 'cls', 0, 0)  22.8 us
    pallas_call x1, Pallas kernels, per_device(): pl.pallas_call(forward_kernel, grid=(steps,), out_shape=(shape((SUB, loca...  22.3 us
    all_to_all x1, blocking collectives, per_device(): got1 = lax.all_to_all(payload, 'dp', 0, 0)  22.1 us
    all_to_all x1, blocking collectives, per_device(): got3 = lax.all_to_all(rows, 'cls', 0, 0, axis_index_groups=groups)  12 us
    pallas_call x1, Pallas kernels, per_device(): pl.pallas_call(backward_kernel, grid=(steps,), out_shape=(shape((n, E), b...  9.12 us
    all_to_all x1, starting transfers between devices, per_device(): got = lax.all_to_all(sent, 'dp', 0, 0)  6.27 us
    unnamed x10, local copies, waits for them, and re-layouts  5.45 us
    all_to_all x1, waiting for transfers between devices, per_device(): got = lax.all_to_all(sent, 'dp', 0, 0)  3.27 us
  transfers between devices with their start and end apart: 1, of which 1 were waited for; matrix products, arithmetic and copies ran while one was open for 0% of the time, Pallas kernels for 2%

profile of v4, /device:TPU:2, one launch (start us, length us, event | category | flops | bytes accessed | tf_op | source)
XLA Modules:
  0.0 111.1 jit_solution(492730990031545243)
XLA Ops:
  0.6 1.7 %shard_map.58 = bf16[16,80,256]{2,1,0:T(8,128)(2,1)} custom-call(s32[1]{0:T(128)} %bitcast.4.slot_ref, bf16[64,256]{1,0:T(8,128)(2,1)} %emb_ref.3, s32[1,64]{1,0:T(1,128)} %bitcast.7), custom_call_target="tpu_custom_call" | custom-call | tf_op jit(solution)/shard_map/pallas_call | solution.py:360
  2.4 6.3 %all-to-all-start = ((bf16[16,80,256]{2,1,0:T(8,128)(2,1)}), bf16[16,80,256]{2,1,0:T(8,128)(2,1)}, u32[]{:S(2)}, u32[]{:S(2)}) async-start(bf16[16,80,256]{2,1,0:T(8,128)(2,1)} %shard_map.58), calls=%async_computation | async-start | bytes 1310720 | tf_op jit(solution)/shard_map/all_to_all | solution.py:366
  8.6 0.0 copy-start
  8.7 1.9 %copy-done = bf16[3,2048,256]{2,1,0:T(8,128)(2,1)S(1)} copy-done((bf16[3,2048,256]{2,1,0:T(8,128)(2,1)S(1)}, bf16[3,2048,256]{2,1,0:T(8,128)(2,1)}, u32[]{:S(2)}) %copy-start) | copy-done | bytes 3145752
  10.5 2.4 %shard_map.60 = (bf16[4,1536,256]{2,1,0:T(8,128)(2,1)S(1)}, bf16[4,256,1536]{2,1,0:T(8,128)(2,1)S(1)}) custom-call(bf16[3,2048,256]{2,1,0:T(8,128)(2,1)S(1)} %copy-done), custom_call_target="tpu_custom_call" | custom-call | flops 1000000000 | bytes 10000000 | tf_op jit(solution)/shard_map/pallas_call | solution.py:370
  12.9 0.0 copy-start.2
  12.9 1.7 %copy-done.2 = bf16[4,256,1536]{2,1,0:T(8,128)(2,1)} copy-done((bf16[4,256,1536]{2,1,0:T(8,128)(2,1)}, bf16[4,256,1536]{2,1,0:T(8,128)(2,1)S(1)}, u32[]{:S(2)}) %copy-start.2) | copy-done | bytes 3145752
  14.6 0.1 pad_add_fusion.where_ref.first_ref
  14.6 3.3 %all-to-all-done.got_ref = bf16[16,80,256]{2,1,0:T(8,128)(2,1)} async-done(((bf16[16,80,256]{2,1,0:T(8,128)(2,1)}), bf16[16,80,256]{2,1,0:T(8,128)(2,1)}, u32[]{:S(2)}, u32[]{:S(2)}) %all-to-all-start) | async-done | bytes 655392 | tf_op jit(solution)/shard_map/all_to_all | solution.py:366
  17.9 1.3 %shard_map.59 = (bf16[256,1024]{1,0:T(8,128)(2,1)S(1)}, s32[1,1024]{1,0:T(1,128)S(1)}, s32[8,128]{1,0:T(8,128)S(1)}) custom-call(s32[4]{0:T(128)S(1)} %pad_add_fusion.where_ref.first_ref, bf16[16,80,256]{2,1,0:T(8,128)(2,1)} %all-to-all-done.got_ref), custom_call_target="tpu_custom_call" | custom-call | tf_op jit(solution)/shard_map/pallas_call | solution.py:379
  19.2 0.0 copy-start.3
  19.2 1.9 %copy-done.3 = bf16[4,256,1536]{2,1,0:T(8,128)(2,1)S(1)} copy-done((bf16[4,256,1536]{2,1,0:T(8,128)(2,1)S(1)}, bf16[4,256,1536]{2,1,0:T(8,128)(2,1)}, u32[]{:S(2)}) %copy-start.3) | copy-done | bytes 3145752
  21.1 22.3 %shard_map.61 = (bf16[3,2048,1024]{2,1,0:T(8,128)(2,1)S(1)}, bf16[16,144,256]{2,1,0:T(8,128)(2,1)S(1)}, f32[8,1024]{1,0:T(8,128)S(1)}, f32[8,1024]{1,0:T(8,128)S(1)}) custom-call(s32[4]{0:T(128)S(1)} %pad_add_fusion.where_ref.first_ref, s32[8,128]{1,0:T(8,128)S(1)} %get-tuple-element.18.flag_ref, bf16[4,1536,256]{2,1,0:T(8,128)(2,1)S(1)} %get-tuple-element.19.cb_ref, ...), custom_call_target="tpu_custom_call" | custom-call | tf_op jit(solution)/shard_map/pallas_call | solution.py:392
  43.4 0.0 copy-start.4
  43.4 0.0 copy-start.1
  43.4 22.1 %all_to_all.20.got_ref = bf16[16,144,256]{2,1,0:T(8,128)(2,1)S(1)} all-to-all(bf16[16,144,256]{2,1,0:T(8,128)(2,1)S(1)} %get-tuple-element.23), channel_id=1, replica_groups=mesh['dp'=16,'cls'=16] {'dp'}, dimensions={0} | all-to-all | bytes 2359296 | tf_op jit(solution)/shard_map/all_to_all | solution.py:417
  65.6 0.2 shard_map.62
  65.8 22.8 %all_to_all.21.got_ref = bf16[16,32,256]{2,1,0:T(8,128)(2,1)S(1)} all-to-all(bf16[16,32,256]{2,1,0:T(8,128)(2,1)S(1)} %shard_map.62), channel_id=1, replica_groups=mesh['dp'=16,'cls'=16] {'cls'}, dimensions={0} | all-to-all | bytes 524288 | tf_op jit(solution)/shard_map/all_to_all | solution.py:425
  88.6 0.0 copy-done.4
  88.6 1.4 %shard_map.63 = (f32[1,1]{1,0:T(1,128)}, bf16[256,1024]{1,0:T(8,128)(2,1)S(1)}, f32[8,1024]{1,0:T(8,128)S(1)}, bf16[8,8,256]{2,1,0:T(8,128)(2,1)S(1)}) custom-call(s32[4]{0:T(128)S(1)} %pad_add_fusion.where_ref.first_ref, bf16[16,32,256]{2,1,0:T(8,128)(2,1)S(1)} %all_to_all.21.got_ref, bf16[64,256]{1,0:T(8,128)(2,1)S(1)} %copy-done.4, ...), custom_call_target="tpu_custom_call" | custom-call | tf_op jit(solution)/shard_map/pallas_call | solution.py:426
  89.9 12.0 %all_to_all.22.got_ref = bf16[8,8,256]{2,1,0:T(8,128)(2,1)S(1)} all-to-all(bf16[8,8,256]{2,1,0:T(8,128)(2,1)S(1)} %get-tuple-element.29), channel_id=1, replica_groups={{0,1,2,3,4,5,6,7},{8,9,10,11,12,13,14,15},{16,17,18,19,20,21,22,23},{24..., dimensions={0} | all-to-all | bytes 65536 | tf_op jit(solution)/shard_map/all_to_all | solution.py:439
  102.0 0.0 copy-done.1
  102.0 9.1 %shard_map.64 = (bf16[64,256]{1,0:T(8,128)(2,1)}, bf16[3,2048,256]{2,1,0:T(8,128)(2,1)}) custom-call(s32[4]{0:T(128)S(1)} %pad_add_fusion.where_ref.first_ref, s32[8,128]{1,0:T(8,128)S(1)} %get-tuple-element.18.flag_ref, f32[8,1024]{1,0:T(8,128)S(1)} %get-tuple-element.27.fac_ref, bf16[256,1024]{1,0:T(8,128)(2,1)S(1)} %get-tuple-element.28.ust_ref, ...), custom_call_target="tpu_custom_call" | custom-call | tf_op jit(solution)/shard_map/pallas_call | solution.py:440
Async XLA Ops:
  2.4 15.5 %all-to-all-start = ((bf16[16,80,256]{2,1,0:T(8,128)(2,1)}), bf16[16,80,256]{2,1,0:T(8,128)(2,1)}, u32[]{:S(2)}, u32[]{:S(2)}) async-start(bf16[16,80,256]{2,1,0:T(8,128)(2,1)} %shard_map.58), calls=%async_computation | async-start | bytes 1310720 | tf_op jit(solution)/shard_map/all_to_all | solution.py:366
  8.6 1.9 %copy-start = (bf16[3,2048,256]{2,1,0:T(8,128)(2,1)S(1)}, bf16[3,2048,256]{2,1,0:T(8,128)(2,1)}, u32[]{:S(2)}) copy-start(bf16[3,2048,256]{2,1,0:T(8,128)(2,1)} %cent_ref.3) | copy-start | bytes 9437188
  12.9 1.7 %copy-start.2 = (bf16[4,256,1536]{2,1,0:T(8,128)(2,1)}, bf16[4,256,1536]{2,1,0:T(8,128)(2,1)S(1)}, u32[]{:S(2)}) copy-start(bf16[4,256,1536]{2,1,0:T(8,128)(2,1)S(1)} %get-tuple-element.20.cbt_ref) | copy-start | bytes 9437188
  19.2 1.9 %copy-start.3 = (bf16[4,256,1536]{2,1,0:T(8,128)(2,1)S(1)}, bf16[4,256,1536]{2,1,0:T(8,128)(2,1)}, u32[]{:S(2)}) copy-start(bf16[4,256,1536]{2,1,0:T(8,128)(2,1)} %copy-done.2) | copy-start | bytes 9437188
  43.4 45.2 %copy-start.4 = (bf16[64,256]{1,0:T(8,128)(2,1)S(1)}, bf16[64,256]{1,0:T(8,128)(2,1)}, u32[]{:S(2)}) copy-start(bf16[64,256]{1,0:T(8,128)(2,1)} %emb_ref.3) | copy-start | bytes 98308
  43.4 58.6 %copy-start.1 = (bf16[3,2048,256]{2,1,0:T(8,128)(2,1)S(1)}, bf16[3,2048,256]{2,1,0:T(8,128)(2,1)}, u32[]{:S(2)}) copy-start(bf16[3,2048,256]{2,1,0:T(8,128)(2,1)} %cent_ref.3) | copy-start | bytes 9437188

commit v5 on v4

--- a/solution.py
+++ b/solution.py
@@ -25,10 +25,15 @@
 TC = 512
 BB = 256
 FT = 256
+FC = 64
+FB = 128
 RC = 16
 AWAY = -1e4
 EXTRA = 16
 GROUP = 8
+
+DIM0 = (((0,), (0,)), ((), ()))
+DIM1 = (((1,), (1,)), ((), ()))
 
 f32 = jnp.float32
 bf16 = jnp.bfloat16
@@ -64,12 +69,11 @@
         out_ref[j, pl.ds(n, 16), :] = digit
 
 
-def centre_kernel(cent_ref, cb_ref, cbt_ref):
+def centre_kernel(cent_ref, cb_ref):
     for k in range(SUB):
         rows = cent_ref[k].astype(f32)
         unit = rows * inv_norm(rows)
         cb_ref[0, pl.ds(k * TC, TC), :] = unit.astype(bf16)
-        cbt_ref[0, :, pl.ds(k * TC, TC)] = unit.T.astype(bf16)
 
 
 def gather_kernel(rows_own, where_ref, got_ref, ut_ref, lab_ref, flag_ref):
@@ -85,16 +89,20 @@
             [got_ref[q * per + j, pl.ds(0, rows_own), :].astype(f32) for j in range(per)], axis=0
         )
         ut_ref[:, pl.ds(q * E, E)] = block.T.astype(bf16)
-    tiles, width = flag_ref.shape
+    words, width = flag_ref.shape
     batch = lab_ref.shape[1]
-    tile = (lab_ref[...] - where_ref[0]) >> (FT.bit_length() - 1)
-    hits = (lax.broadcasted_iota(jnp.int32, (tiles, batch), 0) == tile).astype(f32)
-    lane = lax.broadcasted_iota(jnp.int32, (tiles, width), 1)
-    flags = jnp.zeros((tiles, width), f32)
-    for b in range(batch // BB):
-        count = jnp.sum(hits[:, b * BB : (b + 1) * BB], axis=1, keepdims=True)
-        flags = jnp.where(lane == b, count, flags)
-    flag_ref[...] = flags.astype(jnp.int32)
+    tile = (lab_ref[...] - where_ref[0]) >> (FC.bit_length() - 1)
+    lane = lax.broadcasted_iota(jnp.int32, (words, width), 1)
+    row = lax.broadcasted_iota(jnp.int32, (words, batch), 0) * (FT // FC)
+    flags = jnp.zeros((words, width), jnp.int32)
+    for i in range(FT // FC):
+        hits = (row + i == tile).astype(f32)
+        for b in range(batch // FB):
+            some = jnp.sum(hits[:, b * FB : (b + 1) * FB], axis=1, keepdims=True) > 0
+            j = b % (BB // FB)
+            bit = jnp.where(some, 1 << (i * (BB // FB) + j), 0)
+            flags += jnp.where(lane == b // (BB // FB), bit, 0)
+    flag_ref[...] = flags
 
 
 def elementwise(c0, c1, c2):
@@ -110,7 +118,7 @@
 
 
 def forward_kernel(
-    first_ref, flag_ref, cb_ref, cbt_ref, ut_ref, lab_ref,
+    first_ref, flag_ref, cb_ref, ut_ref, lab_ref,
     pt_ref, out_ref, target, own_ref, xs, sums, g1, g2,
 ):
     step = pl.program_id(0)
@@ -132,27 +140,41 @@
         cols = pl.ds(b * BB, BB)
         xs[b % 2] = jnp.dot(cb_ref[0], ut_ref[:, cols], preferred_element_type=f32)
 
-    def set_labels_apart(b, h):
-        cols = pl.ds(b * BB, BB)
-        row = lax.broadcasted_iota(jnp.int32, (FT, BB), 0) + h * FT
-        hit = row == lab_ref[:, cols] - first
-        known = jnp.sum(jnp.where(hit, 1.0, 0.0), axis=0, keepdims=True) > 0
-        x = []
-        for k in range(SUB):
-            rows = pl.ds(k * TC + h * FT, FT)
-            v = xs[b % 2, rows, :]
-            x.append(jnp.sum(jnp.where(hit, v, 0.0), axis=0, keepdims=True))
-            xs[b % 2, rows, :] = jnp.where(hit, AWAY, v)
-        e1, e2, d1, d2, r, power, shift = elementwise(*x)
-        power = power - MARGIN2
-        target[0:1, cols] += jnp.where(known, power, 0.0)
-        sums[0:1, cols] += jnp.where(known, jnp.exp2(power), 0.0)
-        p = (r * shift, (r * e1) * (d1 + shift), (r * e2) * (d2 + shift))
-        for k in range(SUB):
-            own_ref[k : k + 1, cols] += jnp.where(known, p[k], 0.0)
-            own = jnp.where(hit, p[k], 0.0).astype(bf16)
-            cbt = cbt_ref[0, :, pl.ds(k * TC + h * FT, FT)]
-            g2[:, cols] += jnp.dot(cbt, own, preferred_element_type=f32)
+    def set_labels_apart(b, h, word):
+        per = BB // FB
+
+        def piece(i, carry):
+            @pl.when(((word >> i) & 1) > 0)
+            def _():
+                down = pl.multiple_of((i // per) * FC, FC) + h * FT
+                over = pl.multiple_of((i % per) * FB, FB)
+                here = pl.ds(over, FB)
+                cols = pl.ds(pl.multiple_of(over + b * BB, FB), FB)
+                row = lax.broadcasted_iota(jnp.int32, (FC, FB), 0) + down
+                hit = row == lab_ref[:, cols] - first
+                known = jnp.sum(jnp.where(hit, 1.0, 0.0), axis=0, keepdims=True) > 0
+                x = []
+                for k in range(SUB):
+                    rows = pl.ds(pl.multiple_of(down + k * TC, FC), FC)
+                    v = xs[b % 2, rows, here]
+                    x.append(jnp.sum(jnp.where(hit, v, 0.0), axis=0, keepdims=True))
+                    xs[b % 2, rows, here] = jnp.where(hit, AWAY, v)
+                e1, e2, d1, d2, r, power, shift = elementwise(*x)
+                power = power - MARGIN2
+                target[0:1, cols] += jnp.where(known, power, 0.0)
+                sums[0:1, cols] += jnp.where(known, jnp.exp2(power), 0.0)
+                p = (r * shift, (r * e1) * (d1 + shift), (r * e2) * (d2 + shift))
+                add = jnp.zeros((FB, E), f32)
+                for k in range(SUB):
+                    own_ref[k : k + 1, cols] += jnp.where(known, p[k], 0.0)
+                    own = jnp.where(hit, p[k], 0.0).astype(bf16)
+                    cb = cb_ref[0, pl.ds(pl.multiple_of(down + k * TC, FC), FC), :]
+                    add += lax.dot_general(own, cb, DIM0, preferred_element_type=f32)
+                g2[cols, :] += add
+
+            return carry
+
+        lax.fori_loop(0, (FT // FC) * per, piece, 0)
 
     def terms(b):
         cols = pl.ds(b * BB, BB)
@@ -171,14 +193,13 @@
     def rows_sum(b):
         cols = pl.ds(b * BB, BB)
         p = jnp.concatenate([pt_ref[k, pl.ds(base, TC), cols] for k in range(SUB)], axis=0)
-        g1[:, cols] += jnp.dot(cbt_ref[0], p, preferred_element_type=f32)
+        g1[:, cols] += lax.dot_general(cb_ref[0], p, DIM0, preferred_element_type=f32)
 
     block(0)
     for b in range(batch // BB):
         for h in range(TC // FT):
-            pl.when(flag_ref[step * (TC // FT) + h, b] > 0)(
-                functools.partial(set_labels_apart, b, h)
-            )
+            word = flag_ref[step * (TC // FT) + h, b]
+            pl.when(word > 0)(functools.partial(set_labels_apart, b, h, word))
         if (b + 1) * BB < batch:
             block(b + 1)
         terms(b)
@@ -197,7 +218,7 @@
         for q in range(blocks):
             cols = slice(q * E, (q + 1) * E)
             a = g1[:, cols].T.astype(bf16)
-            o = g2[:, cols].T.astype(bf16)
+            o = g2[q * E : (q + 1) * E, :].astype(bf16)
             extra = pack_extra(totals, tgt[:, cols], all_targets).astype(bf16)
             for j in range(per):
                 out_ref[q * per + j, pl.ds(0, n), :] = a[j * n : (j + 1) * n]
@@ -279,61 +300,58 @@
 
 
 def backward_kernel(
-    first_ref, flag_ref, fac_ref, ust_ref, lab_ref, got_ref, cent_ref, pt_ref, ge_ref, gc_ref, gs
+    first_ref, flag_ref, fac_ref, ust_ref, lab_ref, got_ref, cent_ref, pt_ref, ge_ref, gc_ref
 ):
     step = pl.program_id(0)
     batch = ust_ref.shape[1]
     first = first_ref[0] + step * TC
     base = pl.multiple_of(step * TC, TC)
-    dims = (((1,), (1,)), ((), ()))
 
     @pl.when(step == 0)
     def _():
         parts = [got_ref[j].astype(f32) for j in range(got_ref.shape[0])]
         ge_ref[...] = jnp.concatenate(parts, axis=0).astype(bf16)
 
-    def product(k):
-        return lax.dot_general(
-            pt_ref[k, pl.ds(base, TC), :], ust_ref[...], dims, preferred_element_type=f32
-        )
-
-    def finish(k, g):
-        rows = cent_ref[k].astype(f32)
+    def finish(rows, g):
+        rows = rows.astype(f32)
         r = inv_norm(rows)
         unit = rows * r
         g = (g - unit * jnp.sum(unit * g, axis=1, keepdims=True)) * r
-        gc_ref[k] = g.astype(bf16)
-
-    def add_labels(b, h):
-        cols = pl.ds(b * BB, BB)
-        row = lax.broadcasted_iota(jnp.int32, (FT, BB), 0) + h * FT
-        hit = row == lab_ref[:, cols] - first
-        for k in range(SUB):
-            own = jnp.where(hit, fac_ref[k : k + 1, cols], 0.0).astype(bf16)
-            gs[k, pl.ds(h * FT, FT), :] += lax.dot_general(
-                own, ust_ref[:, cols], dims, preferred_element_type=f32
-            )
-
-    flags = [
-        (b, h, flag_ref[step * (TC // FT) + h, b])
-        for b in range(batch // BB)
-        for h in range(TC // FT)
-    ]
-    some = sum(f for _, _, f in flags) > 0
-
-    @pl.when(jnp.logical_not(some))
-    def _():
-        for k in range(SUB):
-            finish(k, product(k))
-
-    @pl.when(some)
-    def _():
-        for k in range(SUB):
-            gs[k] = product(k)
-        for b, h, flag in flags:
-            pl.when(flag > 0)(functools.partial(add_labels, b, h))
-        for k in range(SUB):
-            finish(k, gs[k])
+        return g.astype(bf16)
+
+    for k in range(SUB):
+        p = pt_ref[k, pl.ds(base, TC), :]
+        g = lax.dot_general(p, ust_ref[...], DIM1, preferred_element_type=f32)
+        gc_ref[k] = finish(cent_ref[k], g)
+
+    per = BB // FB
+    for h in range(TC // FT):
+        words = [flag_ref[step * (TC // FT) + h, b] for b in range(batch // BB)]
+        word = functools.reduce(lambda x, y: x | y, words)
+
+        def piece(i, carry, word=word, h=h):
+            @pl.when(((word >> (i * per)) & ((1 << per) - 1)) > 0)
+            def _():
+                down = pl.multiple_of(i * FC + h * FT, FC)
+                row = lax.broadcasted_iota(jnp.int32, (FC, batch), 0) + down
+                hit = row == lab_ref[...] - first
+                p = []
+                for k in range(SUB):
+                    v = pt_ref[k, pl.ds(pl.multiple_of(base + down, FC), FC), :].astype(f32)
+                    p.append(jnp.where(hit, fac_ref[k : k + 1, :], v).astype(bf16))
+                p = jnp.concatenate(p, axis=0)
+                g = lax.dot_general(p, ust_ref[...], DIM1, preferred_element_type=f32)
+                for k in range(SUB):
+                    rows = pl.ds(down, FC)
+                    gc_ref[k, rows, :] = finish(
+                        cent_ref[k, rows, :], g[k * FC : (k + 1) * FC]
+                    )
+
+            return carry
+
+        @pl.when(word > 0)
+        def _(piece=piece):
+            lax.fori_loop(0, FT // FC, piece, 0)
 
 
 def per_device(embeddings, labels, centres):
@@ -353,7 +371,6 @@
     where = jnp.stack([first, dp * n + at, slot + at, at]).astype(jnp.int32)
     smem = pl.BlockSpec(memory_space=pltpu.SMEM)
     vmem = pl.BlockSpec(memory_space=pltpu.VMEM)
-    whole = lambda shape: pl.BlockSpec(shape, lambda i: (0,) * len(shape))
     params = pltpu.CompilerParams(vmem_limit_bytes=24 * 1024 * 1024)
     shape = jax.ShapeDtypeStruct
 
@@ -366,13 +383,12 @@
     got = lax.all_to_all(sent, "dp", 0, 0)
     tile = pl.BlockSpec((SUB, TC, E), lambda i: (0, i, 0))
     rows_tile = pl.BlockSpec((1, SUB * TC, E), lambda i: (i, 0, 0))
-    cols_tile = pl.BlockSpec((1, E, SUB * TC), lambda i: (i, 0, 0))
-    cb, cbt = pl.pallas_call(
+    cb = pl.pallas_call(
         centre_kernel,
         grid=(steps,),
-        out_shape=(shape((steps, SUB * TC, E), bf16), shape((steps, E, SUB * TC), bf16)),
+        out_shape=shape((steps, SUB * TC, E), bf16),
         in_specs=[tile],
-        out_specs=(rows_tile, cols_tile),
+        out_specs=rows_tile,
         compiler_params=params,
         cost_estimate=pl.CostEstimate(flops=10**9, bytes_accessed=10**7, transcendentals=0),
     )(centres)
@@ -398,21 +414,16 @@
             shape((8, batch), f32),
             shape((8, batch), f32),
         ),
-        in_specs=[smem, smem, rows_tile, cols_tile, whole((E, batch)), whole((1, batch))],
-        out_specs=(
-            vmem,
-            whole((parts, height, E)),
-            whole((8, batch)),
-            whole((8, batch)),
-        ),
+        in_specs=[smem, smem, rows_tile, vmem, vmem],
+        out_specs=(vmem, vmem, vmem, vmem),
         scratch_shapes=[
             pltpu.VMEM((2, SUB * TC, BB), f32),
             pltpu.VMEM((8, batch), f32),
             pltpu.VMEM((E, batch), f32),
-            pltpu.VMEM((E, batch), f32),
+            pltpu.VMEM((batch, E), f32),
         ],
         compiler_params=params,
-    )(where, flags, cb, cbt, ut, all_labels)
+    )(where, flags, cb, ut, all_labels)
 
     got1 = lax.all_to_all(payload, "dp", 0, 0)
     second = pl.pallas_call(
@@ -444,15 +455,14 @@
         in_specs=[
             smem,
             smem,
-            whole((8, batch)),
-            whole((E, batch)),
-            whole((1, batch)),
-            whole((GROUP, m, E)),
+            vmem,
+            vmem,
+            vmem,
+            vmem,
             tile,
             vmem,
         ],
-        out_specs=(whole((n, E)), tile),
-        scratch_shapes=[pltpu.VMEM((SUB, TC, E), f32)],
+        out_specs=(vmem, tile),
         compiler_params=params,
     )(where, flags, fac, ust, all_labels, got3, centres, pt)
     return (loss.reshape(()), grad_embeddings, grad_centres)

time: 112 us -> 109 us (0.973)
  local copies, waits for them, and re-layouts: 5.45 us -> 1.9 us
  waiting for transfers between devices: 3.27 us -> 5.69 us
  Pallas kernels: 38.4 us -> 36.6 us
    unnamed x10 -> x6, local copies, waits for them, and re-layouts: 5.45 us -> 1.9 us
    all_to_all x1, waiting for transfers between devices: 3.27 us -> 5.69 us  [per_device(): got = lax.all_to_all(sent, 'dp', 0, 0)]
  transfers between devices with their start and end apart: 1 -> 1, of which waited for: 1 -> 1; matrix products, arithmetic and copies ran while one was open for 0% -> 0% of each run, Pallas kernels for 2% -> 1%
where the time goes in v5:
time: 109 us
  blocking collectives  57.6 us (53%)
  Pallas kernels  36.6 us (34%)
  starting transfers between devices  6.27 us (6%)
  waiting for transfers between devices  5.69 us (5%)
  local copies, waits for them, and re-layouts  1.9 us (2%)
    all_to_all x1, blocking collectives, per_device(): got2 = lax.all_to_all(second, 'cls', 0, 0)  23.5 us
    all_to_all x1, blocking collectives, per_device(): got1 = lax.all_to_all(payload, 'dp', 0, 0)  22.1 us
    pallas_call x1, Pallas kernels, per_device(): pl.pallas_call(forward_kernel, grid=(steps,), out_shape=(shape((SUB, loca...  21.7 us
    all_to_all x1, blocking collectives, per_device(): got3 = lax.all_to_all(rows, 'cls', 0, 0, axis_index_groups=groups)  12 us
    pallas_call x1, Pallas kernels, per_device(): pl.pallas_call(backward_kernel, grid=(steps,), out_shape=(shape((n, E), b...  8.61 us
    all_to_all x1, starting transfers between devices, per_device(): got = lax.all_to_all(sent, 'dp', 0, 0)  6.27 us
    all_to_all x1, waiting for transfers between devices, per_device(): got = lax.all_to_all(sent, 'dp', 0, 0)  5.69 us
  transfers between devices with their start and end apart: 1, of which 1 were waited for; matrix products, arithmetic and copies ran while one was open for 0% of the time, Pallas kernels for 1%

profile of v5, /device:TPU:2, one launch (start us, length us, event | category | flops | bytes accessed | tf_op | source)
XLA Modules:
  0.0 108.8 jit_solution(358849568880612185)
XLA Ops:
  0.6 1.7 %shard_map.58 = bf16[16,80,256]{2,1,0:T(8,128)(2,1)} custom-call(s32[1]{0:T(128)} %bitcast.4.slot_ref, bf16[64,256]{1,0:T(8,128)(2,1)} %emb_ref.3, s32[1,64]{1,0:T(1,128)} %bitcast.7), custom_call_target="tpu_custom_call" | custom-call | tf_op jit(solution)/shard_map/pallas_call | solution.py:377
  2.4 6.3 %all-to-all-start = ((bf16[16,80,256]{2,1,0:T(8,128)(2,1)}), bf16[16,80,256]{2,1,0:T(8,128)(2,1)}, u32[]{:S(2)}, u32[]{:S(2)}) async-start(bf16[16,80,256]{2,1,0:T(8,128)(2,1)} %shard_map.58), calls=%async_computation | async-start | bytes 1310720 | tf_op jit(solution)/shard_map/all_to_all | solution.py:383
  8.6 0.0 copy-start
  8.6 1.9 %copy-done = bf16[3,2048,256]{2,1,0:T(8,128)(2,1)S(1)} copy-done((bf16[3,2048,256]{2,1,0:T(8,128)(2,1)S(1)}, bf16[3,2048,256]{2,1,0:T(8,128)(2,1)}, u32[]{:S(2)}) %copy-start) | copy-done | bytes 3145752
  10.5 1.6 %shard_map.60.cb_ref = bf16[4,1536,256]{2,1,0:T(8,128)(2,1)S(1)} custom-call(bf16[3,2048,256]{2,1,0:T(8,128)(2,1)S(1)} %copy-done), custom_call_target="tpu_custom_call" | custom-call | flops 1000000000 | bytes 10000000 | tf_op jit(solution)/shard_map/pallas_call | solution.py:386
  12.1 0.1 pad_add_fusion.where_ref.first_ref
  12.2 5.7 %all-to-all-done.got_ref = bf16[16,80,256]{2,1,0:T(8,128)(2,1)} async-done(((bf16[16,80,256]{2,1,0:T(8,128)(2,1)}), bf16[16,80,256]{2,1,0:T(8,128)(2,1)}, u32[]{:S(2)}, u32[]{:S(2)}) %all-to-all-start) | async-done | bytes 655392 | tf_op jit(solution)/shard_map/all_to_all | solution.py:383
  17.9 1.4 %shard_map.59 = (bf16[256,1024]{1,0:T(8,128)(2,1)S(1)}, s32[1,1024]{1,0:T(1,128)S(1)}, s32[8,128]{1,0:T(8,128)S(1)}) custom-call(s32[4]{0:T(128)S(1)} %pad_add_fusion.where_ref.first_ref, bf16[16,80,256]{2,1,0:T(8,128)(2,1)} %all-to-all-done.got_ref), custom_call_target="tpu_custom_call" | custom-call | tf_op jit(solution)/shard_map/pallas_call | solution.py:395
  19.3 0.0 copy-start.2
  19.3 21.7 %shard_map.61 = (bf16[3,2048,1024]{2,1,0:T(8,128)(2,1)S(1)}, bf16[16,144,256]{2,1,0:T(8,128)(2,1)S(1)}, f32[8,1024]{1,0:T(8,128)S(1)}, f32[8,1024]{1,0:T(8,128)S(1)}) custom-call(s32[4]{0:T(128)S(1)} %pad_add_fusion.where_ref.first_ref, s32[8,128]{1,0:T(8,128)S(1)} %get-tuple-element.16.flag_ref, bf16[4,1536,256]{2,1,0:T(8,128)(2,1)S(1)} %shard_map.60.cb_ref, ...), custom_call_target="tpu_custom_call" | custom-call | tf_op jit(solution)/shard_map/pallas_call | solution.py:408
  41.0 0.0 copy-start.1
  41.0 22.1 %all_to_all.20.got_ref = bf16[16,144,256]{2,1,0:T(8,128)(2,1)S(1)} all-to-all(bf16[16,144,256]{2,1,0:T(8,128)(2,1)S(1)} %get-tuple-element.19), channel_id=1, replica_groups=mesh['dp'=16,'cls'=16] {'dp'}, dimensions={0} | all-to-all | bytes 2359296 | tf_op jit(solution)/shard_map/all_to_all | solution.py:428
  63.0 0.2 shard_map.62
  63.3 23.5 %all_to_all.21.got_ref = bf16[16,32,256]{2,1,0:T(8,128)(2,1)S(1)} all-to-all(bf16[16,32,256]{2,1,0:T(8,128)(2,1)S(1)} %shard_map.62), channel_id=1, replica_groups=mesh['dp'=16,'cls'=16] {'cls'}, dimensions={0} | all-to-all | bytes 524288 | tf_op jit(solution)/shard_map/all_to_all | solution.py:436
  86.8 0.0 copy-done.2
  86.8 1.4 %shard_map.63 = (f32[1,1]{1,0:T(1,128)}, bf16[256,1024]{1,0:T(8,128)(2,1)S(1)}, f32[8,1024]{1,0:T(8,128)S(1)}, bf16[8,8,256]{2,1,0:T(8,128)(2,1)S(1)}) custom-call(s32[4]{0:T(128)S(1)} %pad_add_fusion.where_ref.first_ref, bf16[16,32,256]{2,1,0:T(8,128)(2,1)S(1)} %all_to_all.21.got_ref, bf16[64,256]{1,0:T(8,128)(2,1)S(1)} %copy-done.2, ...), custom_call_target="tpu_custom_call" | custom-call | tf_op jit(solution)/shard_map/pallas_call | solution.py:437
  88.2 12.0 %all_to_all.22.got_ref = bf16[8,8,256]{2,1,0:T(8,128)(2,1)S(1)} all-to-all(bf16[8,8,256]{2,1,0:T(8,128)(2,1)S(1)} %get-tuple-element.25), channel_id=1, replica_groups={{0,1,2,3,4,5,6,7},{8,9,10,11,12,13,14,15},{16,17,18,19,20,21,22,23},{24..., dimensions={0} | all-to-all | bytes 65536 | tf_op jit(solution)/shard_map/all_to_all | solution.py:450
  100.2 0.0 copy-done.1
  100.2 8.6 %shard_map.64 = (bf16[64,256]{1,0:T(8,128)(2,1)}, bf16[3,2048,256]{2,1,0:T(8,128)(2,1)}) custom-call(s32[4]{0:T(128)S(1)} %pad_add_fusion.where_ref.first_ref, s32[8,128]{1,0:T(8,128)S(1)} %get-tuple-element.16.flag_ref, f32[8,1024]{1,0:T(8,128)S(1)} %get-tuple-element.23.fac_ref, bf16[256,1024]{1,0:T(8,128)(2,1)S(1)} %get-tuple-element.24.ust_ref, ...), custom_call_target="tpu_custom_call" | custom-call | tf_op jit(solution)/shard_map/pallas_call | solution.py:451
Async XLA Ops:
  2.4 15.5 %all-to-all-start = ((bf16[16,80,256]{2,1,0:T(8,128)(2,1)}), bf16[16,80,256]{2,1,0:T(8,128)(2,1)}, u32[]{:S(2)}, u32[]{:S(2)}) async-start(bf16[16,80,256]{2,1,0:T(8,128)(2,1)} %shard_map.58), calls=%async_computation | async-start | bytes 1310720 | tf_op jit(solution)/shard_map/all_to_all | solution.py:383
  8.6 1.9 %copy-start = (bf16[3,2048,256]{2,1,0:T(8,128)(2,1)S(1)}, bf16[3,2048,256]{2,1,0:T(8,128)(2,1)}, u32[]{:S(2)}) copy-start(bf16[3,2048,256]{2,1,0:T(8,128)(2,1)} %cent_ref.3) | copy-start | bytes 9437188
  19.3 67.6 %copy-start.2 = (bf16[64,256]{1,0:T(8,128)(2,1)S(1)}, bf16[64,256]{1,0:T(8,128)(2,1)}, u32[]{:S(2)}) copy-start(bf16[64,256]{1,0:T(8,128)(2,1)} %emb_ref.3) | copy-start | bytes 98308
  41.0 59.3 %copy-start.1 = (bf16[3,2048,256]{2,1,0:T(8,128)(2,1)S(1)}, bf16[3,2048,256]{2,1,0:T(8,128)(2,1)}, u32[]{:S(2)}) copy-start(bf16[3,2048,256]{2,1,0:T(8,128)(2,1)} %cent_ref.3) | copy-start | bytes 9437188

commit v6 on v5

--- a/solution.py
+++ b/solution.py
@@ -118,7 +118,7 @@
 
 
 def forward_kernel(
-    first_ref, flag_ref, cb_ref, ut_ref, lab_ref,
+    first_ref, flag_ref, cb_ref, next_ref, ut_ref, lab_ref,
     pt_ref, out_ref, target, own_ref, xs, sums, g1, g2,
 ):
     step = pl.program_id(0)
@@ -134,11 +134,11 @@
         g2[...] = jnp.zeros_like(g2)
 
     first = first_ref[0] + step * TC
-    base = pl.multiple_of(step * TC, TC)
-
-    def block(b):
+    tile_ref = pt_ref.at[step]
+
+    def block(ref, b):
         cols = pl.ds(b * BB, BB)
-        xs[b % 2] = jnp.dot(cb_ref[0], ut_ref[:, cols], preferred_element_type=f32)
+        xs[b] = jnp.dot(ref[0], ut_ref[:, cols], preferred_element_type=f32)
 
     def set_labels_apart(b, h, word):
         per = BB // FB
@@ -156,9 +156,9 @@
                 x = []
                 for k in range(SUB):
                     rows = pl.ds(pl.multiple_of(down + k * TC, FC), FC)
-                    v = xs[b % 2, rows, here]
+                    v = xs[b, rows, here]
                     x.append(jnp.sum(jnp.where(hit, v, 0.0), axis=0, keepdims=True))
-                    xs[b % 2, rows, here] = jnp.where(hit, AWAY, v)
+                    xs[b, rows, here] = jnp.where(hit, AWAY, v)
                 e1, e2, d1, d2, r, power, shift = elementwise(*x)
                 power = power - MARGIN2
                 target[0:1, cols] += jnp.where(known, power, 0.0)
@@ -180,29 +180,40 @@
         cols = pl.ds(b * BB, BB)
         total = jnp.zeros((8, BB), f32)
         for c in range(TC // RC):
-            x = [xs[b % 2, pl.ds(k * TC + c * RC, RC), :] for k in range(SUB)]
+            x = [xs[b, pl.ds(k * TC + c * RC, RC), :] for k in range(SUB)]
             e1, e2, d1, d2, r, power, shift = elementwise(*x)
             ex = jnp.exp2(power)
             total += ex[0:8] + ex[8:16]
             g = ex * r
             p = (g * shift, (g * e1) * (d1 + shift), (g * e2) * (d2 + shift))
             for k in range(SUB):
-                pt_ref[k, pl.ds(base + c * RC, RC), cols] = p[k].astype(bf16)
+                tile_ref[k, pl.ds(c * RC, RC), cols] = p[k].astype(bf16)
         sums[:, cols] += total
 
     def rows_sum(b):
         cols = pl.ds(b * BB, BB)
-        p = jnp.concatenate([pt_ref[k, pl.ds(base, TC), cols] for k in range(SUB)], axis=0)
+        p = jnp.concatenate([tile_ref[k, :, cols] for k in range(SUB)], axis=0)
         g1[:, cols] += lax.dot_general(cb_ref[0], p, DIM0, preferred_element_type=f32)
 
-    block(0)
+    @pl.when(step == 0)
+    def _():
+        for b in range(batch // BB):
+            block(cb_ref, b)
+
+    words = [
+        (b, h, flag_ref[step * (TC // FT) + h, b])
+        for b in range(batch // BB)
+        for h in range(TC // FT)
+    ]
+
+    @pl.when(functools.reduce(lambda x, y: x | y, [w for _, _, w in words]) > 0)
+    def _():
+        for b, h, word in words:
+            pl.when(word > 0)(functools.partial(set_labels_apart, b, h, word))
+
     for b in range(batch // BB):
-        for h in range(TC // FT):
-            word = flag_ref[step * (TC // FT) + h, b]
-            pl.when(word > 0)(functools.partial(set_labels_apart, b, h, word))
-        if (b + 1) * BB < batch:
-            block(b + 1)
         terms(b)
+        block(next_ref, b)
         rows_sum(b)
 
     @pl.when(step == steps - 1)
@@ -305,7 +316,6 @@
     step = pl.program_id(0)
     batch = ust_ref.shape[1]
     first = first_ref[0] + step * TC
-    base = pl.multiple_of(step * TC, TC)
 
     @pl.when(step == 0)
     def _():
@@ -320,7 +330,7 @@
         return g.astype(bf16)
 
     for k in range(SUB):
-        p = pt_ref[k, pl.ds(base, TC), :]
+        p = pt_ref[step, k]
         g = lax.dot_general(p, ust_ref[...], DIM1, preferred_element_type=f32)
         gc_ref[k] = finish(cent_ref[k], g)
 
@@ -337,7 +347,7 @@
                 hit = row == lab_ref[...] - first
                 p = []
                 for k in range(SUB):
-                    v = pt_ref[k, pl.ds(pl.multiple_of(base + down, FC), FC), :].astype(f32)
+                    v = pt_ref[step, k, pl.ds(down, FC), :].astype(f32)
                     p.append(jnp.where(hit, fac_ref[k : k + 1, :], v).astype(bf16))
                 p = jnp.concatenate(p, axis=0)
                 g = lax.dot_general(p, ust_ref[...], DIM1, preferred_element_type=f32)
@@ -383,6 +393,7 @@
     got = lax.all_to_all(sent, "dp", 0, 0)
     tile = pl.BlockSpec((SUB, TC, E), lambda i: (0, i, 0))
     rows_tile = pl.BlockSpec((1, SUB * TC, E), lambda i: (i, 0, 0))
+    next_tile = pl.BlockSpec((1, SUB * TC, E), lambda i: (jnp.minimum(i + 1, steps - 1), 0, 0))
     cb = pl.pallas_call(
         centre_kernel,
         grid=(steps,),
@@ -409,21 +420,21 @@
         forward_kernel,
         grid=(steps,),
         out_shape=(
-            shape((SUB, local, batch), bf16),
+            shape((steps, SUB, TC, batch), bf16),
             shape((parts, height, E), bf16),
             shape((8, batch), f32),
             shape((8, batch), f32),
         ),
-        in_specs=[smem, smem, rows_tile, vmem, vmem],
+        in_specs=[smem, smem, rows_tile, next_tile, vmem, vmem],
         out_specs=(vmem, vmem, vmem, vmem),
         scratch_shapes=[
-            pltpu.VMEM((2, SUB * TC, BB), f32),
+            pltpu.VMEM((batch // BB, SUB * TC, BB), f32),
             pltpu.VMEM((8, batch), f32),
             pltpu.VMEM((E, batch), f32),
             pltpu.VMEM((batch, E), f32),
         ],
         compiler_params=params,
-    )(where, flags, cb, ut, all_labels)
+    )(where, flags, cb, cb, ut, all_labels)
 
     got1 = lax.all_to_all(payload, "dp", 0, 0)
     second = pl.pallas_call(

time: 109 us -> 106 us (0.972)
  Pallas kernels: 36.6 us -> 34.6 us
  blocking collectives: 57.6 us -> 56.3 us
    pallas_call x1, Pallas kernels: 21.7 us -> 18.3 us  [per_device(): pl.pallas_call(forward_kernel, grid=(steps,), out_shape=(shape((steps, SU...]
    all_to_all x1, blocking collectives: 23.5 us -> 22.1 us  [per_device(): got2 = lax.all_to_all(second, 'cls', 0, 0)]
    pallas_call x1, Pallas kernels: 8.61 us -> 9.99 us  [per_device(): pl.pallas_call(backward_kernel, grid=(steps,), out_shape=(shape((n, E), b...]
  transfers between devices with their start and end apart: 1 -> 1, of which waited for: 1 -> 1; matrix products, arithmetic and copies ran while one was open for 0% -> 0% of each run, Pallas kernels for 1% -> 2%
where the time goes in v6:
time: 106 us
  blocking collectives  56.3 us (53%)
  Pallas kernels  34.6 us (33%)
  starting transfers between devices  6.27 us (6%)
  waiting for transfers between devices  5.69 us (5%)
  local copies, waits for them, and re-layouts  1.9 us (2%)
    all_to_all x1, blocking collectives, per_device(): got1 = lax.all_to_all(payload, 'dp', 0, 0)  22.2 us
    all_to_all x1, blocking collectives, per_device(): got2 = lax.all_to_all(second, 'cls', 0, 0)  22.1 us
    pallas_call x1, Pallas kernels, per_device(): pl.pallas_call(forward_kernel, grid=(steps,), out_shape=(shape((steps, SU...  18.3 us
    all_to_all x1, blocking collectives, per_device(): got3 = lax.all_to_all(rows, 'cls', 0, 0, axis_index_groups=groups)  12 us
    pallas_call x1, Pallas kernels, per_device(): pl.pallas_call(backward_kernel, grid=(steps,), out_shape=(shape((n, E), b...  9.99 us
    all_to_all x1, starting transfers between devices, per_device(): got = lax.all_to_all(sent, 'dp', 0, 0)  6.27 us
    all_to_all x1, waiting for transfers between devices, per_device(): got = lax.all_to_all(sent, 'dp', 0, 0)  5.69 us
  transfers between devices with their start and end apart: 1, of which 1 were waited for; matrix products, arithmetic and copies ran while one was open for 0% of the time, Pallas kernels for 2%

profile of v6, /device:TPU:2, one launch (start us, length us, event | category | flops | bytes accessed | tf_op | source)
XLA Modules:
  0.0 105.6 jit_solution(10400435975395885836)
XLA Ops:
  0.6 1.7 %shard_map.58 = bf16[16,80,256]{2,1,0:T(8,128)(2,1)} custom-call(s32[1]{0:T(128)} %bitcast.4.slot_ref, bf16[64,256]{1,0:T(8,128)(2,1)} %emb_ref.3, s32[1,64]{1,0:T(1,128)} %bitcast.7), custom_call_target="tpu_custom_call" | custom-call | tf_op jit(solution)/shard_map/pallas_call | solution.py:387
  2.4 6.3 %all-to-all-start = ((bf16[16,80,256]{2,1,0:T(8,128)(2,1)}), bf16[16,80,256]{2,1,0:T(8,128)(2,1)}, u32[]{:S(2)}, u32[]{:S(2)}) async-start(bf16[16,80,256]{2,1,0:T(8,128)(2,1)} %shard_map.58), calls=%async_computation | async-start | bytes 1310720 | tf_op jit(solution)/shard_map/all_to_all | solution.py:393
  8.6 0.0 copy-start
  8.6 1.9 %copy-done = bf16[3,2048,256]{2,1,0:T(8,128)(2,1)S(1)} copy-done((bf16[3,2048,256]{2,1,0:T(8,128)(2,1)S(1)}, bf16[3,2048,256]{2,1,0:T(8,128)(2,1)}, u32[]{:S(2)}) %copy-start) | copy-done | bytes 3145752
  10.5 1.6 %shard_map.60.cb_ref.next_ref = bf16[4,1536,256]{2,1,0:T(8,128)(2,1)S(1)} custom-call(bf16[3,2048,256]{2,1,0:T(8,128)(2,1)S(1)} %copy-done), custom_call_target="tpu_custom_call" | custom-call | flops 1000000000 | bytes 10000000 | tf_op jit(solution)/shard_map/pallas_call | solution.py:397
  12.1 0.1 pad_add_fusion.where_ref.first_ref
  12.2 5.7 %all-to-all-done.got_ref = bf16[16,80,256]{2,1,0:T(8,128)(2,1)} async-done(((bf16[16,80,256]{2,1,0:T(8,128)(2,1)}), bf16[16,80,256]{2,1,0:T(8,128)(2,1)}, u32[]{:S(2)}, u32[]{:S(2)}) %all-to-all-start) | async-done | bytes 655392 | tf_op jit(solution)/shard_map/all_to_all | solution.py:393
  17.9 1.4 %shard_map.59 = (bf16[256,1024]{1,0:T(8,128)(2,1)S(1)}, s32[1,1024]{1,0:T(1,128)S(1)}, s32[8,128]{1,0:T(8,128)S(1)}) custom-call(s32[4]{0:T(128)S(1)} %pad_add_fusion.where_ref.first_ref, bf16[16,80,256]{2,1,0:T(8,128)(2,1)} %all-to-all-done.got_ref), custom_call_target="tpu_custom_call" | custom-call | tf_op jit(solution)/shard_map/pallas_call | solution.py:406
  19.3 18.3 %shard_map.61 = (bf16[4,3,512,1024]{3,2,1,0:T(8,128)(2,1)S(1)}, bf16[16,144,256]{2,1,0:T(8,128)(2,1)S(1)}, f32[8,1024]{1,0:T(8,128)S(1)}, f32[8,1024]{1,0:T(8,128)S(1)}) custom-call(s32[4]{0:T(128)S(1)} %pad_add_fusion.where_ref.first_ref, s32[8,128]{1,0:T(8,128)S(1)} %get-tuple-element.16.flag_ref, bf16[4,1536,256]{2,1,0:T(8,128)(2,1)S(1)} %shard_map.60.cb_ref.next_ref, ...), custom_call_target="tpu_custom_call" | custom-call | tf_op jit(solution)/shard_map/pallas_call | solution.py:419
  37.6 0.0 copy-start.2
  37.6 0.0 copy-start.1
  37.6 22.2 %all_to_all.20.got_ref = bf16[16,144,256]{2,1,0:T(8,128)(2,1)S(1)} all-to-all(bf16[16,144,256]{2,1,0:T(8,128)(2,1)S(1)} %get-tuple-element.19), channel_id=1, replica_groups=mesh['dp'=16,'cls'=16] {'dp'}, dimensions={0} | all-to-all | bytes 2359296 | tf_op jit(solution)/shard_map/all_to_all | solution.py:439
  59.9 0.2 shard_map.62
  60.1 22.1 %all_to_all.21.got_ref = bf16[16,32,256]{2,1,0:T(8,128)(2,1)S(1)} all-to-all(bf16[16,32,256]{2,1,0:T(8,128)(2,1)S(1)} %shard_map.62), channel_id=1, replica_groups=mesh['dp'=16,'cls'=16] {'cls'}, dimensions={0} | all-to-all | bytes 524288 | tf_op jit(solution)/shard_map/all_to_all | solution.py:447
  82.2 0.0 copy-done.2
  82.2 1.4 %shard_map.63 = (f32[1,1]{1,0:T(1,128)}, bf16[256,1024]{1,0:T(8,128)(2,1)S(1)}, f32[8,1024]{1,0:T(8,128)S(1)}, bf16[8,8,256]{2,1,0:T(8,128)(2,1)S(1)}) custom-call(s32[4]{0:T(128)S(1)} %pad_add_fusion.where_ref.first_ref, bf16[16,32,256]{2,1,0:T(8,128)(2,1)S(1)} %all_to_all.21.got_ref, bf16[64,256]{1,0:T(8,128)(2,1)S(1)} %copy-done.2, ...), custom_call_target="tpu_custom_call" | custom-call | tf_op jit(solution)/shard_map/pallas_call | solution.py:448
  83.5 12.0 %all_to_all.22.got_ref = bf16[8,8,256]{2,1,0:T(8,128)(2,1)S(1)} all-to-all(bf16[8,8,256]{2,1,0:T(8,128)(2,1)S(1)} %get-tuple-element.25), channel_id=1, replica_groups={{0,1,2,3,4,5,6,7},{8,9,10,11,12,13,14,15},{16,17,18,19,20,21,22,23},{24..., dimensions={0} | all-to-all | bytes 65536 | tf_op jit(solution)/shard_map/all_to_all | solution.py:461
  95.6 0.0 copy-done.1
  95.6 10.0 %shard_map.64 = (bf16[64,256]{1,0:T(8,128)(2,1)}, bf16[3,2048,256]{2,1,0:T(8,128)(2,1)}) custom-call(s32[4]{0:T(128)S(1)} %pad_add_fusion.where_ref.first_ref, s32[8,128]{1,0:T(8,128)S(1)} %get-tuple-element.16.flag_ref, f32[8,1024]{1,0:T(8,128)S(1)} %get-tuple-element.23.fac_ref, bf16[256,1024]{1,0:T(8,128)(2,1)S(1)} %get-tuple-element.24.ust_ref, ...), custom_call_target="tpu_custom_call" | custom-call | tf_op jit(solution)/shard_map/pallas_call | solution.py:462
Async XLA Ops:
  2.4 15.5 %all-to-all-start = ((bf16[16,80,256]{2,1,0:T(8,128)(2,1)}), bf16[16,80,256]{2,1,0:T(8,128)(2,1)}, u32[]{:S(2)}, u32[]{:S(2)}) async-start(bf16[16,80,256]{2,1,0:T(8,128)(2,1)} %shard_map.58), calls=%async_computation | async-start | bytes 1310720 | tf_op jit(solution)/shard_map/all_to_all | solution.py:393
  8.6 1.9 %copy-start = (bf16[3,2048,256]{2,1,0:T(8,128)(2,1)S(1)}, bf16[3,2048,256]{2,1,0:T(8,128)(2,1)}, u32[]{:S(2)}) copy-start(bf16[3,2048,256]{2,1,0:T(8,128)(2,1)} %cent_ref.3) | copy-start | bytes 9437188
  37.6 44.6 %copy-start.2 = (bf16[64,256]{1,0:T(8,128)(2,1)S(1)}, bf16[64,256]{1,0:T(8,128)(2,1)}, u32[]{:S(2)}) copy-start(bf16[64,256]{1,0:T(8,128)(2,1)} %emb_ref.3) | copy-start | bytes 98308
  37.6 58.0 %copy-start.1 = (bf16[3,2048,256]{2,1,0:T(8,128)(2,1)S(1)}, bf16[3,2048,256]{2,1,0:T(8,128)(2,1)}, u32[]{:S(2)}) copy-start(bf16[3,2048,256]{2,1,0:T(8,128)(2,1)} %cent_ref.3) | copy-start | bytes 9437188

commit v7 on v6

--- a/solution.py
+++ b/solution.py
@@ -117,9 +117,35 @@
     return e1, e2, d1, d2, r, power, shift
 
 
+def piece_of(i, h):
+    per = BB // FB
+    down = pl.multiple_of((i // per) * FC, FC) + h * FT
+    return down, pl.multiple_of((i % per) * FB, FB)
+
+
+def for_labels(flag_ref, step, batch, do):
+    words = [
+        (b, h, flag_ref[step * (TC // FT) + h, b])
+        for b in range(batch // BB)
+        for h in range(TC // FT)
+    ]
+
+    def look(b, h, word):
+        def piece(i, carry):
+            pl.when(((word >> i) & 1) > 0)(functools.partial(do, b, h, i))
+            return carry
+
+        lax.fori_loop(0, (FT // FC) * (BB // FB), piece, 0)
+
+    @pl.when(functools.reduce(lambda x, y: x | y, [w for _, _, w in words]) > 0)
+    def _():
+        for b, h, word in words:
+            pl.when(word > 0)(functools.partial(look, b, h, word))
+
+
 def forward_kernel(
-    first_ref, flag_ref, cb_ref, next_ref, ut_ref, lab_ref,
-    pt_ref, out_ref, target, own_ref, xs, sums, g1, g2,
+    first_ref, flag_ref, cb_ref, ut_ref, lab_ref,
+    pt_ref, out_ref, target, own_ref, xs, sums, g1, g2, apart,
 ):
     step = pl.program_id(0)
     steps = pl.num_programs(0)
@@ -128,53 +154,42 @@
     @pl.when(step == 0)
     def _():
         sums[...] = jnp.zeros_like(sums)
-        target[...] = jnp.zeros_like(target)
-        own_ref[...] = jnp.zeros_like(own_ref)
+        apart[...] = jnp.zeros_like(apart)
         g1[...] = jnp.zeros_like(g1)
         g2[...] = jnp.zeros_like(g2)
 
     first = first_ref[0] + step * TC
     tile_ref = pt_ref.at[step]
 
-    def block(ref, b):
+    def block(at, b):
         cols = pl.ds(b * BB, BB)
-        xs[b] = jnp.dot(ref[0], ut_ref[:, cols], preferred_element_type=f32)
-
-    def set_labels_apart(b, h, word):
-        per = BB // FB
-
-        def piece(i, carry):
-            @pl.when(((word >> i) & 1) > 0)
-            def _():
-                down = pl.multiple_of((i // per) * FC, FC) + h * FT
-                over = pl.multiple_of((i % per) * FB, FB)
-                here = pl.ds(over, FB)
-                cols = pl.ds(pl.multiple_of(over + b * BB, FB), FB)
-                row = lax.broadcasted_iota(jnp.int32, (FC, FB), 0) + down
-                hit = row == lab_ref[:, cols] - first
-                known = jnp.sum(jnp.where(hit, 1.0, 0.0), axis=0, keepdims=True) > 0
-                x = []
-                for k in range(SUB):
-                    rows = pl.ds(pl.multiple_of(down + k * TC, FC), FC)
-                    v = xs[b, rows, here]
-                    x.append(jnp.sum(jnp.where(hit, v, 0.0), axis=0, keepdims=True))
-                    xs[b, rows, here] = jnp.where(hit, AWAY, v)
-                e1, e2, d1, d2, r, power, shift = elementwise(*x)
-                power = power - MARGIN2
-                target[0:1, cols] += jnp.where(known, power, 0.0)
-                sums[0:1, cols] += jnp.where(known, jnp.exp2(power), 0.0)
-                p = (r * shift, (r * e1) * (d1 + shift), (r * e2) * (d2 + shift))
-                add = jnp.zeros((FB, E), f32)
-                for k in range(SUB):
-                    own_ref[k : k + 1, cols] += jnp.where(known, p[k], 0.0)
-                    own = jnp.where(hit, p[k], 0.0).astype(bf16)
-                    cb = cb_ref[0, pl.ds(pl.multiple_of(down + k * TC, FC), FC), :]
-                    add += lax.dot_general(own, cb, DIM0, preferred_element_type=f32)
-                g2[cols, :] += add
-
-            return carry
-
-        lax.fori_loop(0, (FT // FC) * per, piece, 0)
+        xs[b] = jnp.dot(cb_ref[at], ut_ref[:, cols], preferred_element_type=f32)
+
+    def set_labels_apart(b, h, i):
+        down, over = piece_of(i, h)
+        here = pl.ds(over, FB)
+        cols = pl.ds(pl.multiple_of(over + b * BB, FB), FB)
+        row = lax.broadcasted_iota(jnp.int32, (FC, FB), 0) + down
+        hit = row == lab_ref[:, cols] - first
+        found = [jnp.sum(jnp.where(hit, 1.0, 0.0), axis=0, keepdims=True)]
+        for k in range(SUB):
+            rows = pl.ds(pl.multiple_of(down + k * TC, FC), FC)
+            v = xs[b, rows, here]
+            found.append(jnp.sum(jnp.where(hit, v, 0.0), axis=0, keepdims=True))
+            xs[b, rows, here] = jnp.where(hit, AWAY, v)
+        apart[0:4, cols] += jnp.concatenate(found, axis=0)
+
+    def label_rows(at, b, h, i):
+        down, over = piece_of(i, h)
+        cols = pl.ds(pl.multiple_of(over + b * BB, FB), FB)
+        row = lax.broadcasted_iota(jnp.int32, (FC, FB), 0) + (down + at * TC + first_ref[0])
+        hit = row == lab_ref[:, cols]
+        own, rows = [], []
+        for k in range(SUB):
+            own.append(jnp.where(hit, own_ref[k : k + 1, cols], 0.0).astype(bf16))
+            rows.append(cb_ref[at, pl.ds(pl.multiple_of(down + k * TC, FC), FC), :])
+        own, rows = jnp.concatenate(own, axis=0), jnp.concatenate(rows, axis=0)
+        g2[cols, :] += lax.dot_general(own, rows, DIM0, preferred_element_type=f32)
 
     def terms(b):
         cols = pl.ds(b * BB, BB)
@@ -193,28 +208,39 @@
     def rows_sum(b):
         cols = pl.ds(b * BB, BB)
         p = jnp.concatenate([tile_ref[k, :, cols] for k in range(SUB)], axis=0)
-        g1[:, cols] += lax.dot_general(cb_ref[0], p, DIM0, preferred_element_type=f32)
+        g1[:, cols] += lax.dot_general(cb_ref[step], p, DIM0, preferred_element_type=f32)
 
     @pl.when(step == 0)
     def _():
         for b in range(batch // BB):
-            block(cb_ref, b)
-
-    words = [
-        (b, h, flag_ref[step * (TC // FT) + h, b])
-        for b in range(batch // BB)
-        for h in range(TC // FT)
-    ]
-
-    @pl.when(functools.reduce(lambda x, y: x | y, [w for _, _, w in words]) > 0)
-    def _():
-        for b, h, word in words:
-            pl.when(word > 0)(functools.partial(set_labels_apart, b, h, word))
-
+            block(0, b)
+
+    for_labels(flag_ref, step, batch, set_labels_apart)
+    after = jnp.minimum(step + 1, steps - 1)
     for b in range(batch // BB):
         terms(b)
-        block(next_ref, b)
+        block(after, b)
         rows_sum(b)
+
+    @pl.when(step == steps - 1)
+    def _():
+        known = apart[0:1, :] > 0
+        e1, e2, d1, d2, r, power, shift = elementwise(*(apart[k + 1 : k + 2, :] for k in range(SUB)))
+        power = power - MARGIN2
+        p = (r * shift, (r * e1) * (d1 + shift), (r * e2) * (d2 + shift))
+        sums[0:1, :] += jnp.where(known, jnp.exp2(power), 0.0)
+        none = jnp.zeros((8, batch), f32)
+        target[...] = none
+        own_ref[...] = none
+        target[0:1, :] = jnp.where(known, power, 0.0)
+        for k in range(SUB):
+            own_ref[k : k + 1, :] = jnp.where(known, p[k], 0.0)
+
+        def one(at, carry):
+            for_labels(flag_ref, at, batch, functools.partial(label_rows, at))
+            return carry
+
+        lax.fori_loop(0, steps, one, 0)
 
     @pl.when(step == steps - 1)
     def _():
@@ -329,39 +355,20 @@
         g = (g - unit * jnp.sum(unit * g, axis=1, keepdims=True)) * r
         return g.astype(bf16)
 
+    def set_labels(b, h, i):
+        down, over = piece_of(i, h)
+        cols = pl.ds(pl.multiple_of(over + b * BB, FB), FB)
+        row = lax.broadcasted_iota(jnp.int32, (FC, FB), 0) + down
+        hit = row == lab_ref[:, cols] - first
+        for k in range(SUB):
+            v = pt_ref[step, k, pl.ds(down, FC), cols].astype(f32)
+            v = jnp.where(hit, fac_ref[k : k + 1, cols], v)
+            pt_ref[step, k, pl.ds(down, FC), cols] = v.astype(bf16)
+
+    for_labels(flag_ref, step, batch, set_labels)
     for k in range(SUB):
-        p = pt_ref[step, k]
-        g = lax.dot_general(p, ust_ref[...], DIM1, preferred_element_type=f32)
+        g = lax.dot_general(pt_ref[step, k], ust_ref[...], DIM1, preferred_element_type=f32)
         gc_ref[k] = finish(cent_ref[k], g)
-
-    per = BB // FB
-    for h in range(TC // FT):
-        words = [flag_ref[step * (TC // FT) + h, b] for b in range(batch // BB)]
-        word = functools.reduce(lambda x, y: x | y, words)
-
-        def piece(i, carry, word=word, h=h):
-            @pl.when(((word >> (i * per)) & ((1 << per) - 1)) > 0)
-            def _():
-                down = pl.multiple_of(i * FC + h * FT, FC)
-                row = lax.broadcasted_iota(jnp.int32, (FC, batch), 0) + down
-                hit = row == lab_ref[...] - first
-                p = []
-                for k in range(SUB):
-                    v = pt_ref[step, k, pl.ds(down, FC), :].astype(f32)
-                    p.append(jnp.where(hit, fac_ref[k : k + 1, :], v).astype(bf16))
-                p = jnp.concatenate(p, axis=0)
-                g = lax.dot_general(p, ust_ref[...], DIM1, preferred_element_type=f32)
-                for k in range(SUB):
-                    rows = pl.ds(down, FC)
-                    gc_ref[k, rows, :] = finish(
-                        cent_ref[k, rows, :], g[k * FC : (k + 1) * FC]
-                    )
-
-            return carry
-
-        @pl.when(word > 0)
-        def _(piece=piece):
-            lax.fori_loop(0, FT // FC, piece, 0)
 
 
 def per_device(embeddings, labels, centres):
@@ -381,7 +388,7 @@
     where = jnp.stack([first, dp * n + at, slot + at, at]).astype(jnp.int32)
     smem = pl.BlockSpec(memory_space=pltpu.SMEM)
     vmem = pl.BlockSpec(memory_space=pltpu.VMEM)
-    params = pltpu.CompilerParams(vmem_limit_bytes=24 * 1024 * 1024)
+    params = pltpu.CompilerParams(vmem_limit_bytes=30 * 1024 * 1024)
     shape = jax.ShapeDtypeStruct
 
     sent = pl.pallas_call(
@@ -393,7 +400,6 @@
     got = lax.all_to_all(sent, "dp", 0, 0)
     tile = pl.BlockSpec((SUB, TC, E), lambda i: (0, i, 0))
     rows_tile = pl.BlockSpec((1, SUB * TC, E), lambda i: (i, 0, 0))
-    next_tile = pl.BlockSpec((1, SUB * TC, E), lambda i: (jnp.minimum(i + 1, steps - 1), 0, 0))
     cb = pl.pallas_call(
         centre_kernel,
         grid=(steps,),
@@ -425,16 +431,17 @@
             shape((8, batch), f32),
             shape((8, batch), f32),
         ),
-        in_specs=[smem, smem, rows_tile, next_tile, vmem, vmem],
+        in_specs=[smem, smem, vmem, vmem, vmem],
         out_specs=(vmem, vmem, vmem, vmem),
         scratch_shapes=[
             pltpu.VMEM((batch // BB, SUB * TC, BB), f32),
             pltpu.VMEM((8, batch), f32),
             pltpu.VMEM((E, batch), f32),
             pltpu.VMEM((batch, E), f32),
+            pltpu.VMEM((8, batch), f32),
         ],
         compiler_params=params,
-    )(where, flags, cb, cb, ut, all_labels)
+    )(where, flags, cb, ut, all_labels)
 
     got1 = lax.all_to_all(payload, "dp", 0, 0)
     second = pl.pallas_call(

time: 106 us -> 104 us (0.981)
  Pallas kernels: 34.6 us -> 32.5 us
    pallas_call x1, Pallas kernels: 9.99 us -> 7.61 us  [per_device(): pl.pallas_call(backward_kernel, grid=(steps,), out_shape=(shape((n, E), b...]
where the time goes in v7:
time: 104 us; the launch traced here: 103 us
  blocking collectives  56.3 us (54%)
  Pallas kernels  32.5 us (31%)
  starting transfers between devices  6.27 us (6%)
  waiting for transfers between devices  5.69 us (5%)
  local copies, waits for them, and re-layouts  1.9 us (2%)
    all_to_all x1, blocking collectives, per_device(): got2 = lax.all_to_all(second, 'cls', 0, 0)  22.6 us
    all_to_all x1, blocking collectives, per_device(): got1 = lax.all_to_all(payload, 'dp', 0, 0)  21.7 us
    pallas_call x1, Pallas kernels, per_device(): pl.pallas_call(forward_kernel, grid=(steps,), out_shape=(shape((steps, SU...  18.6 us
    all_to_all x1, blocking collectives, per_device(): got3 = lax.all_to_all(rows, 'cls', 0, 0, axis_index_groups=groups)  12 us
    pallas_call x1, Pallas kernels, per_device(): pl.pallas_call(backward_kernel, grid=(steps,), out_shape=(shape((n, E), b...  7.61 us
    all_to_all x1, starting transfers between devices, per_device(): got = lax.all_to_all(sent, 'dp', 0, 0)  6.27 us
    all_to_all x1, waiting for transfers between devices, per_device(): got = lax.all_to_all(sent, 'dp', 0, 0)  5.69 us
  transfers between devices with their start and end apart: 1, of which 1 were waited for; matrix products, arithmetic and copies ran while one was open for 0% of the time, Pallas kernels for 2%

profile of v7, /device:TPU:2, one launch (start us, length us, event | category | flops | bytes accessed | tf_op | source)
XLA Modules:
  0.0 103.5 jit_solution(17512408218467194215)
XLA Ops:
  0.6 1.7 %shard_map.58 = bf16[16,80,256]{2,1,0:T(8,128)(2,1)} custom-call(s32[1]{0:T(128)} %bitcast.4.slot_ref, bf16[64,256]{1,0:T(8,128)(2,1)} %emb_ref.3, s32[1,64]{1,0:T(1,128)} %bitcast.7), custom_call_target="tpu_custom_call" | custom-call | tf_op jit(solution)/shard_map/pallas_call | solution.py:394
  2.4 6.3 %all-to-all-start = ((bf16[16,80,256]{2,1,0:T(8,128)(2,1)}), bf16[16,80,256]{2,1,0:T(8,128)(2,1)}, u32[]{:S(2)}, u32[]{:S(2)}) async-start(bf16[16,80,256]{2,1,0:T(8,128)(2,1)} %shard_map.58), calls=%async_computation | async-start | bytes 1310720 | tf_op jit(solution)/shard_map/all_to_all | solution.py:400
  8.6 0.0 copy-start
  8.6 1.9 %copy-done = bf16[3,2048,256]{2,1,0:T(8,128)(2,1)S(1)} copy-done((bf16[3,2048,256]{2,1,0:T(8,128)(2,1)S(1)}, bf16[3,2048,256]{2,1,0:T(8,128)(2,1)}, u32[]{:S(2)}) %copy-start) | copy-done | bytes 3145752
  10.5 1.6 %shard_map.60.cb_ref = bf16[4,1536,256]{2,1,0:T(8,128)(2,1)S(1)} custom-call(bf16[3,2048,256]{2,1,0:T(8,128)(2,1)S(1)} %copy-done), custom_call_target="tpu_custom_call" | custom-call | flops 1000000000 | bytes 10000000 | tf_op jit(solution)/shard_map/pallas_call | solution.py:403
  12.1 0.1 pad_add_fusion.where_ref.first_ref
  12.2 5.7 %all-to-all-done.got_ref = bf16[16,80,256]{2,1,0:T(8,128)(2,1)} async-done(((bf16[16,80,256]{2,1,0:T(8,128)(2,1)}), bf16[16,80,256]{2,1,0:T(8,128)(2,1)}, u32[]{:S(2)}, u32[]{:S(2)}) %all-to-all-start) | async-done | bytes 655392 | tf_op jit(solution)/shard_map/all_to_all | solution.py:400
  17.9 1.4 %shard_map.59 = (bf16[256,1024]{1,0:T(8,128)(2,1)S(1)}, s32[1,1024]{1,0:T(1,128)S(1)}, s32[8,128]{1,0:T(8,128)S(1)}) custom-call(s32[4]{0:T(128)S(1)} %pad_add_fusion.where_ref.first_ref, bf16[16,80,256]{2,1,0:T(8,128)(2,1)} %all-to-all-done.got_ref), custom_call_target="tpu_custom_call" | custom-call | tf_op jit(solution)/shard_map/pallas_call | solution.py:412
  19.3 0.0 copy-start.2
  19.3 18.6 %shard_map.61 = (bf16[4,3,512,1024]{3,2,1,0:T(8,128)(2,1)S(1)}, bf16[16,144,256]{2,1,0:T(8,128)(2,1)S(1)}, f32[8,1024]{1,0:T(8,128)S(1)}, f32[8,1024]{1,0:T(8,128)S(1)}) custom-call(s32[4]{0:T(128)S(1)} %pad_add_fusion.where_ref.first_ref, s32[8,128]{1,0:T(8,128)S(1)} %get-tuple-element.16.flag_ref, bf16[4,1536,256]{2,1,0:T(8,128)(2,1)S(1)} %shard_map.60.cb_ref, ...), custom_call_target="tpu_custom_call" | custom-call | tf_op jit(solution)/shard_map/pallas_call | solution.py:425
  37.9 0.0 copy-start.1
  37.9 21.7 %all_to_all.20.got_ref = bf16[16,144,256]{2,1,0:T(8,128)(2,1)S(1)} all-to-all(bf16[16,144,256]{2,1,0:T(8,128)(2,1)S(1)} %get-tuple-element.19), channel_id=1, replica_groups=mesh['dp'=16,'cls'=16] {'dp'}, dimensions={0} | all-to-all | bytes 2359296 | tf_op jit(solution)/shard_map/all_to_all | solution.py:446
  59.6 0.2 shard_map.62
  59.9 22.6 %all_to_all.21.got_ref = bf16[16,32,256]{2,1,0:T(8,128)(2,1)S(1)} all-to-all(bf16[16,32,256]{2,1,0:T(8,128)(2,1)S(1)} %shard_map.62), channel_id=1, replica_groups=mesh['dp'=16,'cls'=16] {'cls'}, dimensions={0} | all-to-all | bytes 524288 | tf_op jit(solution)/shard_map/all_to_all | solution.py:454
  82.4 0.0 copy-done.2
  82.4 1.4 %shard_map.63 = (f32[1,1]{1,0:T(1,128)}, bf16[256,1024]{1,0:T(8,128)(2,1)S(1)}, f32[8,1024]{1,0:T(8,128)S(1)}, bf16[8,8,256]{2,1,0:T(8,128)(2,1)S(1)}) custom-call(s32[4]{0:T(128)S(1)} %pad_add_fusion.where_ref.first_ref, bf16[16,32,256]{2,1,0:T(8,128)(2,1)S(1)} %all_to_all.21.got_ref, bf16[64,256]{1,0:T(8,128)(2,1)S(1)} %copy-done.2, ...), custom_call_target="tpu_custom_call" | custom-call | tf_op jit(solution)/shard_map/pallas_call | solution.py:455
  83.8 12.0 %all_to_all.22.got_ref = bf16[8,8,256]{2,1,0:T(8,128)(2,1)S(1)} all-to-all(bf16[8,8,256]{2,1,0:T(8,128)(2,1)S(1)} %get-tuple-element.25), channel_id=1, replica_groups={{0,1,2,3,4,5,6,7},{8,9,10,11,12,13,14,15},{16,17,18,19,20,21,22,23},{24..., dimensions={0} | all-to-all | bytes 65536 | tf_op jit(solution)/shard_map/all_to_all | solution.py:468
  95.8 0.0 copy-done.1
  95.8 7.6 %shard_map.64 = (bf16[64,256]{1,0:T(8,128)(2,1)}, bf16[3,2048,256]{2,1,0:T(8,128)(2,1)}) custom-call(s32[4]{0:T(128)S(1)} %pad_add_fusion.where_ref.first_ref, s32[8,128]{1,0:T(8,128)S(1)} %get-tuple-element.16.flag_ref, f32[8,1024]{1,0:T(8,128)S(1)} %get-tuple-element.23.fac_ref, bf16[256,1024]{1,0:T(8,128)(2,1)S(1)} %get-tuple-element.24.ust_ref, ...), custom_call_target="tpu_custom_call" | custom-call | tf_op jit(solution)/shard_map/pallas_call | solution.py:469
Async XLA Ops:
  2.4 15.5 %all-to-all-start = ((bf16[16,80,256]{2,1,0:T(8,128)(2,1)}), bf16[16,80,256]{2,1,0:T(8,128)(2,1)}, u32[]{:S(2)}, u32[]{:S(2)}) async-start(bf16[16,80,256]{2,1,0:T(8,128)(2,1)} %shard_map.58), calls=%async_computation | async-start | bytes 1310720 | tf_op jit(solution)/shard_map/all_to_all | solution.py:400
  8.6 1.9 %copy-start = (bf16[3,2048,256]{2,1,0:T(8,128)(2,1)S(1)}, bf16[3,2048,256]{2,1,0:T(8,128)(2,1)}, u32[]{:S(2)}) copy-start(bf16[3,2048,256]{2,1,0:T(8,128)(2,1)} %cent_ref.3) | copy-start | bytes 9437188
  19.3 63.2 %copy-start.2 = (bf16[64,256]{1,0:T(8,128)(2,1)S(1)}, bf16[64,256]{1,0:T(8,128)(2,1)}, u32[]{:S(2)}) copy-start(bf16[64,256]{1,0:T(8,128)(2,1)} %emb_ref.3) | copy-start | bytes 98308
  37.9 57.9 %copy-start.1 = (bf16[3,2048,256]{2,1,0:T(8,128)(2,1)S(1)}, bf16[3,2048,256]{2,1,0:T(8,128)(2,1)}, u32[]{:S(2)}) copy-start(bf16[3,2048,256]{2,1,0:T(8,128)(2,1)} %cent_ref.3) | copy-start | bytes 9437188

commit v8 on v7

--- a/solution.py
+++ b/solution.py
@@ -17,8 +17,7 @@
 A = 1.0 / (pool_temp * LN2)
 L = logit_scale * pool_temp
 MARGIN2 = logit_scale * margin_value / LN2
-INV_LN2 = 1.0 / LN2
-OUT_SCALE = logit_scale * LN2
+OUT_SCALE = logit_scale / pool_temp
 
 SUB = 3
 E = 256
@@ -106,21 +105,20 @@
 
 
 def elementwise(c0, c1, c2):
-    d1 = (c1 - c0) * A
-    d2 = (c2 - c0) * A
-    e1 = jnp.exp2(d1)
-    e2 = jnp.exp2(d2)
+    d1 = c1 - c0
+    d2 = c2 - c0
+    e1 = jnp.exp2(d1 * A)
+    e2 = jnp.exp2(d2 * A)
     r = 1.0 / (1.0 + e1 + e2)
     z = (e1 * d1 + e2 * d2) * r
-    power = c0 * (L * A) + z * L
-    shift = INV_LN2 - z
+    power = (c0 + z) * (L * A)
+    shift = pool_temp - z
     return e1, e2, d1, d2, r, power, shift
 
 
 def piece_of(i, h):
     per = BB // FB
-    down = pl.multiple_of((i // per) * FC, FC) + h * FT
-    return down, pl.multiple_of((i % per) * FB, FB)
+    return (i // per) * FC + h * FT, (i % per) * FB
 
 
 def for_labels(flag_ref, step, batch, do):
@@ -131,11 +129,8 @@
     ]
 
     def look(b, h, word):
-        def piece(i, carry):
-            pl.when(((word >> i) & 1) > 0)(functools.partial(do, b, h, i))
-            return carry
-
-        lax.fori_loop(0, (FT // FC) * (BB // FB), piece, 0)
+        for i in range((FT // FC) * (BB // FB)):
+            pl.when((word & (1 << i)) > 0)(functools.partial(do, b, h, i))
 
     @pl.when(functools.reduce(lambda x, y: x | y, [w for _, _, w in words]) > 0)
     def _():
@@ -168,12 +163,12 @@
     def set_labels_apart(b, h, i):
         down, over = piece_of(i, h)
         here = pl.ds(over, FB)
-        cols = pl.ds(pl.multiple_of(over + b * BB, FB), FB)
+        cols = pl.ds(over + b * BB, FB)
         row = lax.broadcasted_iota(jnp.int32, (FC, FB), 0) + down
         hit = row == lab_ref[:, cols] - first
         found = [jnp.sum(jnp.where(hit, 1.0, 0.0), axis=0, keepdims=True)]
         for k in range(SUB):
-            rows = pl.ds(pl.multiple_of(down + k * TC, FC), FC)
+            rows = pl.ds(down + k * TC, FC)
             v = xs[b, rows, here]
             found.append(jnp.sum(jnp.where(hit, v, 0.0), axis=0, keepdims=True))
             xs[b, rows, here] = jnp.where(hit, AWAY, v)
@@ -181,13 +176,13 @@
 
     def label_rows(at, b, h, i):
         down, over = piece_of(i, h)
-        cols = pl.ds(pl.multiple_of(over + b * BB, FB), FB)
+        cols = pl.ds(over + b * BB, FB)
         row = lax.broadcasted_iota(jnp.int32, (FC, FB), 0) + (down + at * TC + first_ref[0])
         hit = row == lab_ref[:, cols]
         own, rows = [], []
         for k in range(SUB):
             own.append(jnp.where(hit, own_ref[k : k + 1, cols], 0.0).astype(bf16))
-            rows.append(cb_ref[at, pl.ds(pl.multiple_of(down + k * TC, FC), FC), :])
+            rows.append(cb_ref[at, pl.ds(down + k * TC, FC), :])
         own, rows = jnp.concatenate(own, axis=0), jnp.concatenate(rows, axis=0)
         g2[cols, :] += lax.dot_general(own, rows, DIM0, preferred_element_type=f32)
 
@@ -357,7 +352,7 @@
 
     def set_labels(b, h, i):
         down, over = piece_of(i, h)
-        cols = pl.ds(pl.multiple_of(over + b * BB, FB), FB)
+        cols = pl.ds(over + b * BB, FB)
         row = lax.broadcasted_iota(jnp.int32, (FC, FB), 0) + down
         hit = row == lab_ref[:, cols] - first
         for k in range(SUB):

time: 104 us -> 101 us (0.971)
  Pallas kernels: 32.5 us -> 30.8 us
    pallas_call x1, Pallas kernels: 18.6 us -> 17.3 us  [per_device(): pl.pallas_call(forward_kernel, grid=(steps,), out_shape=(shape((steps, SU...]
where the time goes in v8:
time: 101 us
  blocking collectives  55.5 us (55%)
  Pallas kernels  30.8 us (30%)
  starting transfers between devices  6.27 us (6%)
  waiting for transfers between devices  5.69 us (6%)
  local copies, waits for them, and re-layouts  1.9 us (2%)
    all_to_all x1, blocking collectives, per_device(): got2 = lax.all_to_all(second, 'cls', 0, 0)  21.9 us
    all_to_all x1, blocking collectives, per_device(): got1 = lax.all_to_all(payload, 'dp', 0, 0)  21.5 us
    pallas_call x1, Pallas kernels, per_device(): pl.pallas_call(forward_kernel, grid=(steps,), out_shape=(shape((steps, SU...  17.3 us
    all_to_all x1, blocking collectives, per_device(): got3 = lax.all_to_all(rows, 'cls', 0, 0, axis_index_groups=groups)  12 us
    pallas_call x1, Pallas kernels, per_device(): pl.pallas_call(backward_kernel, grid=(steps,), out_shape=(shape((n, E), b...  7.28 us
    all_to_all x1, starting transfers between devices, per_device(): got = lax.all_to_all(sent, 'dp', 0, 0)  6.27 us
    all_to_all x1, waiting for transfers between devices, per_device(): got = lax.all_to_all(sent, 'dp', 0, 0)  5.69 us
  transfers between devices with their start and end apart: 1, of which 1 were waited for; matrix products, arithmetic and copies ran while one was open for 0% of the time, Pallas kernels for 2%

profile of v8, /device:TPU:2, one launch (start us, length us, event | category | flops | bytes accessed | tf_op | source)
XLA Modules:
  0.0 100.9 jit_solution(12839582347560640761)
XLA Ops:
  0.6 1.7 %shard_map.58 = bf16[16,80,256]{2,1,0:T(8,128)(2,1)} custom-call(s32[1]{0:T(128)} %bitcast.4.slot_ref, bf16[64,256]{1,0:T(8,128)(2,1)} %emb_ref.3, s32[1,64]{1,0:T(1,128)} %bitcast.7), custom_call_target="tpu_custom_call" | custom-call | tf_op jit(solution)/shard_map/pallas_call | solution.py:389
  2.4 6.3 %all-to-all-start = ((bf16[16,80,256]{2,1,0:T(8,128)(2,1)}), bf16[16,80,256]{2,1,0:T(8,128)(2,1)}, u32[]{:S(2)}, u32[]{:S(2)}) async-start(bf16[16,80,256]{2,1,0:T(8,128)(2,1)} %shard_map.58), calls=%async_computation | async-start | bytes 1310720 | tf_op jit(solution)/shard_map/all_to_all | solution.py:395
  8.6 0.0 copy-start
  8.6 1.9 %copy-done = bf16[3,2048,256]{2,1,0:T(8,128)(2,1)S(1)} copy-done((bf16[3,2048,256]{2,1,0:T(8,128)(2,1)S(1)}, bf16[3,2048,256]{2,1,0:T(8,128)(2,1)}, u32[]{:S(2)}) %copy-start) | copy-done | bytes 3145752
  10.5 1.6 %shard_map.60.cb_ref = bf16[4,1536,256]{2,1,0:T(8,128)(2,1)S(1)} custom-call(bf16[3,2048,256]{2,1,0:T(8,128)(2,1)S(1)} %copy-done), custom_call_target="tpu_custom_call" | custom-call | flops 1000000000 | bytes 10000000 | tf_op jit(solution)/shard_map/pallas_call | solution.py:398
  12.1 0.1 pad_add_fusion.where_ref.first_ref
  12.2 5.7 %all-to-all-done.got_ref = bf16[16,80,256]{2,1,0:T(8,128)(2,1)} async-done(((bf16[16,80,256]{2,1,0:T(8,128)(2,1)}), bf16[16,80,256]{2,1,0:T(8,128)(2,1)}, u32[]{:S(2)}, u32[]{:S(2)}) %all-to-all-start) | async-done | bytes 655392 | tf_op jit(solution)/shard_map/all_to_all | solution.py:395
  17.9 1.4 %shard_map.59 = (bf16[256,1024]{1,0:T(8,128)(2,1)S(1)}, s32[1,1024]{1,0:T(1,128)S(1)}, s32[8,128]{1,0:T(8,128)S(1)}) custom-call(s32[4]{0:T(128)S(1)} %pad_add_fusion.where_ref.first_ref, bf16[16,80,256]{2,1,0:T(8,128)(2,1)} %all-to-all-done.got_ref), custom_call_target="tpu_custom_call" | custom-call | tf_op jit(solution)/shard_map/pallas_call | solution.py:407
  19.3 0.0 copy-start.2
  19.3 17.3 %shard_map.61 = (bf16[4,3,512,1024]{3,2,1,0:T(8,128)(2,1)S(1)}, bf16[16,144,256]{2,1,0:T(8,128)(2,1)S(1)}, f32[8,1024]{1,0:T(8,128)S(1)}, f32[8,1024]{1,0:T(8,128)S(1)}) custom-call(s32[4]{0:T(128)S(1)} %pad_add_fusion.where_ref.first_ref, s32[8,128]{1,0:T(8,128)S(1)} %get-tuple-element.16.flag_ref, bf16[4,1536,256]{2,1,0:T(8,128)(2,1)S(1)} %shard_map.60.cb_ref, ...), custom_call_target="tpu_custom_call" | custom-call | tf_op jit(solution)/shard_map/pallas_call | solution.py:420
  36.5 0.0 copy-start.1
  36.5 21.5 %all_to_all.20.got_ref = bf16[16,144,256]{2,1,0:T(8,128)(2,1)S(1)} all-to-all(bf16[16,144,256]{2,1,0:T(8,128)(2,1)S(1)} %get-tuple-element.19), channel_id=1, replica_groups=mesh['dp'=16,'cls'=16] {'dp'}, dimensions={0} | all-to-all | bytes 2359296 | tf_op jit(solution)/shard_map/all_to_all | solution.py:441
  58.1 0.2 shard_map.62
  58.3 21.9 %all_to_all.21.got_ref = bf16[16,32,256]{2,1,0:T(8,128)(2,1)S(1)} all-to-all(bf16[16,32,256]{2,1,0:T(8,128)(2,1)S(1)} %shard_map.62), channel_id=1, replica_groups=mesh['dp'=16,'cls'=16] {'cls'}, dimensions={0} | all-to-all | bytes 524288 | tf_op jit(solution)/shard_map/all_to_all | solution.py:449
  80.2 0.0 copy-done.2
  80.2 1.4 %shard_map.63 = (f32[1,1]{1,0:T(1,128)}, bf16[256,1024]{1,0:T(8,128)(2,1)S(1)}, f32[8,1024]{1,0:T(8,128)S(1)}, bf16[8,8,256]{2,1,0:T(8,128)(2,1)S(1)}) custom-call(s32[4]{0:T(128)S(1)} %pad_add_fusion.where_ref.first_ref, bf16[16,32,256]{2,1,0:T(8,128)(2,1)S(1)} %all_to_all.21.got_ref, bf16[64,256]{1,0:T(8,128)(2,1)S(1)} %copy-done.2, ...), custom_call_target="tpu_custom_call" | custom-call | tf_op jit(solution)/shard_map/pallas_call | solution.py:450
  81.6 12.0 %all_to_all.22.got_ref = bf16[8,8,256]{2,1,0:T(8,128)(2,1)S(1)} all-to-all(bf16[8,8,256]{2,1,0:T(8,128)(2,1)S(1)} %get-tuple-element.25), channel_id=1, replica_groups={{0,1,2,3,4,5,6,7},{8,9,10,11,12,13,14,15},{16,17,18,19,20,21,22,23},{24..., dimensions={0} | all-to-all | bytes 65536 | tf_op jit(solution)/shard_map/all_to_all | solution.py:463
  93.6 0.0 copy-done.1
  93.6 7.3 %shard_map.64 = (bf16[64,256]{1,0:T(8,128)(2,1)}, bf16[3,2048,256]{2,1,0:T(8,128)(2,1)}) custom-call(s32[4]{0:T(128)S(1)} %pad_add_fusion.where_ref.first_ref, s32[8,128]{1,0:T(8,128)S(1)} %get-tuple-element.16.flag_ref, f32[8,1024]{1,0:T(8,128)S(1)} %get-tuple-element.23.fac_ref, bf16[256,1024]{1,0:T(8,128)(2,1)S(1)} %get-tuple-element.24.ust_ref, ...), custom_call_target="tpu_custom_call" | custom-call | tf_op jit(solution)/shard_map/pallas_call | solution.py:464
Async XLA Ops:
  2.4 15.5 %all-to-all-start = ((bf16[16,80,256]{2,1,0:T(8,128)(2,1)}), bf16[16,80,256]{2,1,0:T(8,128)(2,1)}, u32[]{:S(2)}, u32[]{:S(2)}) async-start(bf16[16,80,256]{2,1,0:T(8,128)(2,1)} %shard_map.58), calls=%async_computation | async-start | bytes 1310720 | tf_op jit(solution)/shard_map/all_to_all | solution.py:395
  8.6 1.9 %copy-start = (bf16[3,2048,256]{2,1,0:T(8,128)(2,1)S(1)}, bf16[3,2048,256]{2,1,0:T(8,128)(2,1)}, u32[]{:S(2)}) copy-start(bf16[3,2048,256]{2,1,0:T(8,128)(2,1)} %cent_ref.3) | copy-start | bytes 9437188
  19.3 61.0 %copy-start.2 = (bf16[64,256]{1,0:T(8,128)(2,1)S(1)}, bf16[64,256]{1,0:T(8,128)(2,1)}, u32[]{:S(2)}) copy-start(bf16[64,256]{1,0:T(8,128)(2,1)} %emb_ref.3) | copy-start | bytes 98308
  36.5 57.1 %copy-start.1 = (bf16[3,2048,256]{2,1,0:T(8,128)(2,1)S(1)}, bf16[3,2048,256]{2,1,0:T(8,128)(2,1)}, u32[]{:S(2)}) copy-start(bf16[3,2048,256]{2,1,0:T(8,128)(2,1)} %cent_ref.3) | copy-start | bytes 9437188

commit v9 on v8

--- a/solution.py
+++ b/solution.py
@@ -53,19 +53,19 @@
 
 def send_kernel(slot_ref, emb_ref, lab_ref, out_ref):
     rows = emb_ref[...].astype(f32)
-    unit = (rows * inv_norm(rows)).astype(bf16)
+    unit = rows * inv_norm(rows)
     n = rows.shape[0]
     labels = lab_ref[...]
     lane = lax.broadcasted_iota(jnp.int32, (1, E), 1)
     wide = jnp.concatenate([labels] * (E // n), axis=1)
     mine = (lane >= slot_ref[0]) & (lane < slot_ref[0] + n)
     wide = jnp.where(mine, wide, 0)
-    row = lax.broadcasted_iota(jnp.int32, (16, E), 0)
+    row = lax.broadcasted_iota(jnp.int32, (8, E), 0)
     digit = jnp.where(row == 0, wide & 127, jnp.where(row == 1, (wide >> 7) & 127, wide >> 14))
-    digit = jnp.where(row < 3, digit, 0).astype(f32).astype(bf16)
+    digit = jnp.where(row < 3, digit, 0).astype(f32)
+    block = jnp.concatenate([unit, digit], axis=0).astype(bf16)
     for j in range(out_ref.shape[0]):
-        out_ref[j, pl.ds(0, n), :] = unit
-        out_ref[j, pl.ds(n, 16), :] = digit
+        out_ref[j] = block
 
 
 def centre_kernel(cent_ref, cb_ref):
@@ -79,14 +79,11 @@
     parts = got_ref.shape[0]
     per = E // rows_own
     for q in range(parts // per):
-        digits = jnp.zeros((16, E), f32)
-        for j in range(per):
-            digits += got_ref[q * per + j, pl.ds(rows_own, 16), :].astype(f32)
+        whole = [got_ref[q * per + j].astype(f32) for j in range(per)]
+        digits = sum(w[rows_own:] for w in whole)
         lab = digits[0:1] + 128.0 * digits[1:2] + 16384.0 * digits[2:3]
         lab_ref[:, pl.ds(q * E, E)] = lab.astype(jnp.int32)
-        block = jnp.concatenate(
-            [got_ref[q * per + j, pl.ds(0, rows_own), :].astype(f32) for j in range(per)], axis=0
-        )
+        block = jnp.concatenate([w[:rows_own] for w in whole], axis=0)
         ut_ref[:, pl.ds(q * E, E)] = block.T.astype(bf16)
     words, width = flag_ref.shape
     batch = lab_ref.shape[1]
@@ -388,7 +385,7 @@
 
     sent = pl.pallas_call(
         send_kernel,
-        out_shape=shape((parts, n + 16, E), bf16),
+        out_shape=shape((parts, n + 8, E), bf16),
         in_specs=[smem, vmem, vmem],
         out_specs=vmem,
     )(slot.astype(jnp.int32).reshape(1), embeddings, labels.reshape(1, n))

time: 101 us -> 101 us (level)
  blocking collectives: 55.5 us -> 57.8 us
  Pallas kernels: 30.8 us -> 29.3 us
    all_to_all x1, blocking collectives: 21.5 us -> 22.9 us  [per_device(): got1 = lax.all_to_all(payload, 'dp', 0, 0)]
    pallas_call x1, Pallas kernels: 17.3 us -> 16 us  [per_device(): pl.pallas_call(forward_kernel, grid=(steps,), out_shape=(shape((steps, SU...]
where the time goes in v9:
time: 101 us
  blocking collectives  57.8 us (57%)
  Pallas kernels  29.3 us (29%)
  starting transfers between devices  6.25 us (6%)
  waiting for transfers between devices  4.88 us (5%)
  local copies, waits for them, and re-layouts  1.9 us (2%)
    all_to_all x1, blocking collectives, per_device(): got1 = lax.all_to_all(payload, 'dp', 0, 0)  22.9 us
    all_to_all x1, blocking collectives, per_device(): got2 = lax.all_to_all(second, 'cls', 0, 0)  22.9 us
    pallas_call x1, Pallas kernels, per_device(): pl.pallas_call(forward_kernel, grid=(steps,), out_shape=(shape((steps, SU...  16 us
    all_to_all x1, blocking collectives, per_device(): got3 = lax.all_to_all(rows, 'cls', 0, 0, axis_index_groups=groups)  12 us
    pallas_call x1, Pallas kernels, per_device(): pl.pallas_call(backward_kernel, grid=(steps,), out_shape=(shape((n, E), b...  7.02 us
    all_to_all x1, starting transfers between devices, per_device(): got = lax.all_to_all(sent, 'dp', 0, 0)  6.25 us
    all_to_all x1, waiting for transfers between devices, per_device(): got = lax.all_to_all(sent, 'dp', 0, 0)  4.88 us
  transfers between devices with their start and end apart: 1, of which 1 were waited for; matrix products, arithmetic and copies ran while one was open for 0% of the time, Pallas kernels for 2%

profile of v9, /device:TPU:2, one launch (start us, length us, event | category | flops | bytes accessed | tf_op | source)
XLA Modules:
  0.0 100.9 jit_solution(10056811490708437046)
XLA Ops:
  0.6 1.7 %shard_map.58 = bf16[16,72,256]{2,1,0:T(8,128)(2,1)} custom-call(s32[1]{0:T(128)} %bitcast.4.slot_ref, bf16[64,256]{1,0:T(8,128)(2,1)} %emb_ref.3, s32[1,64]{1,0:T(1,128)} %bitcast.7), custom_call_target="tpu_custom_call" | custom-call | tf_op jit(solution)/shard_map/pallas_call | solution.py:386
  2.3 6.3 %all-to-all-start = ((bf16[16,72,256]{2,1,0:T(8,128)(2,1)}), bf16[16,72,256]{2,1,0:T(8,128)(2,1)}, u32[]{:S(2)}, u32[]{:S(2)}) async-start(bf16[16,72,256]{2,1,0:T(8,128)(2,1)} %shard_map.58), calls=%async_computation | async-start | bytes 1179648 | tf_op jit(solution)/shard_map/all_to_all | solution.py:392
  8.6 0.0 copy-start
  8.6 1.9 %copy-done = bf16[3,2048,256]{2,1,0:T(8,128)(2,1)S(1)} copy-done((bf16[3,2048,256]{2,1,0:T(8,128)(2,1)S(1)}, bf16[3,2048,256]{2,1,0:T(8,128)(2,1)}, u32[]{:S(2)}) %copy-start) | copy-done | bytes 3145752
  10.5 1.6 %shard_map.60.cb_ref = bf16[4,1536,256]{2,1,0:T(8,128)(2,1)S(1)} custom-call(bf16[3,2048,256]{2,1,0:T(8,128)(2,1)S(1)} %copy-done), custom_call_target="tpu_custom_call" | custom-call | flops 1000000000 | bytes 10000000 | tf_op jit(solution)/shard_map/pallas_call | solution.py:395
  12.1 0.1 pad_add_fusion.where_ref.first_ref
  12.2 4.9 %all-to-all-done.got_ref = bf16[16,72,256]{2,1,0:T(8,128)(2,1)} async-done(((bf16[16,72,256]{2,1,0:T(8,128)(2,1)}), bf16[16,72,256]{2,1,0:T(8,128)(2,1)}, u32[]{:S(2)}, u32[]{:S(2)}) %all-to-all-start) | async-done | bytes 589856 | tf_op jit(solution)/shard_map/all_to_all | solution.py:392
  17.1 1.3 %shard_map.59 = (bf16[256,1024]{1,0:T(8,128)(2,1)S(1)}, s32[1,1024]{1,0:T(1,128)S(1)}, s32[8,128]{1,0:T(8,128)S(1)}) custom-call(s32[4]{0:T(128)S(1)} %pad_add_fusion.where_ref.first_ref, bf16[16,72,256]{2,1,0:T(8,128)(2,1)} %all-to-all-done.got_ref), custom_call_target="tpu_custom_call" | custom-call | tf_op jit(solution)/shard_map/pallas_call | solution.py:404
  18.4 0.0 copy-start.2
  18.4 16.0 %shard_map.61 = (bf16[4,3,512,1024]{3,2,1,0:T(8,128)(2,1)S(1)}, bf16[16,144,256]{2,1,0:T(8,128)(2,1)S(1)}, f32[8,1024]{1,0:T(8,128)S(1)}, f32[8,1024]{1,0:T(8,128)S(1)}) custom-call(s32[4]{0:T(128)S(1)} %pad_add_fusion.where_ref.first_ref, s32[8,128]{1,0:T(8,128)S(1)} %get-tuple-element.16.flag_ref, bf16[4,1536,256]{2,1,0:T(8,128)(2,1)S(1)} %shard_map.60.cb_ref, ...), custom_call_target="tpu_custom_call" | custom-call | tf_op jit(solution)/shard_map/pallas_call | solution.py:417
  34.4 0.0 copy-start.1
  34.4 22.9 %all_to_all.20.got_ref = bf16[16,144,256]{2,1,0:T(8,128)(2,1)S(1)} all-to-all(bf16[16,144,256]{2,1,0:T(8,128)(2,1)S(1)} %get-tuple-element.19), channel_id=1, replica_groups=mesh['dp'=16,'cls'=16] {'dp'}, dimensions={0} | all-to-all | bytes 2359296 | tf_op jit(solution)/shard_map/all_to_all | solution.py:438
  57.4 0.2 shard_map.62
  57.6 22.9 %all_to_all.21.got_ref = bf16[16,32,256]{2,1,0:T(8,128)(2,1)S(1)} all-to-all(bf16[16,32,256]{2,1,0:T(8,128)(2,1)S(1)} %shard_map.62), channel_id=1, replica_groups=mesh['dp'=16,'cls'=16] {'cls'}, dimensions={0} | all-to-all | bytes 524288 | tf_op jit(solution)/shard_map/all_to_all | solution.py:446
  80.5 0.0 copy-done.2
  80.5 1.4 %shard_map.63 = (f32[1,1]{1,0:T(1,128)}, bf16[256,1024]{1,0:T(8,128)(2,1)S(1)}, f32[8,1024]{1,0:T(8,128)S(1)}, bf16[8,8,256]{2,1,0:T(8,128)(2,1)S(1)}) custom-call(s32[4]{0:T(128)S(1)} %pad_add_fusion.where_ref.first_ref, bf16[16,32,256]{2,1,0:T(8,128)(2,1)S(1)} %all_to_all.21.got_ref, bf16[64,256]{1,0:T(8,128)(2,1)S(1)} %copy-done.2, ...), custom_call_target="tpu_custom_call" | custom-call | tf_op jit(solution)/shard_map/pallas_call | solution.py:447
  81.8 12.0 %all_to_all.22.got_ref = bf16[8,8,256]{2,1,0:T(8,128)(2,1)S(1)} all-to-all(bf16[8,8,256]{2,1,0:T(8,128)(2,1)S(1)} %get-tuple-element.25), channel_id=1, replica_groups={{0,1,2,3,4,5,6,7},{8,9,10,11,12,13,14,15},{16,17,18,19,20,21,22,23},{24..., dimensions={0} | all-to-all | bytes 65536 | tf_op jit(solution)/shard_map/all_to_all | solution.py:460
  93.9 0.0 copy-done.1
  93.9 7.0 %shard_map.64 = (bf16[64,256]{1,0:T(8,128)(2,1)}, bf16[3,2048,256]{2,1,0:T(8,128)(2,1)}) custom-call(s32[4]{0:T(128)S(1)} %pad_add_fusion.where_ref.first_ref, s32[8,128]{1,0:T(8,128)S(1)} %get-tuple-element.16.flag_ref, f32[8,1024]{1,0:T(8,128)S(1)} %get-tuple-element.23.fac_ref, bf16[256,1024]{1,0:T(8,128)(2,1)S(1)} %get-tuple-element.24.ust_ref, ...), custom_call_target="tpu_custom_call" | custom-call | tf_op jit(solution)/shard_map/pallas_call | solution.py:461
Async XLA Ops:
  2.3 14.7 %all-to-all-start = ((bf16[16,72,256]{2,1,0:T(8,128)(2,1)}), bf16[16,72,256]{2,1,0:T(8,128)(2,1)}, u32[]{:S(2)}, u32[]{:S(2)}) async-start(bf16[16,72,256]{2,1,0:T(8,128)(2,1)} %shard_map.58), calls=%async_computation | async-start | bytes 1179648 | tf_op jit(solution)/shard_map/all_to_all | solution.py:392
  8.6 1.9 %copy-start = (bf16[3,2048,256]{2,1,0:T(8,128)(2,1)S(1)}, bf16[3,2048,256]{2,1,0:T(8,128)(2,1)}, u32[]{:S(2)}) copy-start(bf16[3,2048,256]{2,1,0:T(8,128)(2,1)} %cent_ref.3) | copy-start | bytes 9437188
  18.4 62.1 %copy-start.2 = (bf16[64,256]{1,0:T(8,128)(2,1)S(1)}, bf16[64,256]{1,0:T(8,128)(2,1)}, u32[]{:S(2)}) copy-start(bf16[64,256]{1,0:T(8,128)(2,1)} %emb_ref.3) | copy-start | bytes 98308
  34.4 59.5 %copy-start.1 = (bf16[3,2048,256]{2,1,0:T(8,128)(2,1)S(1)}, bf16[3,2048,256]{2,1,0:T(8,128)(2,1)}, u32[]{:S(2)}) copy-start(bf16[3,2048,256]{2,1,0:T(8,128)(2,1)} %cent_ref.3) | copy-start | bytes 9437188
